TPU v7x, 32 devices: a whole 2x2x4 slice. The times are simulated.
32 devices in a mesh: parts: 2 (over y), elem: 4 (over z), comp: 2 (over core), sub: 2 (over x).
Axes of the slice: x: 2, y: 2, z: 4, core: 2. Of those that a mesh axis runs over, the one named last changes fastest.
Arguments:
- field: float32 [2, 4, 64, 64, 128], P('comp', None, ('parts', 'elem'), 'sub'), parts along dimension 2, may hold values from -6 to 6
- register: float32 [2, 4, 64, 64, 128], P('comp', None, ('parts', 'elem'), 'sub'), parts along dimension 2, may hold values from -6 to 6
- advect: float32 [2, 3], replicated, may hold values from -0.5 to 0.5
- mixing: float32 [2, 4, 4], replicated, may hold values from -3 to 3
- drag: float32 [2, 4], replicated, may hold values from 0.5 to 2
- face_elem: int32 [2, 8, 2, 192], P('comp', ('parts', 'elem'), 'sub'), parts along dimension 1, may hold values from 0 to 63
- face_side: int32 [2, 8, 2, 192], P('comp', ('parts', 'elem'), 'sub'), parts along dimension 1, may hold values from 0 to 5
- mortar_code: int32 [2, 8, 2, 192], P('comp', ('parts', 'elem'), 'sub'), parts along dimension 1, may hold values from 0 to 5
- partner_rank: int32 [2, 8, 2, 192, 1], P('comp', ('parts', 'elem'), 'sub'), parts along dimension 1, may hold values from 0 to 3; in each aligned block of 192 rows (0 to 191, 192 to 383, ..., all dimensions but the last counted through in order) at most 96 rows name the same one
- partner_elem: int32 [2, 8, 2, 192], P('comp', ('parts', 'elem'), 'sub'), parts along dimension 1, may hold values from 0 to 63
- partner_side: int32 [2, 8, 2, 192], P('comp', ('parts', 'elem'), 'sub'), parts along dimension 1, may hold values from 0 to 5
- partner_quadrant: int32 [2, 8, 2, 192], P('comp', ('parts', 'elem'), 'sub'), parts along dimension 1, may hold values from 0 to 3
- face_count: int32 [2, 8, 2], P('comp', ('parts', 'elem'), 'sub'), parts along dimension 1, may hold values from 144 to 192, as said below
Outputs:
- new_register: float32 [2, 4, 64, 64, 128], P('comp', None, ('parts', 'elem'), 'sub'), parts along dimension 2
- advanced_field: float32 [2, 4, 64, 64, 128], P('comp', None, ('parts', 'elem'), 'sub'), parts along dimension 2
There are 2 independent parts, one for each index of `parts`. A program takes and returns all parts, laid end to end along the dimension named above; an argument that names none is the same for every part. Nothing has to cross between parts.
Inputs may be any that keep to these rules, and one draw needn't show every extreme that they name: `partner_rank`: in the records of one device, at most 96 name the same partner rank. `face_count`: records of a device at positions at or beyond its count are unused.
All inputs are finite; a program needn't handle non-finite values.
Results may differ from a plain program's by a relative error of at most 0.0003.
Values sent between devices are 32-bit elements; how exact they have to be, the bound alone decides.
No kernel may reach another device: no remote copies, remote signals or barrier semaphores. Data moves between devices by JAX's collectives and lax.ppermute only.
A program may use at most 192 MiB of HBM per device.

v0:
```python
import math

import jax
import jax.numpy as jnp
from jax import lax
from jax.sharding import PartitionSpec as P

P_SIZE = 8
EY = 4
EZ = 16


upwind_share = 0.5
register_keep = -0.4178904745
section_weight = 1.7201463215
time_step = 0.05
highest = lax.Precision.HIGHEST


def swapped(shard, axis, apart):
    return lax.ppermute(shard, axis, [(i, i ^ 1 << apart) for i in range(lax.axis_size(axis))])


def padded_2(shard, sides, width):
    for axis, dim in sides:
        devices, length = (lax.axis_size(axis), shard.shape[dim])
        up = [(i, (i + 1) % devices) for i in range(devices - 1)]
        down = [(j, i) for i, j in up]
        last = lax.slice_in_dim(shard, length - width, length, axis=dim)
        leading = lax.slice_in_dim(shard, 0, width, axis=dim)
        before = lax.ppermute(last, axis, up)
        after = lax.ppermute(leading, axis, down)
        shard = jnp.concatenate([before, shard, after], axis=dim)
    return shard


def legendre_values(point, count):
    values = [1.0, point]
    for power in range(2, count):
        values.append(
            ((2 * power - 1) * point * values[power - 1] - (power - 1) * values[power - 2]) / power
        )
    return values[:count]


def matrix_product(left, right):
    inner_count = len(right)
    columns = len(right[0])
    return [
        [
            sum((left[row_pos][middle] * right[middle][column] for middle in range(inner_count)))
            for column in range(columns)
        ]
        for row_pos in range(len(left))
    ]


def lagrange_rows(points, targets):
    total = len(points)
    result = []
    for target in targets:
        row_values = []
        for column in range(total):
            product = 1.0
            for other in range(total):
                if other != column:
                    product = product * (target - points[other]) / (points[column] - points[other])
            row_values.append(product)
        result.append(row_values)
    return result


def node_tables(nodes):
    degree = nodes - 1
    guesses = [math.cos(math.pi * position / degree) for position in range(nodes)]
    for sweep in range(100):
        updated = []
        for point in guesses:
            values = legendre_values(point, nodes)
            updated.append(
                point - (point * values[degree] - values[degree - 1]) / (nodes * values[degree])
            )
        guesses = updated
    points = sorted(guesses)
    points[0] = -1.0
    points[-1] = 1.0
    modal_basis = [legendre_values(point, nodes) for point in points]
    weights = [
        2.0 / (degree * nodes * legendre_values(point, nodes)[degree] ** 2) for point in points
    ]
    norms = [2.0 / (2 * power + 1) for power in range(degree)] + [2.0 / degree]
    inverse = [
        [
            modal_basis[position][power] * weights[position] / norms[power]
            for position in range(nodes)
        ]
        for power in range(nodes)
    ]
    end_weight = 2.0 / (degree * nodes)
    barycentric = []
    for position in range(nodes):
        product = 1.0
        for other in range(nodes):
            if other != position:
                product = product * (points[position] - points[other])
        barycentric.append(1.0 / product)
    derivative = []
    for position in range(nodes):
        row_values = []
        for other in range(nodes):
            if other != position:
                row_values.append(
                    barycentric[other] / barycentric[position] / (points[position] - points[other])
                )
            else:
                row_values.append(0.0)
        row_values[position] = -sum(row_values)
        derivative.append(row_values)
    lower_mask = [1.0 if point < 0 else 0.0 for point in points]
    upper_mask = [1.0 if point > 0 else 0.0 for point in points]
    send_table = [
        inverse,
        matrix_product(inverse, lagrange_rows(points, [(point - 1.0) / 2.0 for point in points])),
        matrix_product(inverse, lagrange_rows(points, [(point + 1.0) / 2.0 for point in points])),
    ]
    lower_eval = [
        [
            value * lower_mask[position]
            for value in legendre_values(2.0 * points[position] + 1.0, nodes)
        ]
        for position in range(nodes)
    ]
    upper_eval = [
        [
            value * upper_mask[position]
            for value in legendre_values(2.0 * points[position] - 1.0, nodes)
        ]
        for position in range(nodes)
    ]
    receive_table = [modal_basis, lower_eval, upper_eval]
    masks = [[1.0] * nodes, lower_mask, upper_mask]
    return (
        jnp.asarray(derivative, jnp.float32),
        float(1.0 / end_weight),
        jnp.asarray(send_table, jnp.float32),
        jnp.asarray(receive_table, jnp.float32),
        jnp.asarray(masks, jnp.float32),
    )


def volume_rate(field, derivative, speeds):
    variables, size_x, size_y, size_z = field.shape
    nodes = derivative.shape[0]
    shaped = field.reshape(
        variables, size_x // nodes, nodes, size_y // nodes, nodes, size_z // nodes, nodes
    )
    along_x = jnp.einsum("mi,vaibjck->vambjck", derivative, shaped, precision=highest)
    along_y = jnp.einsum("mj,vaibjck->vaibmck", derivative, shaped, precision=highest)
    along_z = jnp.einsum("mk,vaibjck->vaibjcm", derivative, shaped, precision=highest)
    total = speeds[0] * along_x + speeds[1] * along_y + speeds[2] * along_z
    return -total.reshape(field.shape)


def surface_rate(field, neighbours, speeds, end_scale, nodes):
    total = jnp.zeros(field.shape, jnp.float32)
    for axis_pos in range(3):
        before, after = neighbours[axis_pos]
        speed = speeds[axis_pos]
        place = lax.broadcasted_iota(jnp.int32, field.shape, axis_pos + 1) % nodes
        first_node = (place == 0).astype(jnp.float32)
        last_node = (place == nodes - 1).astype(jnp.float32)
        right_flux = 0.5 * speed * (field + after) + 0.5 * upwind_share * jnp.abs(speed) * (
            field - after
        )
        left_flux = 0.5 * speed * (before + field) + 0.5 * upwind_share * jnp.abs(speed) * (
            before - field
        )
        total = total + end_scale * (
            first_node * (left_flux - speed * field) - last_node * (right_flux - speed * field)
        )
    return total


def component_rate(field, neighbours, speeds, mixing_here, derivative, end_scale, nodes):
    coupled = jnp.einsum("vw,wxyz->vxyz", mixing_here, field, precision=highest)
    return (
        volume_rate(field, derivative, speeds)
        + surface_rate(field, neighbours, speeds, end_scale, nodes)
        + coupled
    )


def face_coordinates(side, nodes):
    shape = side.shape + (nodes, nodes)
    first = lax.broadcasted_iota(jnp.int32, shape, side.ndim)
    second = lax.broadcasted_iota(jnp.int32, shape, side.ndim + 1)
    direction = (side // 2)[..., None, None]
    endpoint = (side % 2 * (nodes - 1))[..., None, None]
    along_x = jnp.where(direction == 0, endpoint, first)
    along_y = jnp.where(direction == 0, first, jnp.where(direction == 1, endpoint, second))
    along_z = jnp.where(direction == 2, endpoint, second)
    return (along_x, along_y, along_z)


def node_index(elem, side, base_x, base_y, blocks_y, blocks_z, span_y, span_z, nodes):
    along_x, along_y, along_z = face_coordinates(side, nodes)
    elem_x = elem // (blocks_y * blocks_z)
    elem_y = elem // blocks_z % blocks_y
    elem_z = elem % blocks_z
    global_x = (base_x + elem_x * nodes)[..., None, None] + along_x
    global_y = (base_y + elem_y * nodes)[..., None, None] + along_y
    global_z = (elem_z * nodes)[..., None, None] + along_z
    return ((global_x * span_y + global_y) * span_z + global_z).astype(jnp.int32)


def pick(table, index):
    onehot = (index[:, None] == jnp.arange(3, dtype=jnp.int32)[None, :]).astype(jnp.float32)
    return jnp.einsum("ro,o...->r...", onehot, table, precision=highest)


def half_index(code, digit):
    quadrant = jnp.maximum(code - 1, 0)
    half = quadrant // 2 if digit == 0 else quadrant % 2
    return jnp.where(code == 0, 0, 1 + half).astype(jnp.int32)


def project(values, code, send_table):
    first_table = pick(send_table, half_index(code, 0))
    second_table = pick(send_table, half_index(code, 1))
    return jnp.einsum("rka,vrab,rlb->rvkl", first_table, values, second_table, precision=highest)


def evaluate(coefs, own, code, receive_table, masks):
    first_table = pick(receive_table, half_index(code, 0))
    second_table = pick(receive_table, half_index(code, 1))
    first_mask = pick(masks, half_index(code, 0))
    second_mask = pick(masks, half_index(code, 1))
    evaluated = jnp.einsum(
        "rik,rvkl,rjl->vrij", first_table, coefs, second_table, precision=highest
    )
    return evaluated - first_mask[None, :, :, None] * second_mask[None, :, None, :] * own


def fill_slots(slot_rows, coefs, header, total_rows):
    outgoing = (
        jnp.zeros((total_rows, coefs.shape[1]), jnp.float32).at[slot_rows].set(coefs, mode="drop")
    )
    heads = (
        jnp.zeros((total_rows, header.shape[1]), jnp.int32).at[slot_rows].set(header, mode="drop")
    )
    return (outgoing, heads)


def on_device(
    field,
    register,
    advect,
    mixing,
    drag,
    face_elem,
    face_side,
    mortar_code,
    partner_rank,
    partner_elem,
    partner_side,
    partner_quadrant,
    face_count,
):
    derivative, end_scale, send_table, receive_table, masks = node_tables(P_SIZE)
    block_field = field[0]
    variables, size_x, size_y, size_z = block_field.shape
    comp_index = lax.axis_index("comp")
    speeds = lax.dynamic_index_in_dim(advect, comp_index, 0, keepdims=False)
    mixing_here = lax.dynamic_index_in_dim(mixing, comp_index, 0, keepdims=False)
    drag_here = lax.dynamic_index_in_dim(drag, comp_index, 0, keepdims=False)
    flat_field = block_field.reshape(variables, -1)
    capacity = face_elem.shape[-1]
    rank_total = lax.axis_size("elem")
    slot_count = max(2, 2 * capacity // rank_total)
    elements = face_elem.reshape(-1)
    sides = face_side.reshape(-1)
    codes = mortar_code.reshape(-1)
    target_rank = partner_rank.reshape(-1)
    in_use = jnp.arange(capacity, dtype=jnp.int32) < jnp.reshape(face_count, ())
    source_index = node_index(elements, sides, 0, 0, EY, EZ, size_y, size_z, P_SIZE)
    values = jnp.take(flat_field, source_index, axis=1)
    send_code = jnp.where((codes >= 1) & (codes <= 4), codes, 0)
    coefs = project(values, send_code, send_table).reshape(capacity, -1)
    receive_code = jnp.where(codes == 5, 1 + partner_quadrant.reshape(-1), 0)
    header = jnp.stack(
        [
            partner_elem.reshape(-1),
            partner_side.reshape(-1),
            receive_code,
            in_use.astype(jnp.int32),
        ],
        axis=1,
    )
    member = (
        (target_rank[:, None] == jnp.arange(rank_total, dtype=jnp.int32)[None, :]) & in_use[:, None]
    ).astype(jnp.int32)
    position = jnp.sum((jnp.cumsum(member, axis=0) - 1) * member, axis=1)
    total_rows = rank_total * slot_count
    slot_rows = jnp.where(in_use, target_rank * slot_count + position, total_rows)
    outgoing, heads = fill_slots(slot_rows, coefs, header, total_rows)
    crossed, crossed_head = swapped((outgoing, heads), "comp", 0)
    incoming, incoming_head = (
        lax.all_to_all(crossed, "elem", split_axis=0, concat_axis=0, tiled=True),
        lax.all_to_all(crossed_head, "elem", split_axis=0, concat_axis=0, tiled=True),
    )
    padded = padded_2(block_field, (("elem", 1), ("sub", 2)), 1)
    padded_z = jnp.pad(block_field, ((0, 0), (0, 0), (0, 0), (1, 1)))
    neighbours = [
        (padded[:, :-2, 1:-1, :], padded[:, 2:, 1:-1, :]),
        (padded[:, 1:-1, :-2, :], padded[:, 1:-1, 2:, :]),
        (padded_z[:, :, :, :-2], padded_z[:, :, :, 2:]),
    ]
    rate = component_rate(
        block_field, neighbours, speeds, mixing_here, derivative, end_scale, P_SIZE
    )
    received = incoming.reshape(-1, variables, P_SIZE, P_SIZE)
    target_index = node_index(
        incoming_head[:, 0], incoming_head[:, 1], 0, 0, EY, EZ, size_y, size_z, P_SIZE
    )
    own = jnp.take(flat_field, target_index, axis=1)
    term = evaluate(received, own, incoming_head[:, 2], receive_table, masks)
    scale = (
        drag_here[:, None, None, None]
        * end_scale
        * incoming_head[:, 3].astype(jnp.float32)[None, :, None, None]
    )
    flat_rate = rate.reshape(variables, -1).at[:, target_index].add(term * scale)
    rate = flat_rate.reshape(block_field.shape)
    new_register = register_keep * register[0] + time_step * rate
    advanced_field = block_field + section_weight * new_register
    return (new_register[None], advanced_field[None])


def solution(mesh):
    in_specs = (
        P("comp", None, ("parts", "elem"), "sub", None),
        P("comp", None, ("parts", "elem"), "sub", None),
        P(),
        P(),
        P(),
        P("comp", ("parts", "elem"), "sub", None),
        P("comp", ("parts", "elem"), "sub", None),
        P("comp", ("parts", "elem"), "sub", None),
        P("comp", ("parts", "elem"), "sub", None, None),
        P("comp", ("parts", "elem"), "sub", None),
        P("comp", ("parts", "elem"), "sub", None),
        P("comp", ("parts", "elem"), "sub", None),
        P("comp", ("parts", "elem"), "sub"),
    )
    out_specs = (
        P("comp", None, ("parts", "elem"), "sub", None),
        P("comp", None, ("parts", "elem"), "sub", None),
    )
    return jax.shard_map(
        on_device, mesh=mesh, in_specs=in_specs, out_specs=out_specs, check_vma=False
    )
```

profile of v0, /device:TPU:0, one launch (start us, length us, event | category | flops | bytes accessed | tf_op | source)
XLA Modules:
  0.0 658.0 jit_solution(6626356913179033712)
XLA Ops:
  1.3 0.7 fusion.52
  2.0 1.2 reduce-window.6
  3.7 0.7 fusion.50
  4.4 0.7 fusion.84
  5.1 0.7 pad_add_fusion
  5.9 0.7 compare_select_fusion.4
  6.6 1.7 scatter_custom_fusion
  8.2 0.5 collective-permute-start.4
  8.7 0.7 broadcast_compare_fusion.8
  9.4 0.7 fusion.80
  10.1 0.7 fusion.85
  10.8 1.5 compare_select_fusion.1
  12.4 10.0 %copy.162 = f32[1,4,8,32,128]{1,4,3,2,0:T(8,128)} copy(f32[1,4,8,32,128]{4,3,2,1,0:T(8,128)} %param.17) | data formatting | bytes 1048576 | tf_op args[0]
  22.8 47.1 %gather_fusion = f32[12288,4]{1,0:T(8,128)} fusion(f32[4,32768]{0,1:T(8,128)} %bitcast.147, s32[12288]{0:T(1024)S(1)} %broadcast_clamp_fusion.1), kind=kCustom, calls=%fused_computation | custom fusion | bytes 442368 | tf_op jit(solution)/shard_map/jit(_take)/gather | solution.py:286
  69.9 11.1 %copy.163 = f32[192,8,8,4]{1,2,3,0:T(8,128)S(1)} copy(f32[192,8,8,4]{3,2,1,0:T(8,128)} %bitcast.152) | data formatting | bytes 393216 | tf_op jit(solution)/shard_map/jit(_take)/gather | solution.py:286
  81.7 1.2 copy.186
  83.1 1.2 copy.188
  84.3 4.4 fusion.5
  88.8 5.4 fusion.3
  94.2 1.6 copy.167
  95.9 1.9 scatter_custom_fusion.1
  97.9 1.4 copy.217
  99.3 4.9 collective-permute-start
  104.2 1.3 collective-permute-start.1
  105.5 7.0 %reshape.689 = f32[4,8,4,8,16,8]{5,4,3,2,1,0:T(8,128)} reshape(f32[1,4,8,32,128]{4,3,2,1,0:T(8,128)} %param.17) | data formatting | bytes 1048576 | tf_op jit(solution)/shard_map/reshape.5
  112.6 6.9 %copy.149 = f32[4,8,4,8,16,8]{4,3,5,2,1,0:T(8,128)} copy(f32[4,8,4,8,16,8]{5,4,3,2,1,0:T(8,128)} %reshape.689) | data formatting | bytes 1048576 | tf_op jit(solution)/shard_map/reshape.5
  119.5 6.8 %copy.148 = f32[4,8,4,8,16,8]{4,1,5,3,2,0:T(8,128)} copy(f32[4,8,4,8,16,8]{5,4,3,2,1,0:T(8,128)} %reshape.689) | data formatting | bytes 1048576 | tf_op jit(solution)/shard_map/reshape.5
  126.3 0.5 iota_and_fusion.1
  126.8 0.6 iota_and_fusion.2
  127.4 0.6 compare_and_fusion.2
  128.0 0.5 compare_and_fusion.3
  128.5 0.7 fusion.92
  129.2 61.6 %fusion.94 = f32[8,4,8,4,8,16]{5,0,4,3,2,1:T(8,128)S(1)} fusion(f32[8,8,1,1,1,1]{1,0,5,4,3,2:T(8,128)S(1)} %copy-done.14, f32[4,8,4,8,16,8]{5,4,3,2,1,0:T(8,128)} %reshape.689), kind=kOutput, calls=%fused_computation.228 | convolution fusion | flops 12582912 | bytes 1048832 | tf_op jit(solution)/shard_map/mk,vaibjck->vaibjcm/dot_general | solution.py:159
  190.8 3.7 fusion.93
  194.6 11.0 %fusion.2 = f32[4,1,8,4,8,16,8]{5,2,6,4,3,0,1:T(8,128)} fusion(f32[8,4,8,4,8,16]{5,0,4,3,2,1:T(8,128)S(1)} %fusion.94, f32[8,4,8,4,16,8]{4,0,5,3,2,1:T(8,128)S(1)} %fusion.93, f32[8,8,1,1,1,1]{1,0,5,4,3,2:T(8,128)S(1)} %copy-done.14, f32[4,8,4,8,16,8]{4,1,5,3,2,0:T(8,128)S(1)} %copy-done.3, f32[]{:T(128)} %bitcast.11, f32[]{:T(128)} %bitcast.6, f32[]{:T(128)} %bitcast), kind=kOutput, calls=%fused_computation.11 | convolution fusion | flops 13369344 | bytes 2097420 | tf_op jit(solution)/shard_map/mi,vaibjck->vambjck/dot_general | solution.py:157
  205.6 0.6 compare_and_fusion.4
  206.2 1.6 copy.159
  207.8 6.1 all-to-all-start
  217.9 7.0 %copy.194 = f32[4,1,8,4,8,16,8]{6,5,0,4,3,2,1:T(8,128)} copy(f32[4,1,8,4,8,16,8]{5,2,6,4,3,0,1:T(8,128)} %fusion.2) | data formatting | bytes 1048576 | tf_op jit(solution)/shard_map/neg | solution.py:161
  224.9 7.2 %reshape.753 = f32[4,8,32,128]{3,0,2,1:T(4,128)} reshape(f32[4,1,8,4,8,16,8]{6,5,0,4,3,2,1:T(8,128)} %copy.194) | data formatting | bytes 1048576 | tf_op jit(solution)/shard_map/neg | solution.py:161
  232.3 3.0 compare_select_fusion
  235.3 0.8 reshape.734
  236.9 1.6 broadcast_multiply_fusion.1
  239.0 0.6 pad_maximum_fusion.8
  239.6 4.0 collective-permute-start.2
  243.6 1.3 collective-permute-start.3
  245.1 87.2 %gather_fusion.1 = f32[24576,4]{1,0:T(8,128)} fusion(f32[4,32768]{0,1:T(8,128)} %bitcast.148, s32[24576]{0:T(1024)S(1)} %broadcast_clamp_fusion), kind=kCustom, calls=%fused_computation.1 | custom fusion | bytes 884736 | tf_op jit(solution)/shard_map/jit(_take)/gather | solution.py:325
  332.4 21.6 %copy.178 = f32[384,8,8,4]{2,1,3,0:T(8,128)} copy(f32[384,8,8,4]{3,2,1,0:T(8,128)} %bitcast.151) | data formatting | bytes 786432 | tf_op jit(solution)/shard_map/jit(_take)/gather | solution.py:325
  354.0 1.3 copy.176
  355.3 0.6 copy.189
  355.9 0.6 copy.191
  356.5 5.1 all-to-all-start.1
  361.6 8.0 %convolution_add_fusion = f32[4,8,32,128]{3,0,2,1:T(4,128)} fusion(f32[4,8,32,128]{3,0,2,1:T(4,128)} %bitcast.155, f32[4,8,32,128]{3,0,2,1:T(4,128)} %reshape.753, f32[4,1,32,128]{3,0,2,1:T(4,128)} %copy-done.13, f32[4,1,32,128]{3,0,2,1:T(4,128)} %copy-done.12, f32[4,10,1,128]{3,0,2,1:T(4,128)} %collective-permute-done.2, ...), kind=kOutput, calls=%fused_computation.23 | convolution fusion | flops 15466496 | bytes 2277404 | tf_op jit(solution)/shard_map/vw,wxyz->vxyz/dot_general | solution.py:185
  369.6 9.1 %copy.180 = f32[4,32768]{0,1:T(8,128)} copy(f32[4,32768]{1,0:T(4,128)} %bitcast.157) | data formatting | bytes 1048576 | tf_op jit(solution)/shard_map/reshape | solution.py:332
  378.8 2.0 copy.169
  380.8 2.0 reshape.698
  382.8 6.9 %copy.170 = f32[384,4,8,8]{2,3,1,0:T(8,128)} copy(f32[384,4,8,8]{0,3,2,1:T(8,128)} %reshape.698) | data formatting | bytes 786432 | tf_op jit(solution)/shard_map/reshape | solution.py:321
  389.7 85.5 %fusion.95 = f32[384,4,8,8]{2,3,1,0:T(8,128)S(1)} fusion(f32[384,4,8,8]{2,3,1,0:T(8,128)} %copy.170, f32[384,8,8,1]{2,1,3,0:T(8,128)S(1)} %copy.189), kind=kOutput, calls=%fused_computation.229 | convolution fusion | flops 9437184 | bytes 884736 | tf_op jit(solution)/shard_map/rik,rvkl,rjl->vrij/dot_general | solution.py:238
  475.2 9.9 %fusion.1 = f32[384,8,8,4]{2,1,3,0:T(8,128)} fusion(f32[384,8,8,4]{2,1,3,0:T(8,128)} %copy.178, f32[384,8,8]{2,1,0:T(8,128)S(1)} %copy-done.5, f32[4,384]{0,1:T(8,128)S(1)} %broadcast_multiply_fusion.2, pred[384,8,8]{2,1,0:T(8,128)(4,1)S(1)} %copy-done.8, f32[384,4,8,8]{2,3,1,0:T(8,128)S(1)} %fusion.95, f32[384,8,8,1]{2,1,3,0:T(8,128)S(1)} %copy.191), kind=kOutput, calls=%fused_computation.8 | convolution fusion | flops 9830400 | bytes 1406976 | tf_op jit(solution)/shard_map/rik,rvkl,rjl->vrij/dot_general | solution.py:238
  485.1 20.8 %copy.205 = f32[384,8,8,4]{3,2,1,0:T(8,128)} copy(f32[384,8,8,4]{2,1,3,0:T(8,128)} %fusion.1) | data formatting | bytes 786432 | tf_op jit(solution)/shard_map/mul | solution.py:332
  505.9 129.1 %scatter_fusion = f32[4,32768]{0,1:T(8,128)} fusion(f32[4,32768]{0,1:T(8,128)} %copy.180, s32[24576]{0:T(1024)S(1)} %reshape.734, f32[24576,4]{1,0:T(8,128)} %bitcast.150), kind=kCustom, calls=%fused_computation.4 | custom fusion | flops 98304 | bytes 1277952 | tf_op jit(solution)/shard_map/scatter-add | solution.py:332
  635.1 11.4 %broadcast_multiply_fusion = f32[4,32768]{0,1:T(8,128)} fusion(f32[4,32768]{0,1:T(8,128)} %scatter_fusion), kind=kLoop, calls=%fused_computation.5 | loop fusion | flops 131072 | bytes 1048576 | tf_op jit(solution)/shard_map/mul | solution.py:334
  646.5 10.1 %copy.182 = f32[1,4,8,32,128]{4,3,2,1,0:T(8,128)S(1)} copy(f32[1,4,8,32,128]{1,4,3,2,0:T(8,128)} %bitcast.149) | data formatting | bytes 1048576 | tf_op jit(solution)/shard_map/mul | solution.py:334
  656.6 1.2 multiply_add_fusion.1
  (83 shorter events, 3.7 us)
Async XLA Ops:
  0.6 361.0 %copy-start = (f32[2,4,4]{2,1,0:T(4,128)S(1)}, f32[2,4,4]{2,1,0:T(4,128)}, u32[]{:S(2)}) copy-start(f32[2,4,4]{2,1,0:T(4,128)} %param.20) | copy-start | bytes 388
  8.2 198.0 %collective-permute-start.4 = (s32[384,4]{1,0:T(8,128)}, s32[384,4]{1,0:T(8,128)}, u32[]{:S(2)}, u32[]{:S(2)}) collective-permute-start(s32[384,4]{1,0:T(8,128)} %scatter_custom_fusion), channel_id=1, source_target_pairs={{0,2},{2,0},{1,3},{3,1},{4,6},{6,4},{5,7},{7,5},{8,10},{10,8},{9,1... | collective-permute-start | bytes 18440 | tf_op jit(solution)/shard_map/ppermute | solution.py:21
  69.9 11.5 %copy-start.11 = (f32[3,8,8]{2,0,1:T(4,128)S(1)}, f32[3,8,8]{2,0,1:T(4,128)}, u32[]{:S(2)}) copy-start(f32[3,8,8]{2,0,1:T(4,128)} %constant.288.clone) | copy-start | bytes 2308
  84.3 4.5 copy-start.6
  97.8 258.6 %collective-permute-start.5 = (f32[384,256]{1,0:T(8,128)}, f32[384,256]{1,0:T(8,128)}, u32[]{:S(2)}, u32[]{:S(2)}) collective-permute-start(f32[384,256]{1,0:T(8,128)} %scatter_custom_fusion.1), channel_id=1, source_target_pairs={{0,2},{2,0},{1,3},{3,1},{4,6},{6,4},{5,7},{7,5},{8,10},{10,8},{9,1... | collective-permute-start | bytes 1179656 | tf_op jit(solution)/shard_map/ppermute | solution.py:21
  99.3 139.7 %copy-start.7 = (f32[1,4,8,32,128]{4,1,3,2,0:T(4,128)}, f32[1,4,8,32,128]{4,1,3,2,0:T(4,128)S(1)}, u32[]{:S(2)}) copy-start(f32[1,4,8,32,128]{4,1,3,2,0:T(4,128)S(1)} %copy.217) | copy-start | bytes 1572868
  99.3 139.6 %collective-permute-start = (f32[4,1,32,128]{3,0,2,1:T(4,128)S(1)}, f32[4,1,32,128]{3,0,2,1:T(4,128)S(1)}, u32[]{:S(2)}, u32[]{:S(2)}) collective-permute-start(f32[4,1,32,128]{3,0,2,1:T(4,128)S(1)} %get-tuple-element.14), channel_id=1, source_target_pairs={{0,4},{4,8},{8,12},{1,5},{5,9},{9,13},{2,6},{6,10},{10,14},{3,7},{... | collective-permute-start | bytes 196616 | tf_op jit(solution)/shard_map/ppermute | solution.py:31
  104.2 134.7 %collective-permute-start.1 = (f32[4,1,32,128]{3,0,2,1:T(4,128)S(1)}, f32[4,1,32,128]{3,0,2,1:T(4,128)S(1)}, u32[]{:S(2)}, u32[]{:S(2)}) collective-permute-start(f32[4,1,32,128]{3,0,2,1:T(4,128)S(1)} %get-tuple-element.15), channel_id=1, source_target_pairs={{4,0},{8,4},{12,8},{5,1},{9,5},{13,9},{6,2},{10,6},{14,10},{7,3},{... | collective-permute-start | bytes 196616 | tf_op jit(solution)/shard_map/ppermute | solution.py:32
  119.4 9.1 %copy-start.16 = (f32[2,3]{1,0:T(2,128)S(1)}, f32[2,3]{1,0:T(2,128)}, u32[]{:S(2)}) copy-start(f32[2,3]{1,0:T(2,128)} %param.19) | copy-start | bytes 76
  119.4 9.7 %copy-start.14 = (f32[8,8,1,1,1,1]{1,0,5,4,3,2:T(8,128)S(1)}, f32[8,8,1,1,1,1]{1,0,5,4,3,2:T(8,128)}, u32[]{:S(2)}) copy-start(f32[8,8,1,1,1,1]{1,0,5,4,3,2:T(8,128)} %constant.305) | copy-start | bytes 772
  129.2 61.6 %copy-start.2 = (f32[4,8,4,8,16,8]{4,3,5,2,1,0:T(8,128)S(1)}, f32[4,8,4,8,16,8]{4,3,5,2,1,0:T(8,128)}, u32[]{:S(2)}) copy-start(f32[4,8,4,8,16,8]{4,3,5,2,1,0:T(8,128)} %copy.149) | copy-start | bytes 1572868
  190.8 3.8 copy-start.3
  194.6 19.4 %copy-start.17 = (f32[2,4]{1,0:T(2,128)S(1)}, f32[2,4]{1,0:T(2,128)}, u32[]{:S(2)}) copy-start(f32[2,4]{1,0:T(2,128)} %param.21) | copy-start | bytes 100
  207.8 24.2 %all-to-all-start = ((s32[4,96,4]{1,2,0:T(4,128)}), s32[4,96,4]{1,2,0:T(4,128)S(1)}, u32[]{:S(2)}, u32[]{:S(2)}) async-start(s32[4,96,4]{1,2,0:T(4,128)} %copy.159), calls=%async_computation | async-start | bytes 16384 | tf_op jit(solution)/shard_map/all_to_all | solution.py:309
  224.9 11.3 %copy-start.15 = (f32[3,8]{1,0:T(4,128)S(1)}, f32[3,8]{1,0:T(4,128)}, u32[]{:S(2)}) copy-start(f32[3,8]{1,0:T(4,128)} %constant.290.clone) | copy-start | bytes 292
  232.1 6.6 %copy-start.10 = (f32[3,8,8]{2,0,1:T(4,128)S(1)}, f32[3,8,8]{2,0,1:T(4,128)}, u32[]{:S(2)}) copy-start(f32[3,8,8]{2,0,1:T(4,128)} %constant.289.clone) | copy-start | bytes 2308
  239.0 93.4 %copy-start.12 = (f32[4,1,32,128]{3,0,2,1:T(4,128)}, f32[4,1,32,128]{3,0,2,1:T(4,128)S(1)}, u32[]{:S(2)}) copy-start(f32[4,1,32,128]{3,0,2,1:T(4,128)S(1)} %collective-permute-done) | copy-start | bytes 196612
  239.0 93.4 %copy-start.13 = (f32[4,1,32,128]{3,0,2,1:T(4,128)}, f32[4,1,32,128]{3,0,2,1:T(4,128)S(1)}, u32[]{:S(2)}) copy-start(f32[4,1,32,128]{3,0,2,1:T(4,128)S(1)} %collective-permute-done.1) | copy-start | bytes 196612
  239.6 121.9 %collective-permute-start.2 = (f32[4,10,1,128]{3,0,2,1:T(4,128)}, f32[4,10,1,128]{3,0,2,1:T(4,128)}, u32[]{:S(2)}, u32[]{:S(2)}) collective-permute-start(f32[4,10,1,128]{3,0,2,1:T(4,128)} %get-tuple-element.13), channel_id=1, source_target_pairs={{0,1},{2,3},{4,5},{6,7},{8,9},{10,11},{12,13},{14,15},{16,17},{18,... | collective-permute-start | bytes 61448 | tf_op jit(solution)/shard_map/ppermute | solution.py:31
  243.6 118.0 %collective-permute-start.3 = (f32[4,10,1,128]{3,0,2,1:T(4,128)}, f32[4,10,1,128]{3,0,2,1:T(4,128)}, u32[]{:S(2)}, u32[]{:S(2)}) collective-permute-start(f32[4,10,1,128]{3,0,2,1:T(4,128)} %get-tuple-element.12), channel_id=1, source_target_pairs={{1,0},{3,2},{5,4},{7,6},{9,8},{11,10},{13,12},{15,14},{17,16},{19,... | collective-permute-start | bytes 61448 | tf_op jit(solution)/shard_map/ppermute | solution.py:32
  356.5 22.3 %all-to-all-start.1 = ((f32[4,96,256]{2,1,0:T(8,128)}), f32[4,96,256]{2,1,0:T(8,128)}, u32[]{:S(2)}, u32[]{:S(2)}) async-start(f32[4,96,256]{2,1,0:T(8,128)} %bitcast.42), calls=%async_computation.1 | async-start | bytes 786432 | tf_op jit(solution)/shard_map/all_to_all | solution.py:308
  389.7 85.5 %copy-start.5 = (f32[384,8,8]{2,1,0:T(8,128)S(1)}, f32[384,8,8]{2,1,0:T(8,128)}, u32[]{:S(2)}) copy-start(f32[384,8,8]{2,1,0:T(8,128)} %broadcast_multiply_fusion.1) | copy-start | bytes 294916
  389.7 85.5 %copy-start.8 = (pred[384,8,8]{2,1,0:T(8,128)(4,1)S(1)}, pred[384,8,8]{2,1,0:T(8,128)(4,1)}, u32[]{:S(2)}) copy-start(pred[384,8,8]{2,1,0:T(8,128)(4,1)} %copy.176) | copy-start | bytes 73732
  646.5 10.1 %copy-start.4 = (f32[1,4,8,32,128]{4,3,2,1,0:T(8,128)S(1)}, f32[1,4,8,32,128]{4,3,2,1,0:T(8,128)}, u32[]{:S(2)}) copy-start(f32[1,4,8,32,128]{4,3,2,1,0:T(8,128)} %param.17) | copy-start | bytes 1572868
  646.5 10.1 %copy-start.9 = (f32[1,4,8,32,128]{4,3,2,1,0:T(8,128)S(1)}, f32[1,4,8,32,128]{4,3,2,1,0:T(8,128)}, u32[]{:S(2)}) copy-start(f32[1,4,8,32,128]{4,3,2,1,0:T(8,128)} %param.18) | copy-start | bytes 1572868
  646.5 11.3 %copy-start.1 = (f32[2,4,4]{2,1,0:T(4,128)S(1)}, f32[2,4,4]{2,1,0:T(4,128)}, u32[]{:S(2)}) copy-start(f32[2,4,4]{2,1,0:T(4,128)} %param.20) | copy-start | bytes 388
where the time goes:
time: 663 us; the launch traced here: 658 us
  local copies, waits for them, and re-layouts  279 us (42%)
  matrix products  191 us (29%)
  other arithmetic  159 us (24%)
  starting transfers between devices  23.2 us (3%)
    scatter-add x1, other arithmetic, on_device(): rate.reshape(variables, -1).at[:, target_index].add(term * scale)  129 us
    gather x2, local copies, waits for them, and re-layouts, on_device(): own = jnp.take(flat_field, target_index, axis=1)  109 us
    dot_general x2, matrix products, evaluate(): jnp.einsum('rik,rvkl,rjl->vrij', first_table, coefs, second_table, precis...  95.4 us
    dot_general x1, matrix products, volume_rate(): jnp.einsum('mk,vaibjck->vaibjcm', derivative, shaped, precision=highest)  61.6 us
    gather x2, local copies, waits for them, and re-layouts, on_device(): values = jnp.take(flat_field, source_index, axis=1)  58.2 us
    another operation x6, local copies, waits for them, and re-layouts  20.9 us
    mul x1, local copies, waits for them, and re-layouts, on_device(): term * scale  20.8 us
    neg x2, local copies, waits for them, and re-layouts, volume_rate(): return -total.reshape(field.shape)  14.2 us
  transfers between devices with their start and end apart: 8, of which 0 were waited for; matrix products, arithmetic and copies ran while one was open for 52% of the time, Pallas kernels for 0%

commit v1 on v0

v1 whole, which is shorter than its diff:
```python
import functools
import math

import jax
import jax.numpy as jnp
import ml_dtypes
import numpy as np
from jax import lax
from jax.experimental import pallas as pl
from jax.experimental.pallas import tpu as pltpu
from jax.sharding import PartitionSpec as P

NODES = 8
EY = 4
EZ = 16
FACES = 384
CODES = 8

upwind_share = 0.5
register_keep = -0.4178904745
section_weight = 1.7201463215
time_step = 0.05

f32 = jnp.float32
bf16 = jnp.bfloat16


def legendre_values(point, count):
    values = [1.0, point]
    for power in range(2, count):
        values.append(
            ((2 * power - 1) * point * values[power - 1] - (power - 1) * values[power - 2]) / power
        )
    return values[:count]


def lagrange_rows(points, targets):
    total = len(points)
    result = np.ones((len(targets), total))
    for row, target in enumerate(targets):
        for column in range(total):
            for other in range(total):
                if other != column:
                    result[row, column] *= (target - points[other]) / (
                        points[column] - points[other]
                    )
    return result


@functools.lru_cache
def node_tables(nodes):
    degree = nodes - 1
    guesses = [math.cos(math.pi * position / degree) for position in range(nodes)]
    for sweep in range(100):
        updated = []
        for point in guesses:
            values = legendre_values(point, nodes)
            updated.append(
                point - (point * values[degree] - values[degree - 1]) / (nodes * values[degree])
            )
        guesses = updated
    points = sorted(guesses)
    points[0] = -1.0
    points[-1] = 1.0
    basis = np.array([legendre_values(point, nodes) for point in points])
    inverse = np.linalg.inv(basis)
    barycentric = []
    for position in range(nodes):
        product = 1.0
        for other in range(nodes):
            if other != position:
                product = product * (points[position] - points[other])
        barycentric.append(1.0 / product)
    derivative = np.zeros((nodes, nodes))
    for position in range(nodes):
        for other in range(nodes):
            if other != position:
                derivative[position, other] = (
                    barycentric[other] / barycentric[position] / (points[position] - points[other])
                )
        derivative[position, position] = -derivative[position].sum()
    mask = np.array([[point < 0 for point in points], [point > 0 for point in points]], np.float64)
    fine = [lagrange_rows(points, [(point + shift) / 2.0 for point in points]) for shift in (-1, 1)]
    coarse = []
    for half, shift in ((0, 1.0), (1, -1.0)):
        values = np.array([legendre_values(2.0 * point + shift, nodes) for point in points])
        coarse.append((values * mask[half][:, None]) @ inverse)
    return derivative, degree * nodes / 2.0, fine, coarse


def two_parts(matrix):
    high = matrix.astype(np.float32).astype(ml_dtypes.bfloat16)
    low = (matrix - high.astype(np.float64)).astype(ml_dtypes.bfloat16)
    return high, low


@functools.lru_cache
def face_maps():
    _, _, fine, coarse = node_tables(NODES)
    maps = []
    for tables in (fine, coarse):
        for quadrant in range(4):
            first, second = tables[quadrant // 2], tables[quadrant % 2]
            one = np.kron(second.T, first.T)
            maps.append(np.kron(np.eye(2), one))
    return two_parts(np.concatenate(maps, axis=1))


def split(values):
    high = values.astype(bf16)
    return high, (values - high.astype(f32)).astype(bf16)


def dot(left, right):
    return lax.dot_general(left, right, (((1,), (0,)), ((), ())), preferred_element_type=f32)


def dot_t(left, right):
    return lax.dot_general(left, right, (((1,), (1,)), ((), ())), preferred_element_type=f32)


def iota(shape, dim):
    return lax.broadcasted_iota(jnp.int32, shape, dim)


def one(condition):
    return jnp.where(condition, 1.0, 0.0).astype(bf16)


def twice(matrix):
    return jnp.concatenate([matrix, matrix], axis=0)


def block_transpose(parts):
    parts = list(parts)
    block = iota(parts[0].shape, 1) // 16
    for bit in (1, 2, 4):
        upper = (block & bit) != 0
        for g in range(8):
            if g & bit:
                continue
            low, high = parts[g], parts[g | bit]
            parts[g] = jnp.where(upper, pltpu.roll(high, 16 * bit, 1), low)
            parts[g | bit] = jnp.where(upper, high, pltpu.roll(low, 128 - 16 * bit, 1))
    return parts


def lane_order(inverse):
    row, column = iota((128, 128), 1 if inverse else 0), iota((128, 128), 0 if inverse else 1)
    return one(((row // 8) == (column % 16)) & ((row % 8) == (column // 16)))


def end_lanes(ey, inverse):
    z, lane = iota((128, 128), 1 if inverse else 0), iota((128, 128), 0 if inverse else 1)
    return one(
        (lane // 32 == ey) & (z // 8 == lane % 16) & (z % 8 == (NODES - 1) * ((lane // 16) % 2))
    )


def y_row(ref, y):
    return ref[pl.ds(y, 32, stride=32), :]


def face_number(elem, side):
    direction, end = side >> 1, side & 1
    ey, ez = elem >> 4, elem & 15
    group = jnp.where(direction == 2, 16 + 2 * ey + end, direction * 8 + end * 4 + ey)
    return group, ez


def send_kernel(
    ranks, slots, field, elem, side, code, rank, p_elem, p_side, p_quadrant, count, high, low,
    *outs,
):
    messages, faces_out = outs[:ranks], outs[ranks]
    capacity = elem.shape[1]
    me = lax.axis_index("elem")
    used = iota((1, capacity), 1) < count[0, 0]
    group, ez = face_number(elem[...], side[...])
    codes = code[...]
    map_index = jnp.where(codes == 5, 5 + p_quadrant[...], codes)
    apart = rank[...] - me
    apart = jnp.where(apart < 0, apart + ranks, apart)
    apart = jnp.where(used, apart, 200)
    to_group, to_ez = face_number(p_elem[...], p_side[...])
    kind = jnp.where(used, jnp.where(codes == 5, 2 + p_quadrant[...], 1), 0)
    rows = [group, ez, map_index, apart, to_group, to_ez, kind]
    head = jnp.concatenate(
        [row.astype(f32) for row in rows] + [jnp.zeros((1, capacity), f32)], axis=0
    ).astype(bf16)
    here, there = iota((capacity, capacity), 0), iota((capacity, capacity), 1)
    columns = dot_t(one(here == there), head)
    earlier = (columns[:, 3:4] == apart.astype(f32)) & (here < there)
    position = jnp.sum(jnp.where(earlier, 1.0, 0.0), axis=0, keepdims=True)
    slot = apart * slots + position.astype(jnp.int32)

    order = lane_order(False)
    parts = []
    for kind_of in (0, 1):
        blocks = []
        for end in (0, 1):
            for ey in range(EY):
                if kind_of == 0:
                    blocks += [
                        field[pl.ds(v * 256 + (NODES - 1) * end * 32 + ey * 8, 8), :]
                        for v in range(4)
                    ]
                else:
                    blocks.append(y_row(field, ey * 8 + (NODES - 1) * end))
        stacked_high, stacked_low = split(jnp.concatenate(blocks, axis=0))
        moved = dot(jnp.concatenate([stacked_high, stacked_low], axis=1), twice(order))
        turned = block_transpose([moved[g * 32 : (g + 1) * 32] for g in range(8)])
        parts.append(
            jnp.concatenate(
                [turned[b][v * 8 : (v + 1) * 8] for v in range(4) for b in range(8)], axis=0
            )
        )
    ends = jnp.zeros((256, 128), f32)
    for ey in range(EY):
        lines = [y_row(field, ey * 8 + b) for b in range(8)]
        stacked = jnp.concatenate(
            [lines[b][v * 8 : (v + 1) * 8] for v in range(4) for b in range(8)], axis=0
        )
        stacked_high, stacked_low = split(stacked)
        ends += dot(
            jnp.concatenate([stacked_high, stacked_low], axis=1), twice(end_lanes(ey, False))
        )
    parts.append(ends)
    faces = jnp.concatenate(parts, axis=1)
    faces_out[...] = faces

    faces_high, faces_low = split(faces)
    source = (columns[:, 0:1] * 16.0 + columns[:, 1:2]).astype(jnp.int32)
    picked = one(source == iota((capacity, FACES), 1))
    values = dot_t(picked, faces_high) + dot_t(picked, faces_low)
    which = columns[:, 2:3]
    mapped = []
    for half in range(2):
        part = values[:, half * 128 : (half + 1) * 128]
        part_high, part_low = split(part)
        out = dot(jnp.concatenate([part_high, part_low], axis=1), twice(high[...])) + dot(
            part_high, low[...]
        )
        result = part
        for index in range(CODES):
            result = jnp.where(
                which == float(index + 1), out[:, index * 128 : (index + 1) * 128], result
            )
        mapped.append(result)
    mapped_high, mapped_low = split(jnp.concatenate(mapped, axis=1))
    for k in range(ranks):
        placed = one(iota((slots, capacity), 0) + k * slots == slot)
        messages[k][0:slots, :] = dot(placed, mapped_high) + dot(placed, mapped_low)
        messages[k][slots : slots + 8, :] = jnp.zeros((8, 256), f32)
        messages[k][slots : slots + 8, 0:slots] = dot_t(head, placed)


def local_kernel(field, register, advect, mixing, derivative_y, derivative_z, base):
    comp = lax.axis_index("comp")
    derivative, scale, _, _ = node_tables(NODES)
    left, right, speed = [], [], []
    for d in range(3):
        a = advect[comp, d]
        speed.append(a)
        left.append(scale * (0.5 * a + 0.5 * upwind_share * jnp.abs(a)))
        right.append(scale * (0.5 * upwind_share * jnp.abs(a) - 0.5 * a))

    def both_ways(row, column, node, gain_left, gain_right):
        first, last = node == 0, node == NODES - 1
        out = jnp.where((row == column) & first, -gain_left, 0.0)
        out = jnp.where((row == column) & last, -gain_right, out)
        out = jnp.where((row == column - 1) & first, gain_left, out)
        return jnp.where((row == column + 1) & last, gain_right, out)

    row, column = iota((128, 128), 0), iota((128, 128), 1)
    along_z = both_ways(row, column, column % 8, left[2], right[2]) - speed[2] * derivative_z[...]
    z_high, z_low = split(along_z)
    z_high = twice(z_high)
    row, column = iota((256, 256), 0), iota((256, 256), 1)
    node = row % 8
    across = -speed[0] * derivative_y[...]
    across += jnp.where((row == column) & (node == 0), -left[0], 0.0)
    across += jnp.where((row == column) & (node == NODES - 1), -right[0], 0.0)
    same = (row // 32 == column // 32) & (node == column % 8)
    mixed = jnp.zeros((256, 256), f32)
    for v in range(4):
        for w in range(4):
            mixed = jnp.where(
                ((row // 8) % 4 == v) & ((column // 8) % 4 == w), mixing[comp, v, w], mixed
            )
    across += jnp.where(same, mixed, 0.0)
    across_high, across_low = split(across)

    for ey in range(EY):
        lines = [y_row(field, ey * 8 + j) for j in range(8)]
        stacked = jnp.concatenate(lines, axis=0)
        stacked_high, stacked_low = split(stacked)
        rate = dot(jnp.concatenate([stacked_high, stacked_low], axis=1), z_high)
        rate += dot(stacked_high, z_low)
        pair = dot(across_high, jnp.concatenate([stacked_high, stacked_low], axis=1))
        rate += pair[:, :128] + pair[:, 128:] + dot(across_low, stacked_high)
        along_y = []
        for m in range(8):
            total = float(derivative[m, 0]) * lines[0]
            for j in range(1, 8):
                total += float(derivative[m, j]) * lines[j]
            total = -speed[1] * total
            if m == 0:
                total -= left[1] * lines[0]
                if ey > 0:
                    total += left[1] * y_row(field, ey * 8 - 1)
            if m == NODES - 1:
                total -= right[1] * lines[m]
                if ey < EY - 1:
                    total += right[1] * y_row(field, ey * 8 + 8)
            along_y.append(total)
        rate += jnp.concatenate(along_y, axis=0)
        kept = jnp.concatenate([y_row(register, ey * 8 + j) for j in range(8)], axis=0)
        base[ey * 256 : (ey + 1) * 256, :] = register_keep * kept + time_step * rate


def finish_kernel(ranks, slots, *refs):
    messages = refs[:ranks]
    (base, field, faces, x_before, x_after, y_before, y_after, advect, drag, new, advanced) = refs[
        ranks:
    ]
    comp = lax.axis_index("comp")
    scale = node_tables(NODES)[1]
    total = jnp.zeros((FACES, 256), f32)
    masks = jnp.zeros((16, FACES), f32)
    for k in range(ranks):
        head = messages[k][slots : slots + 8, 0:slots]
        kind = head[6:7]
        target = jnp.where(kind > 0.0, head[4:5] * 16.0 + head[5:6], -1.0).astype(jnp.int32)
        placed = one(iota((FACES, slots), 0) == target)
        values_high, values_low = split(messages[k][0:slots, :])
        total += dot(placed, values_high) + dot(placed, values_low)
        row = iota((16, slots), 0)
        quadrant = ((row % 8) // 4) * 2 + row // 8
        live = (kind == 1.0) | (kind == 2.0 + quadrant.astype(f32))
        masks += dot_t(one(live & (kind > 0.0)), placed)
    total = total.T
    terms = []
    for v in range(4):
        gain = drag[comp, v] * (scale * time_step)
        for b in range(8):
            rows = pl.ds((v * 8 + b) * 8, 8)
            count = masks[0:8] if b < 4 else masks[8:16]
            at = (v * 8 + b) * 8
            terms.append(gain * (total[at : at + 8] - count * faces[rows, :]))
    order = twice(lane_order(True))
    on_x = on_y = None
    for kind_of in (0, 1):
        lanes = slice(kind_of * 128, kind_of * 128 + 128)
        turned = block_transpose(
            [jnp.concatenate([terms[v * 8 + b][:, lanes] for v in range(4)], axis=0) for b in range(8)]
        )
        high, low = split(jnp.concatenate(turned, axis=0))
        moved = dot(jnp.concatenate([high, low], axis=1), order)
        if kind_of == 0:
            on_x = moved
        else:
            on_y = moved
    high, low = split(jnp.concatenate([term[:, 256:384] for term in terms], axis=0))
    ends = jnp.concatenate([high, low], axis=1)
    flux = [jnp.abs(advect[comp, d]) for d in range(2)]
    left = [
        time_step * scale * (0.5 * advect[comp, d] + 0.5 * upwind_share * flux[d]) for d in range(2)
    ]
    right = [
        time_step * scale * (0.5 * upwind_share * flux[d] - 0.5 * advect[comp, d]) for d in range(2)
    ]
    for ey in range(EY):
        on_z = dot(ends, twice(end_lanes(ey, True)))
        for j in range(8):
            y = ey * 8 + j
            rate = base[y * 32 : (y + 1) * 32, :]
            rate += jnp.concatenate(
                [on_z[(v * 8 + j) * 8 : (v * 8 + j) * 8 + 8] for v in range(4)], axis=0
            )
            if j in (0, NODES - 1):
                g = (4 if j else 0) + ey
                rate += on_y[g * 32 : (g + 1) * 32]
            if y == 0:
                rate += left[1] * y_before[...]
            if y == 31:
                rate += right[1] * y_after[...]
            new[pl.ds(y, 32, stride=32), :] = rate
    for end in (0, 1):
        for v in range(4):
            at = v * 256 + (NODES - 1) * end * 32
            rows = pl.ds(at, 32)
            coupled = jnp.concatenate(
                [on_x[((end * 4 + ey) * 4 + v) * 8 : ((end * 4 + ey) * 4 + v) * 8 + 8] for ey in range(EY)],
                axis=0,
            )
            beside = left[0] * x_before[v * 32 : v * 32 + 32, :] if end == 0 else right[0] * x_after[v * 32 : v * 32 + 32, :]
            new[rows, :] = new[rows, :] + coupled + beside
    for at in range(0, 1024, 128):
        rows = pl.ds(at, 128)
        advanced[rows, :] = field[rows, :] + section_weight * new[rows, :]


def along(layer, axis, step):
    devices = lax.axis_size(axis)
    pairs = [(i, i + step) for i in range(devices) if 0 <= i + step < devices]
    return lax.ppermute(layer, axis, pairs)


def on_device(
    field, register, advect, mixing, drag, face_elem, face_side, mortar_code, partner_rank,
    partner_elem, partner_side, partner_quadrant, face_count,
):
    ranks = lax.axis_size("elem")
    capacity = face_elem.shape[-1]
    slots = max(2, 2 * capacity // ranks)
    block = field[0]
    flat = field.reshape(1024, 128)
    x_before = along(block[:, -1], "elem", 1).reshape(128, 128)
    x_after = along(block[:, 0], "elem", -1).reshape(128, 128)
    y_before = along(block[:, :, -1], "sub", 1).reshape(32, 128)
    y_after = along(block[:, :, 0], "sub", -1).reshape(32, 128)

    vmem = pl.BlockSpec(memory_space=pltpu.VMEM)
    smem = pl.BlockSpec(memory_space=pltpu.SMEM)
    row = (1, capacity)
    map_high, map_low = face_maps()
    outs = pl.pallas_call(
        functools.partial(send_kernel, ranks, slots),
        out_shape=[jax.ShapeDtypeStruct((slots + 8, 256), f32)] * ranks
        + [jax.ShapeDtypeStruct((256, FACES), f32)],
        in_specs=[vmem] * 8 + [smem] + [vmem] * 2,
        out_specs=[vmem] * (ranks + 1),
        compiler_params=pltpu.CompilerParams(vmem_limit_bytes=32 << 20),
        cost_estimate=pl.CostEstimate(flops=10**8, bytes_accessed=2 << 20, transcendentals=0),
        name="send_faces",
    )(
        flat, face_elem.reshape(row), face_side.reshape(row), mortar_code.reshape(row),
        partner_rank.reshape(row), partner_elem.reshape(row), partner_side.reshape(row),
        partner_quadrant.reshape(row), face_count.reshape(1, 1), map_high, map_low,
    )
    faces = outs[ranks]
    received = []
    for k in range(ranks):
        pairs = [
            (2 * e + c, 2 * ((e + k) % ranks) + 1 - c) for e in range(ranks) for c in range(2)
        ]
        received.append(lax.ppermute(outs[k], ("elem", "comp"), pairs))

    derivative = node_tables(NODES)[0]
    base = pl.pallas_call(
        local_kernel,
        out_shape=jax.ShapeDtypeStruct((1024, 128), f32),
        in_specs=[vmem, vmem, smem, smem, vmem, vmem],
        out_specs=vmem,
        compiler_params=pltpu.CompilerParams(vmem_limit_bytes=32 << 20),
        cost_estimate=pl.CostEstimate(flops=5 * 10**8, bytes_accessed=4 << 20, transcendentals=0),
        name="local_rate",
    )(
        flat, register.reshape(1024, 128), advect, mixing,
        np.kron(np.eye(32), derivative).astype(np.float32),
        np.kron(np.eye(16), derivative.T).astype(np.float32),
    )
    new, advanced = pl.pallas_call(
        functools.partial(finish_kernel, ranks, slots),
        out_shape=[jax.ShapeDtypeStruct((1024, 128), f32)] * 2,
        in_specs=[vmem] * (ranks + 7) + [smem] * 2,
        out_specs=[vmem] * 2,
        compiler_params=pltpu.CompilerParams(vmem_limit_bytes=32 << 20),
        cost_estimate=pl.CostEstimate(flops=10**8, bytes_accessed=4 << 20, transcendentals=0),
        name="couple_and_finish",
    )(*received, base, flat, faces, x_before, x_after, y_before, y_after, advect, drag)
    return new.reshape(field.shape), advanced.reshape(field.shape)


def solution(mesh):
    block = P("comp", None, ("parts", "elem"), "sub", None)
    records = P("comp", ("parts", "elem"), "sub", None)
    in_specs = (
        block, block, P(), P(), P(), records, records, records,
        P("comp", ("parts", "elem"), "sub", None, None), records, records, records,
        P("comp", ("parts", "elem"), "sub"),
    )
    return jax.shard_map(
        on_device, mesh=mesh, in_specs=in_specs, out_specs=(block, block), check_vma=False
    )
```

time: 663 us -> 34.3 us (0.05)
  the two profiles are of different devices: /device:TPU:0 before, /device:TPU:18 now
where the time goes in v1:
time: 34.3 us; the launch traced here: 34 us
  starting transfers between devices  14.1 us (41%)
  Pallas kernels  7.38 us (22%)
  waiting for transfers between devices  5.74 us (17%)
  local copies, waits for them, and re-layouts  5.33 us (16%)
  between operations  1.49 us (4%)
    ppermute x4, starting transfers between devices, along(): return lax.ppermute(layer, axis, pairs)  11.1 us
    ppermute x4, waiting for transfers between devices, along(): return lax.ppermute(layer, axis, pairs)  5.73 us
    pallas_call x1, Pallas kernels, on_device(): pl.pallas_call(functools.partial(finish_kernel, ranks, slots), out_shape=...  3.49 us
    unnamed x32, local copies, waits for them, and re-layouts  3.4 us
    ppermute x4, starting transfers between devices, on_device(): received.append(lax.ppermute(outs[k], ('elem', 'comp'), pairs))  2.96 us
    pallas_call x1, Pallas kernels, on_device(): pl.pallas_call(local_kernel, out_shape=jax.ShapeDtypeStruct((1024, 128),...  2.04 us
    pallas_call x1, Pallas kernels, on_device(): pl.pallas_call(functools.partial(send_kernel, ranks, slots), out_shape=[j...  1.85 us
    slice x1, local copies, waits for them, and re-layouts, on_device(): y_after = along(block[:, :, 0], 'sub', -1).reshape(32, 128)  1 us
  transfers between devices with their start and end apart: 8, of which 1 were waited for; matrix products, arithmetic and copies ran while one was open for 3% of the time, Pallas kernels for 11%

profile of v1, /device:TPU:18, one launch (start us, length us, event | category | flops | bytes accessed | tf_op | source)
XLA Modules:
  0.0 34.0 jit_solution(13935521672091433027)
XLA Ops:
  0.6 0.0 copy-start.3
  0.6 0.9 %slice_bitcast_fusion = (f32[4,32,128]{2,1,0:T(8,128)S(1)}, f32[4,32,128]{2,1,0:T(8,128)S(1)}) fusion(f32[4,8,32,128]{3,2,1,0:T(8,128)} %bitcast.24), kind=kLoop, calls=%fused_computation | loop fusion | bytes 262144 | tf_op jit(solution)/shard_map/squeeze | solution.py:420
  1.6 2.4 %collective-permute-start.5 = (f32[4,32,128]{2,1,0:T(8,128)S(1)}, f32[4,32,128]{2,1,0:T(8,128)S(1)}, u32[]{:S(2)}, u32[]{:S(2)}) collective-permute-start(f32[4,32,128]{2,1,0:T(8,128)S(1)} %get-tuple-element.18), channel_id=1, source_target_pairs={{4,0},{8,4},{12,8},{5,1},{9,5},{13,9},{6,2},{10,6},{14,10},{7,3},{... | collective-permute-start | bytes 196616 | tf_op jit(solution)/shard_map/ppermute | solution.py:407
  3.9 1.0 %fusion = (f32[4,8,1,128]{3,2,1,0:T(1,128)S(1)}, f32[4,8,1,128]{3,2,1,0:T(1,128)S(1)}) fusion(f32[4,8,32,128]{3,2,1,0:T(8,128)} %bitcast.25), kind=kLoop, calls=%fused_computation.2 | loop fusion | bytes 65536 | tf_op jit(solution)/shard_map/slice | solution.py:422
  4.9 1.3 %collective-permute-start.6 = (f32[4,8,128]{2,1,0:T(8,128)S(1)}, f32[4,8,128]{2,1,0:T(8,128)S(1)}, u32[]{:S(2)}, u32[]{:S(2)}) collective-permute-start(f32[4,8,128]{2,1,0:T(8,128)S(1)} %bitcast.42), channel_id=1, source_target_pairs={{0,1},{2,3},{4,5},{6,7},{8,9},{10,11},{12,13},{14,15},{16,17},{18,... | collective-permute-start | bytes 49160 | tf_op jit(solution)/shard_map/ppermute | solution.py:407
  6.2 4.5 %collective-permute-start.7 = (f32[4,8,128]{2,1,0:T(8,128)S(1)}, f32[4,8,128]{2,1,0:T(8,128)S(1)}, u32[]{:S(2)}, u32[]{:S(2)}) collective-permute-start(f32[4,8,128]{2,1,0:T(8,128)S(1)} %bitcast.41), channel_id=1, source_target_pairs={{1,0},{3,2},{5,4},{7,6},{9,8},{11,10},{13,12},{15,14},{17,16},{19,... | collective-permute-start | bytes 49160 | tf_op jit(solution)/shard_map/ppermute | solution.py:407
  11.4 0.0 copy-start.13
  11.4 0.0 copy-start.14
  11.5 0.0 copy-start.9
  11.5 0.0 copy-start.10
  11.5 0.0 copy-start.11
  11.5 0.0 copy-start.12
  11.5 0.0 copy-start.8
  11.5 0.0 copy-done.3
  11.5 0.6 %copy-done.13 = s32[1,1,1,192]{3,2,1,0:T(1,128)S(1)} copy-done((s32[1,1,1,192]{3,2,1,0:T(1,128)S(1)}, s32[1,1,1,192]{3,2,1,0:T(1,128)}, u32[]{:S(2)}) %copy-start.13) | copy-done | bytes 792
  12.1 0.0 copy-done.14
  12.1 0.0 copy-done.9
  12.2 0.0 copy-done.10
  12.2 0.0 copy-done.11
  12.2 0.0 copy-done.12
  12.2 0.0 copy-done.8
  12.2 0.0 copy-start
  12.2 1.0 %copy-done = f32[1,4,8,32,128]{4,3,2,1,0:T(8,128)S(1)} copy-done((f32[1,4,8,32,128]{4,3,2,1,0:T(8,128)S(1)}, f32[1,4,8,32,128]{4,3,2,1,0:T(8,128)}, u32[]{:S(2)}) %copy-start) | copy-done | bytes 524312
  13.3 0.0 copy-start.4
  13.3 0.9 %copy-done.4 = bf16[128,1024]{1,0:T(8,128)(2,1)S(1)} copy-done((bf16[128,1024]{1,0:T(8,128)(2,1)S(1)}, bf16[128,1024]{1,0:T(8,128)(2,1)}, u32[]{:S(2)}) %copy-start.4) | copy-done | bytes 262168
  14.2 0.0 copy-start.1
  14.2 0.0 copy-start.2
  14.2 0.0 copy-start.5
  14.2 1.8 %send_faces.1 = (f32[104,256]{1,0:T(8,128)S(1)}, f32[104,256]{1,0:T(8,128)S(1)}, f32[104,256]{1,0:T(8,128)S(1)}, f32[104,256]{1,0:T(8,128)S(1)}, f32[256,384]{1,0:T(8,128)S(1)}) custom-call(f32[1024,128]{1,0:T(8,128)S(1)} %bitcast.26, s32[1,192]{1,0:T(1,128)S(1)} %bitcast.34, s32[1,192]{1,0:T(1,128)S(1)} %bitcast.35, s32[1,192]{1,0:T(1,128)S(1)} %bitcast.36, ...), custom_call_target="tpu_custom_call" | custom-call | flops 100000000 | bytes 2097152 | tf_op jit(solution)/shard_map/send_faces/pallas_call | solution.py:428
  16.1 0.1 collective-permute-start
  16.1 0.0 copy-start.7
  16.2 1.7 %collective-permute-start.1 = (f32[104,256]{1,0:T(8,128)S(1)}, f32[104,256]{1,0:T(8,128)S(1)}, u32[]{:S(2)}, u32[]{:S(2)}) collective-permute-start(f32[104,256]{1,0:T(8,128)S(1)} %get-tuple-element.10), channel_id=1, source_target_pairs={{0,6},{2,4},{4,10},{6,8},{8,14},{10,12},{12,2},{14,0},{1,7},{3,5},... | collective-permute-start | bytes 319496 | tf_op jit(solution)/shard_map/ppermute | solution.py:448
  17.8 0.0 collective-permute-done.6
  17.8 0.0 collective-permute-start.2
  17.8 0.0 collective-permute-done.7
  17.9 1.2 %collective-permute-start.3 = (f32[104,256]{1,0:T(8,128)S(1)}, f32[104,256]{1,0:T(8,128)S(1)}, u32[]{:S(2)}, u32[]{:S(2)}) collective-permute-start(f32[104,256]{1,0:T(8,128)S(1)} %get-tuple-element.12), channel_id=1, source_target_pairs={{0,14},{2,12},{4,2},{6,0},{8,6},{10,4},{12,10},{14,8},{1,15},{3,13... | collective-permute-start | bytes 319496 | tf_op jit(solution)/shard_map/ppermute | solution.py:448
  19.1 0.0 collective-permute-done.5
  19.1 0.0 copy-start.6
  19.1 2.9 %collective-permute-start.4 = (f32[4,32,128]{2,1,0:T(8,128)S(1)}, f32[4,32,128]{2,1,0:T(8,128)S(1)}, u32[]{:S(2)}, u32[]{:S(2)}) collective-permute-start(f32[4,32,128]{2,1,0:T(8,128)S(1)} %get-tuple-element.19), channel_id=1, source_target_pairs={{0,4},{4,8},{8,12},{1,5},{5,9},{9,13},{2,6},{6,10},{10,14},{3,7},{... | collective-permute-start | bytes 196616 | tf_op jit(solution)/shard_map/ppermute | solution.py:407
  22.0 0.0 copy-done.1
  22.0 0.0 copy-done.2
  22.0 0.0 copy-done.5
  22.0 0.0 copy-done.7
  22.0 0.0 copy-done.6
  22.0 2.0 %local_rate.1.refs_4_ = f32[1024,128]{1,0:T(8,128)S(1)} custom-call(f32[1024,128]{1,0:T(8,128)S(1)} %bitcast.27, f32[1024,128]{1,0:T(8,128)S(1)} %bitcast.29, f32[2,3]{1,0:T(2,128)S(1)} %copy-done.6, f32[2,4,4]{2,1,0:T(4,128)S(1)} %copy-done.7, f32[256,256]{1,0:T(8,128)S(1)} %copy-done.2, f32[128,128]{1,0:T(8,128)S(1)} %copy-done.5), custom_call_target="tpu_custom_call" | custom-call | flops 500000000 | bytes 4194304 | tf_op jit(solution)/shard_map/local_rate/pallas_call | solution.py:451
  24.1 5.7 %collective-permute-done.4 = f32[4,32,128]{2,1,0:T(8,128)S(1)} collective-permute-done((f32[4,32,128]{2,1,0:T(8,128)S(1)}, f32[4,32,128]{2,1,0:T(8,128)S(1)}, u32[]{:S(2)}, u32[]{:S(2)}) %collective-permute-start.4) | collective-permute-done | bytes 65568 | tf_op jit(solution)/shard_map/ppermute | solution.py:407
  29.8 0.0 collective-permute-done.refs_0_
  29.8 0.0 collective-permute-done.1.refs_1_
  29.8 0.0 collective-permute-done.2.refs_2_
  29.8 0.0 collective-permute-done.3.refs_3_
  29.8 0.0 copy-start.15
  29.8 0.7 %copy-done.15 = f32[2,4]{1,0:T(2,128)S(1)} copy-done((f32[2,4]{1,0:T(2,128)S(1)}, f32[2,4]{1,0:T(2,128)}, u32[]{:S(2)}) %copy-start.15) | copy-done | bytes 56
  30.5 3.5 %couple_and_finish.1 = (f32[1024,128]{1,0:T(8,128)}, f32[1024,128]{1,0:T(8,128)}) custom-call(f32[104,256]{1,0:T(8,128)S(1)} %collective-permute-done.refs_0_, f32[104,256]{1,0:T(8,128)S(1)} %collective-permute-done.1.refs_1_, f32[104,256]{1,0:T(8,128)S(1)} %collective-permute-done.2.refs_2_, f32[104,256]{1,0:T(8,128)S(1)} %collective-permute-done.3.refs_3_, ...), custom_call_target="tpu_custom_call" | custom-call | flops 100000000 | bytes 4194304 | tf_op jit(solution)/shard_map/couple_and_finish/pallas_call | solution.py:464
Async XLA Ops:
  0.6 10.9 %copy-start.3 = (bf16[128,1024]{1,0:T(8,128)(2,1)S(1)}, bf16[128,1024]{1,0:T(8,128)(2,1)}, u32[]{:S(2)}) copy-start(bf16[128,1024]{1,0:T(8,128)(2,1)} %constant.9.clone.low) | copy-start | bytes 786436
  1.6 17.5 %collective-permute-start.5 = (f32[4,32,128]{2,1,0:T(8,128)S(1)}, f32[4,32,128]{2,1,0:T(8,128)S(1)}, u32[]{:S(2)}, u32[]{:S(2)}) collective-permute-start(f32[4,32,128]{2,1,0:T(8,128)S(1)} %get-tuple-element.18), channel_id=1, source_target_pairs={{4,0},{8,4},{12,8},{5,1},{9,5},{13,9},{6,2},{10,6},{14,10},{7,3},{... | collective-permute-start | bytes 196616 | tf_op jit(solution)/shard_map/ppermute | solution.py:407
  4.9 12.9 %collective-permute-start.6 = (f32[4,8,128]{2,1,0:T(8,128)S(1)}, f32[4,8,128]{2,1,0:T(8,128)S(1)}, u32[]{:S(2)}, u32[]{:S(2)}) collective-permute-start(f32[4,8,128]{2,1,0:T(8,128)S(1)} %bitcast.42), channel_id=1, source_target_pairs={{0,1},{2,3},{4,5},{6,7},{8,9},{10,11},{12,13},{14,15},{16,17},{18,... | collective-permute-start | bytes 49160 | tf_op jit(solution)/shard_map/ppermute | solution.py:407
  6.2 11.6 %collective-permute-start.7 = (f32[4,8,128]{2,1,0:T(8,128)S(1)}, f32[4,8,128]{2,1,0:T(8,128)S(1)}, u32[]{:S(2)}, u32[]{:S(2)}) collective-permute-start(f32[4,8,128]{2,1,0:T(8,128)S(1)} %bitcast.41), channel_id=1, source_target_pairs={{1,0},{3,2},{5,4},{7,6},{9,8},{11,10},{13,12},{15,14},{17,16},{19,... | collective-permute-start | bytes 49160 | tf_op jit(solution)/shard_map/ppermute | solution.py:407
  11.4 0.7 %copy-start.13 = (s32[1,1,1,192]{3,2,1,0:T(1,128)S(1)}, s32[1,1,1,192]{3,2,1,0:T(1,128)}, u32[]{:S(2)}) copy-start(s32[1,1,1,192]{3,2,1,0:T(1,128)} %param.27) | copy-start | bytes 2308
  11.4 0.7 %copy-start.14 = (s32[1,1,1,192]{3,2,1,0:T(1,128)S(1)}, s32[1,1,1,192]{3,2,1,0:T(1,128)}, u32[]{:S(2)}) copy-start(s32[1,1,1,192]{3,2,1,0:T(1,128)} %param.28) | copy-start | bytes 2308
  11.5 0.7 %copy-start.9 = (s32[1,1,1,192]{3,2,1,0:T(1,128)S(1)}, s32[1,1,1,192]{3,2,1,0:T(1,128)}, u32[]{:S(2)}) copy-start(s32[1,1,1,192]{3,2,1,0:T(1,128)} %param.23) | copy-start | bytes 2308
  11.5 0.7 %copy-start.10 = (s32[1,1,1,192]{3,2,1,0:T(1,128)S(1)}, s32[1,1,1,192]{3,2,1,0:T(1,128)}, u32[]{:S(2)}) copy-start(s32[1,1,1,192]{3,2,1,0:T(1,128)} %param.24) | copy-start | bytes 2308
  11.5 0.7 %copy-start.11 = (s32[1,1,1,192,1]{3,4,2,1,0:T(1,128)S(1)}, s32[1,1,1,192,1]{3,4,2,1,0:T(1,128)}, u32[]{:S(2)}) copy-start(s32[1,1,1,192,1]{3,4,2,1,0:T(1,128)} %param.25) | copy-start | bytes 2308
  11.5 0.7 %copy-start.12 = (s32[1,1,1,192]{3,2,1,0:T(1,128)S(1)}, s32[1,1,1,192]{3,2,1,0:T(1,128)}, u32[]{:S(2)}) copy-start(s32[1,1,1,192]{3,2,1,0:T(1,128)} %param.26) | copy-start | bytes 2308
  11.5 0.7 %copy-start.8 = (s32[1,1,1,192]{3,2,1,0:T(1,128)S(1)}, s32[1,1,1,192]{3,2,1,0:T(1,128)}, u32[]{:S(2)}) copy-start(s32[1,1,1,192]{3,2,1,0:T(1,128)} %param.22) | copy-start | bytes 2308
  12.2 1.0 %copy-start = (f32[1,4,8,32,128]{4,3,2,1,0:T(8,128)S(1)}, f32[1,4,8,32,128]{4,3,2,1,0:T(8,128)}, u32[]{:S(2)}) copy-start(f32[1,4,8,32,128]{4,3,2,1,0:T(8,128)} %param.17) | copy-start | bytes 1572868
  13.3 0.9 %copy-start.4 = (bf16[128,1024]{1,0:T(8,128)(2,1)S(1)}, bf16[128,1024]{1,0:T(8,128)(2,1)}, u32[]{:S(2)}) copy-start(bf16[128,1024]{1,0:T(8,128)(2,1)} %constant.8.clone.high) | copy-start | bytes 786436
  14.2 7.8 %copy-start.1 = (f32[1,4,8,32,128]{4,3,2,1,0:T(8,128)S(1)}, f32[1,4,8,32,128]{4,3,2,1,0:T(8,128)}, u32[]{:S(2)}) copy-start(f32[1,4,8,32,128]{4,3,2,1,0:T(8,128)} %param.18) | copy-start | bytes 1572868
  14.2 7.8 %copy-start.2 = (f32[256,256]{1,0:T(8,128)S(1)}, f32[256,256]{1,0:T(8,128)}, u32[]{:S(2)}) copy-start(f32[256,256]{1,0:T(8,128)} %constant.10.clone.derivative_y) | copy-start | bytes 786436
  14.2 7.8 %copy-start.5 = (f32[128,128]{1,0:T(8,128)S(1)}, f32[128,128]{1,0:T(8,128)}, u32[]{:S(2)}) copy-start(f32[128,128]{1,0:T(8,128)} %constant.11.clone.derivative_z) | copy-start | bytes 196612
  16.1 13.7 %collective-permute-start = (f32[104,256]{1,0:T(8,128)S(1)}, f32[104,256]{1,0:T(8,128)S(1)}, u32[]{:S(2)}, u32[]{:S(2)}) collective-permute-start(f32[104,256]{1,0:T(8,128)S(1)} %get-tuple-element.9), channel_id=1, source_target_pairs={{0,2},{2,0},{4,6},{6,4},{8,10},{10,8},{12,14},{14,12},{1,3},{3,1},... | collective-permute-start | bytes 319496 | tf_op jit(solution)/shard_map/ppermute | solution.py:448
  16.1 5.9 %copy-start.7 = (f32[2,4,4]{2,1,0:T(4,128)S(1)}, f32[2,4,4]{2,1,0:T(4,128)}, u32[]{:S(2)}) copy-start(f32[2,4,4]{2,1,0:T(4,128)} %mixing.1) | copy-start | bytes 388
  16.2 13.6 %collective-permute-start.1 = (f32[104,256]{1,0:T(8,128)S(1)}, f32[104,256]{1,0:T(8,128)S(1)}, u32[]{:S(2)}, u32[]{:S(2)}) collective-permute-start(f32[104,256]{1,0:T(8,128)S(1)} %get-tuple-element.10), channel_id=1, source_target_pairs={{0,6},{2,4},{4,10},{6,8},{8,14},{10,12},{12,2},{14,0},{1,7},{3,5},... | collective-permute-start | bytes 319496 | tf_op jit(solution)/shard_map/ppermute | solution.py:448
  17.8 11.9 %collective-permute-start.2 = (f32[104,256]{1,0:T(8,128)S(1)}, f32[104,256]{1,0:T(8,128)S(1)}, u32[]{:S(2)}, u32[]{:S(2)}) collective-permute-start(f32[104,256]{1,0:T(8,128)S(1)} %get-tuple-element.11), channel_id=1, source_target_pairs={{0,10},{2,8},{4,14},{6,12},{8,2},{10,0},{12,6},{14,4},{1,11},{3,9}... | collective-permute-start | bytes 319496 | tf_op jit(solution)/shard_map/ppermute | solution.py:448
  17.9 11.9 %collective-permute-start.3 = (f32[104,256]{1,0:T(8,128)S(1)}, f32[104,256]{1,0:T(8,128)S(1)}, u32[]{:S(2)}, u32[]{:S(2)}) collective-permute-start(f32[104,256]{1,0:T(8,128)S(1)} %get-tuple-element.12), channel_id=1, source_target_pairs={{0,14},{2,12},{4,2},{6,0},{8,6},{10,4},{12,10},{14,8},{1,15},{3,13... | collective-permute-start | bytes 319496 | tf_op jit(solution)/shard_map/ppermute | solution.py:448
  19.1 2.9 %copy-start.6 = (f32[2,3]{1,0:T(2,128)S(1)}, f32[2,3]{1,0:T(2,128)}, u32[]{:S(2)}) copy-start(f32[2,3]{1,0:T(2,128)} %refs_11_.1) | copy-start | bytes 76
  19.1 10.7 %collective-permute-start.4 = (f32[4,32,128]{2,1,0:T(8,128)S(1)}, f32[4,32,128]{2,1,0:T(8,128)S(1)}, u32[]{:S(2)}, u32[]{:S(2)}) collective-permute-start(f32[4,32,128]{2,1,0:T(8,128)S(1)} %get-tuple-element.19), channel_id=1, source_target_pairs={{0,4},{4,8},{8,12},{1,5},{5,9},{9,13},{2,6},{6,10},{10,14},{3,7},{... | collective-permute-start | bytes 196616 | tf_op jit(solution)/shard_map/ppermute | solution.py:407
  29.8 0.7 %copy-start.15 = (f32[2,4]{1,0:T(2,128)S(1)}, f32[2,4]{1,0:T(2,128)}, u32[]{:S(2)}) copy-start(f32[2,4]{1,0:T(2,128)} %refs_12_.1) | copy-start | bytes 100

commit v2 on v1

--- a/solution.py
+++ b/solution.py
@@ -3,7 +3,6 @@
 
 import jax
 import jax.numpy as jnp
-import ml_dtypes
 import numpy as np
 from jax import lax
 from jax.experimental import pallas as pl
@@ -88,24 +87,6 @@
     return derivative, degree * nodes / 2.0, fine, coarse
 
 
-def two_parts(matrix):
-    high = matrix.astype(np.float32).astype(ml_dtypes.bfloat16)
-    low = (matrix - high.astype(np.float64)).astype(ml_dtypes.bfloat16)
-    return high, low
-
-
-@functools.lru_cache
-def face_maps():
-    _, _, fine, coarse = node_tables(NODES)
-    maps = []
-    for tables in (fine, coarse):
-        for quadrant in range(4):
-            first, second = tables[quadrant // 2], tables[quadrant % 2]
-            one = np.kron(second.T, first.T)
-            maps.append(np.kron(np.eye(2), one))
-    return two_parts(np.concatenate(maps, axis=1))
-
-
 def split(values):
     high = values.astype(bf16)
     return high, (values - high.astype(f32)).astype(bf16)
@@ -157,6 +138,18 @@
     )
 
 
+def table_tiles(tables, node):
+    place = iota((8, 128), 0) * 8 + node
+    tiles = [jnp.zeros((8, 128), f32) for _ in tables]
+    for i in range(8):
+        for j in range(8):
+            here = place == i * 8 + j
+            tiles = [
+                jnp.where(here, float(table[j, i]), tile) for table, tile in zip(tables, tiles)
+            ]
+    return tiles
+
+
 def y_row(ref, y):
     return ref[pl.ds(y, 32, stride=32), :]
 
@@ -168,31 +161,68 @@
     return group, ez
 
 
-def send_kernel(
-    ranks, slots, field, elem, side, code, rank, p_elem, p_side, p_quadrant, count, high, low,
-    *outs,
+def send_order(ranks):
+    return sorted(range(ranks), key=lambda k: -min(k, ranks - k))
+
+
+def plan_kernel(
+    ranks, slots, elem, side, code, rank, p_elem, p_side, p_quadrant,
+    head_out, columns_out, slot_out, maps_high, maps_low,
 ):
-    messages, faces_out = outs[:ranks], outs[ranks]
     capacity = elem.shape[1]
     me = lax.axis_index("elem")
-    used = iota((1, capacity), 1) < count[0, 0]
     group, ez = face_number(elem[...], side[...])
     codes = code[...]
     map_index = jnp.where(codes == 5, 5 + p_quadrant[...], codes)
     apart = rank[...] - me
     apart = jnp.where(apart < 0, apart + ranks, apart)
-    apart = jnp.where(used, apart, 200)
     to_group, to_ez = face_number(p_elem[...], p_side[...])
-    kind = jnp.where(used, jnp.where(codes == 5, 2 + p_quadrant[...], 1), 0)
+    kind = jnp.where(codes == 5, 2 + p_quadrant[...], 1)
     rows = [group, ez, map_index, apart, to_group, to_ez, kind]
     head = jnp.concatenate(
         [row.astype(f32) for row in rows] + [jnp.zeros((1, capacity), f32)], axis=0
-    ).astype(bf16)
+    )
+    head_out[...] = head
     here, there = iota((capacity, capacity), 0), iota((capacity, capacity), 1)
-    columns = dot_t(one(here == there), head)
+    columns = dot_t(one(here == there), head.astype(bf16))
+    columns_out[...] = columns
     earlier = (columns[:, 3:4] == apart.astype(f32)) & (here < there)
-    position = jnp.sum(jnp.where(earlier, 1.0, 0.0), axis=0, keepdims=True)
-    slot = apart * slots + position.astype(jnp.int32)
+    position = jnp.sum(jnp.where(earlier, 1.0, 0.0), axis=0, keepdims=True).astype(jnp.int32)
+    slot_out[...] = jnp.where(position < slots, apart * slots + position, -1)
+
+    _, _, fine, coarse = node_tables(NODES)
+    lane = iota((8, 128), 1)
+    along_a = table_tiles(fine + coarse, lane % 8)
+    along_b = table_tiles(fine + coarse, lane // 8 % 8)
+    for index in range(CODES):
+        first = along_a[index // 4 * 2 + index % 4 // 2]
+        second = along_b[index // 4 * 2 + index % 2]
+        blocks = []
+        for v in range(2):
+            kept = jnp.where(lane // 64 == v, first, 0.0)
+            blocks += [kept * second[b : b + 1, :] for b in range(8)]
+        high, low = split(jnp.concatenate(blocks, axis=0))
+        lanes = slice(index * 128, index * 128 + 128)
+        maps_high[0:128, lanes] = high
+        maps_high[128:256, lanes] = high
+        maps_low[:, lanes] = low
+
+
+def send_kernel(ranks, slots, field, count, planned, columns_in, slot_in, maps_high, maps_low, *outs):
+    messages, faces_out, layers = outs[:ranks], outs[ranks], outs[ranks + 1 :]
+    capacity = planned.shape[1]
+    lines = iota((8, capacity), 0)
+    unused = (lines == 6) & (iota((8, capacity), 1) >= count[...])
+    head = jnp.where(unused, 0.0, planned[...]).astype(bf16)
+    columns, slot = columns_in[...], slot_in[...]
+    for v in range(4):
+        layers[0][v * 32 : v * 32 + 32, :] = field[v * 256 : v * 256 + 32, :]
+        layers[1][v * 32 : v * 32 + 32, :] = field[v * 256 + 224 : v * 256 + 256, :]
+    if len(layers) == 3:
+        layers[2][...] = jnp.where(lax.axis_index("sub") == 0, y_row(field, 31), y_row(field, 0))
+    else:
+        layers[2][...] = y_row(field, 0)
+        layers[3][...] = y_row(field, 31)
 
     order = lane_order(False)
     parts = []
@@ -234,28 +264,27 @@
     picked = one(source == iota((capacity, FACES), 1))
     values = dot_t(picked, faces_high) + dot_t(picked, faces_low)
     which = columns[:, 2:3]
-    mapped = []
-    for half in range(2):
-        part = values[:, half * 128 : (half + 1) * 128]
-        part_high, part_low = split(part)
-        out = dot(jnp.concatenate([part_high, part_low], axis=1), twice(high[...])) + dot(
-            part_high, low[...]
-        )
-        result = part
-        for index in range(CODES):
-            result = jnp.where(
-                which == float(index + 1), out[:, index * 128 : (index + 1) * 128], result
-            )
-        mapped.append(result)
+    pair = jnp.concatenate([values[:, :128], values[:, 128:]], axis=0)
+    pair_high, pair_low = split(pair)
+    out = dot(jnp.concatenate([pair_high, pair_low], axis=1), maps_high[...])
+    out += dot(pair_high, maps_low[...])
+    which = jnp.concatenate([which, which], axis=0)
+    for index in range(CODES):
+        pair = jnp.where(which == float(index + 1), out[:, index * 128 : (index + 1) * 128], pair)
+    mapped = [pair[:capacity], pair[capacity:]]
     mapped_high, mapped_low = split(jnp.concatenate(mapped, axis=1))
-    for k in range(ranks):
+    for message, k in zip(messages, send_order(ranks)):
         placed = one(iota((slots, capacity), 0) + k * slots == slot)
-        messages[k][0:slots, :] = dot(placed, mapped_high) + dot(placed, mapped_low)
-        messages[k][slots : slots + 8, :] = jnp.zeros((8, 256), f32)
-        messages[k][slots : slots + 8, 0:slots] = dot_t(head, placed)
-
-
-def local_kernel(field, register, advect, mixing, derivative_y, derivative_z, base):
+        rows = dot(placed, mapped_high) + dot(placed, mapped_low)
+        message[0:slots, :] = rows[:, :128]
+        message[slots : 2 * slots, :] = rows[:, 128:]
+        message[2 * slots : 2 * slots + 8, :] = jnp.zeros((8, 128), f32)
+        message[2 * slots : 2 * slots + 8, 0:slots] = dot_t(head, placed)
+
+
+def local_kernel(
+    ranks, field, register, advect, mixing, drag, after, base, gains
+):
     comp = lax.axis_index("comp")
     derivative, scale, _, _ = node_tables(NODES)
     left, right, speed = [], [], []
@@ -265,6 +294,19 @@
         left.append(scale * (0.5 * a + 0.5 * upwind_share * jnp.abs(a)))
         right.append(scale * (0.5 * upwind_share * jnp.abs(a) - 0.5 * a))
 
+    me, sub, subs = lax.axis_index("elem"), lax.axis_index("sub"), lax.axis_size("sub")
+    values = [drag[comp, v] * scale for v in range(4)]
+    values.append(jnp.where(me > 0, left[0], 0.0))
+    values.append(jnp.where(me < ranks - 1, right[0], 0.0))
+    values.append(jnp.where(sub > 0, left[1], 0.0))
+    values.append(jnp.where(sub < subs - 1, right[1], 0.0))
+    line = iota((8, 128), 0)
+    lines = jnp.zeros((8, 128), f32)
+    for i, value in enumerate(values):
+        lines = jnp.where(line == i, time_step * value, lines)
+    gains[...] = lines
+    tile_z, tile_y = table_tiles([derivative, derivative.T], iota((8, 128), 1) % 8)
+
     def both_ways(row, column, node, gain_left, gain_right):
         first, last = node == 0, node == NODES - 1
         out = jnp.where((row == column) & first, -gain_left, 0.0)
@@ -273,12 +315,17 @@
         return jnp.where((row == column + 1) & last, gain_right, out)
 
     row, column = iota((128, 128), 0), iota((128, 128), 1)
-    along_z = both_ways(row, column, column % 8, left[2], right[2]) - speed[2] * derivative_z[...]
+    along_z = both_ways(row, column, column % 8, left[2], right[2]) - speed[2] * jnp.where(
+        row // 8 == column // 8, jnp.concatenate([tile_z] * 16, axis=0), 0.0
+    )
     z_high, z_low = split(along_z)
     z_high = twice(z_high)
     row, column = iota((256, 256), 0), iota((256, 256), 1)
     node = row % 8
-    across = -speed[0] * derivative_y[...]
+    tile = jnp.concatenate([tile_y] * 2, axis=1)
+    across = jnp.where(
+        row // 8 == column // 8, -speed[0] * jnp.concatenate([tile] * 32, axis=0), 0.0
+    )
     across += jnp.where((row == column) & (node == 0), -left[0], 0.0)
     across += jnp.where((row == column) & (node == NODES - 1), -right[0], 0.0)
     same = (row // 32 == column // 32) & (node == column % 8)
@@ -321,84 +368,82 @@
 
 def finish_kernel(ranks, slots, *refs):
     messages = refs[:ranks]
-    (base, field, faces, x_before, x_after, y_before, y_after, advect, drag, new, advanced) = refs[
-        ranks:
-    ]
-    comp = lax.axis_index("comp")
-    scale = node_tables(NODES)[1]
+    base, field, faces, x_before, x_after, y_before, y_after, gains = refs[ranks : ranks + 8]
+    new_out, advanced_out, new, advanced, left = refs[ranks + 8 :]
     total = jnp.zeros((FACES, 256), f32)
     masks = jnp.zeros((16, FACES), f32)
-    for k in range(ranks):
-        head = messages[k][slots : slots + 8, 0:slots]
+    for message in messages:
+        head = message[2 * slots : 2 * slots + 8, 0:slots]
         kind = head[6:7]
         target = jnp.where(kind > 0.0, head[4:5] * 16.0 + head[5:6], -1.0).astype(jnp.int32)
-        placed = one(iota((FACES, slots), 0) == target)
-        values_high, values_low = split(messages[k][0:slots, :])
-        total += dot(placed, values_high) + dot(placed, values_low)
-        row = iota((16, slots), 0)
+        both = jnp.concatenate([target, target], axis=1)
+        placed = one(iota((FACES, 2 * slots), 0) == both)
+        values = jnp.concatenate([message[0:slots, :], message[slots : 2 * slots, :]], axis=1)
+        high = values.astype(bf16).astype(f32)
+        total += dot(placed, jnp.concatenate([high, values - high], axis=0).astype(bf16))
+        row = iota((16, 2 * slots), 0)
         quadrant = ((row % 8) // 4) * 2 + row // 8
+        kind = jnp.where(iota((1, 2 * slots), 1) < slots, jnp.concatenate([kind, kind], axis=1), 0.0)
         live = (kind == 1.0) | (kind == 2.0 + quadrant.astype(f32))
         masks += dot_t(one(live & (kind > 0.0)), placed)
     total = total.T
     terms = []
     for v in range(4):
-        gain = drag[comp, v] * (scale * time_step)
+        gain = gains[v : v + 1, 0:1]
         for b in range(8):
-            rows = pl.ds((v * 8 + b) * 8, 8)
+            at = (v * 8 + b) * 8
             count = masks[0:8] if b < 4 else masks[8:16]
-            at = (v * 8 + b) * 8
-            terms.append(gain * (total[at : at + 8] - count * faces[rows, :]))
-    order = twice(lane_order(True))
-    on_x = on_y = None
-    for kind_of in (0, 1):
-        lanes = slice(kind_of * 128, kind_of * 128 + 128)
-        turned = block_transpose(
-            [jnp.concatenate([terms[v * 8 + b][:, lanes] for v in range(4)], axis=0) for b in range(8)]
+            terms.append(gain * (total[at : at + 8] - count * faces[at : at + 8, :]))
+    turned = []
+    for lanes in (slice(0, 128), slice(128, 256)):
+        turned += block_transpose(
+            [
+                jnp.concatenate([terms[v * 8 + b][:, lanes] for v in range(4)], axis=0)
+                for b in range(8)
+            ]
         )
-        high, low = split(jnp.concatenate(turned, axis=0))
-        moved = dot(jnp.concatenate([high, low], axis=1), order)
-        if kind_of == 0:
-            on_x = moved
-        else:
-            on_y = moved
+    high, low = split(jnp.concatenate(turned, axis=0))
+    moved = dot(jnp.concatenate([high, low], axis=1), twice(lane_order(True)))
     high, low = split(jnp.concatenate([term[:, 256:384] for term in terms], axis=0))
-    ends = jnp.concatenate([high, low], axis=1)
-    flux = [jnp.abs(advect[comp, d]) for d in range(2)]
-    left = [
-        time_step * scale * (0.5 * advect[comp, d] + 0.5 * upwind_share * flux[d]) for d in range(2)
-    ]
-    right = [
-        time_step * scale * (0.5 * upwind_share * flux[d] - 0.5 * advect[comp, d]) for d in range(2)
-    ]
-    for ey in range(EY):
-        on_z = dot(ends, twice(end_lanes(ey, True)))
-        for j in range(8):
-            y = ey * 8 + j
-            rate = base[y * 32 : (y + 1) * 32, :]
-            rate += jnp.concatenate(
-                [on_z[(v * 8 + j) * 8 : (v * 8 + j) * 8 + 8] for v in range(4)], axis=0
-            )
-            if j in (0, NODES - 1):
-                g = (4 if j else 0) + ey
-                rate += on_y[g * 32 : (g + 1) * 32]
-            if y == 0:
-                rate += left[1] * y_before[...]
-            if y == 31:
-                rate += right[1] * y_after[...]
-            new[pl.ds(y, 32, stride=32), :] = rate
-    for end in (0, 1):
-        for v in range(4):
+    ends = jnp.concatenate([end_lanes(ey, True) for ey in range(EY)], axis=1)
+    on_z = dot(jnp.concatenate([high, low], axis=1), twice(ends))
+
+    copies = []
+    for v in range(4):
+        for ey in range(EY):
+            for j in range(8):
+                y = ey * 8 + j
+                at = (v * 8 + j) * 8
+                rate = base[y * 32 + v * 8 : y * 32 + v * 8 + 8, :]
+                rate += on_z[at : at + 8, ey * 128 : ey * 128 + 128]
+                if j in (0, NODES - 1):
+                    at = ((8 + (4 if j else 0) + ey) * 4 + v) * 8
+                    rate += moved[at : at + 8]
+                if y == 0:
+                    rate += gains[6:7, :] * y_before[v * 8 : v * 8 + 8, :]
+                if y == 31:
+                    rate += gains[7:8, :] * y_after[v * 8 : v * 8 + 8, :]
+                new[pl.ds(v * 256 + y, 8, stride=32), :] = rate
+        for end, beside in ((0, x_before), (1, x_after)):
             at = v * 256 + (NODES - 1) * end * 32
-            rows = pl.ds(at, 32)
             coupled = jnp.concatenate(
-                [on_x[((end * 4 + ey) * 4 + v) * 8 : ((end * 4 + ey) * 4 + v) * 8 + 8] for ey in range(EY)],
+                [
+                    moved[((end * 4 + ey) * 4 + v) * 8 : ((end * 4 + ey) * 4 + v) * 8 + 8]
+                    for ey in range(EY)
+                ],
                 axis=0,
             )
-            beside = left[0] * x_before[v * 32 : v * 32 + 32, :] if end == 0 else right[0] * x_after[v * 32 : v * 32 + 32, :]
-            new[rows, :] = new[rows, :] + coupled + beside
-    for at in range(0, 1024, 128):
-        rows = pl.ds(at, 128)
+            coupled += gains[4 + end : 5 + end, :] * beside[v * 32 : v * 32 + 32, :]
+            new[pl.ds(at, 32), :] = new[pl.ds(at, 32), :] + coupled
+        rows = pl.ds(v * 256, 256)
         advanced[rows, :] = field[rows, :] + section_weight * new[rows, :]
+        for i, (source, place) in enumerate(((new, new_out), (advanced, advanced_out))):
+            copies.append(
+                pltpu.make_async_copy(source.at[rows], place.at[rows], left.at[v * 2 + i])
+            )
+            copies[-1].start()
+    for copy in copies:
+        copy.wait()
 
 
 def along(layer, axis, step):
@@ -414,62 +459,85 @@
     ranks = lax.axis_size("elem")
     capacity = face_elem.shape[-1]
     slots = max(2, 2 * capacity // ranks)
-    block = field[0]
+    subs = lax.axis_size("sub")
+    layers = 1 if subs == 2 else 2
     flat = field.reshape(1024, 128)
-    x_before = along(block[:, -1], "elem", 1).reshape(128, 128)
-    x_after = along(block[:, 0], "elem", -1).reshape(128, 128)
-    y_before = along(block[:, :, -1], "sub", 1).reshape(32, 128)
-    y_after = along(block[:, :, 0], "sub", -1).reshape(32, 128)
-
     vmem = pl.BlockSpec(memory_space=pltpu.VMEM)
     smem = pl.BlockSpec(memory_space=pltpu.SMEM)
     row = (1, capacity)
-    map_high, map_low = face_maps()
+    plan = pl.pallas_call(
+        functools.partial(plan_kernel, ranks, slots),
+        out_shape=[
+            jax.ShapeDtypeStruct((8, capacity), f32),
+            jax.ShapeDtypeStruct((capacity, 8), f32),
+            jax.ShapeDtypeStruct(row, jnp.int32),
+            jax.ShapeDtypeStruct((256, CODES * 128), bf16),
+            jax.ShapeDtypeStruct((128, CODES * 128), bf16),
+        ],
+        in_specs=[vmem] * 7,
+        out_specs=[vmem] * 5,
+        compiler_params=pltpu.CompilerParams(vmem_limit_bytes=32 << 20),
+        cost_estimate=pl.CostEstimate(flops=10**7, bytes_accessed=1 << 20, transcendentals=0),
+        name="plan_records",
+    )(
+        face_elem.reshape(row), face_side.reshape(row), mortar_code.reshape(row),
+        partner_rank.reshape(row), partner_elem.reshape(row), partner_side.reshape(row),
+        partner_quadrant.reshape(row),
+    )
     outs = pl.pallas_call(
         functools.partial(send_kernel, ranks, slots),
-        out_shape=[jax.ShapeDtypeStruct((slots + 8, 256), f32)] * ranks
-        + [jax.ShapeDtypeStruct((256, FACES), f32)],
-        in_specs=[vmem] * 8 + [smem] + [vmem] * 2,
-        out_specs=[vmem] * (ranks + 1),
+        out_shape=[jax.ShapeDtypeStruct((2 * slots + 8, 128), f32)] * ranks
+        + [jax.ShapeDtypeStruct((256, FACES), f32)]
+        + [jax.ShapeDtypeStruct((128, 128), f32)] * 2
+        + [jax.ShapeDtypeStruct((32, 128), f32)] * layers,
+        in_specs=[vmem] * 7,
+        out_specs=[vmem] * (ranks + 3 + layers),
         compiler_params=pltpu.CompilerParams(vmem_limit_bytes=32 << 20),
         cost_estimate=pl.CostEstimate(flops=10**8, bytes_accessed=2 << 20, transcendentals=0),
         name="send_faces",
-    )(
-        flat, face_elem.reshape(row), face_side.reshape(row), mortar_code.reshape(row),
-        partner_rank.reshape(row), partner_elem.reshape(row), partner_side.reshape(row),
-        partner_quadrant.reshape(row), face_count.reshape(1, 1), map_high, map_low,
-    )
+    )(flat, face_count.reshape(1, 1), *plan)
     faces = outs[ranks]
-    received = []
-    for k in range(ranks):
+    received = [None] * ranks
+    for out, k in zip(outs, send_order(ranks)):
         pairs = [
             (2 * e + c, 2 * ((e + k) % ranks) + 1 - c) for e in range(ranks) for c in range(2)
         ]
-        received.append(lax.ppermute(outs[k], ("elem", "comp"), pairs))
-
-    derivative = node_tables(NODES)[0]
-    base = pl.pallas_call(
-        local_kernel,
-        out_shape=jax.ShapeDtypeStruct((1024, 128), f32),
-        in_specs=[vmem, vmem, smem, smem, vmem, vmem],
-        out_specs=vmem,
+        received[k] = lax.ppermute(out, ("elem", "comp"), pairs)
+
+    (x_first, x_last, *y_layers), received[0] = lax.optimization_barrier(
+        (outs[ranks + 1 :], received[0])
+    )
+    x_before = along(x_last, "elem", 1)
+    x_after = along(x_first, "elem", -1)
+    if layers == 1:
+        y_before = y_after = lax.ppermute(y_layers[0], "sub", [(0, 1), (1, 0)])
+    else:
+        y_before = along(y_layers[1], "sub", 1)
+        y_after = along(y_layers[0], "sub", -1)
+    base, gains = pl.pallas_call(
+        functools.partial(local_kernel, ranks),
+        out_shape=[
+            jax.ShapeDtypeStruct((1024, 128), f32),
+            jax.ShapeDtypeStruct((8, 128), f32),
+        ],
+        in_specs=[vmem, vmem, smem, smem, smem, pl.BlockSpec(memory_space=pl.ANY)],
+        out_specs=[vmem] * 2,
         compiler_params=pltpu.CompilerParams(vmem_limit_bytes=32 << 20),
         cost_estimate=pl.CostEstimate(flops=5 * 10**8, bytes_accessed=4 << 20, transcendentals=0),
         name="local_rate",
     )(
-        flat, register.reshape(1024, 128), advect, mixing,
-        np.kron(np.eye(32), derivative).astype(np.float32),
-        np.kron(np.eye(16), derivative.T).astype(np.float32),
+        flat, register.reshape(1024, 128), advect, mixing, drag, received[0],
     )
     new, advanced = pl.pallas_call(
         functools.partial(finish_kernel, ranks, slots),
         out_shape=[jax.ShapeDtypeStruct((1024, 128), f32)] * 2,
-        in_specs=[vmem] * (ranks + 7) + [smem] * 2,
-        out_specs=[vmem] * 2,
+        in_specs=[vmem] * (ranks + 8),
+        out_specs=[pl.BlockSpec(memory_space=pl.ANY)] * 2,
+        scratch_shapes=[pltpu.VMEM((1024, 128), f32)] * 2 + [pltpu.SemaphoreType.DMA((8,))],
         compiler_params=pltpu.CompilerParams(vmem_limit_bytes=32 << 20),
         cost_estimate=pl.CostEstimate(flops=10**8, bytes_accessed=4 << 20, transcendentals=0),
         name="couple_and_finish",
-    )(*received, base, flat, faces, x_before, x_after, y_before, y_after, advect, drag)
+    )(*received, base, flat, faces, x_before, x_after, y_before, y_after, gains)
     return new.reshape(field.shape), advanced.reshape(field.shape)
 
 

time: 34.3 us -> 24 us (0.70)
  the two profiles are of different devices: /device:TPU:18 before, /device:TPU:0 now
where the time goes in v2:
time: 24 us; the launch traced here: 23.7 us
  starting transfers between devices  12.4 us (52%)
  Pallas kernels  7.01 us (29%)
  local copies, waits for them, and re-layouts  1.77 us (7%)
  between operations  1.42 us (6%)
  waiting for transfers between devices  1.13 us (5%)
    ppermute x4, starting transfers between devices, on_device(): received[k] = lax.ppermute(out, ('elem', 'comp'), pairs)  6.86 us
    ppermute x2, starting transfers between devices, along(): return lax.ppermute(layer, axis, pairs)  4 us
    pallas_call x1, Pallas kernels, on_device(): pl.pallas_call(functools.partial(finish_kernel, ranks, slots), out_shape=...  2.29 us
    pallas_call x1, Pallas kernels, on_device(): pl.pallas_call(functools.partial(local_kernel, ranks), out_shape=[jax.Sha...  2.13 us
    pallas_call x1, Pallas kernels, on_device(): pl.pallas_call(functools.partial(send_kernel, ranks, slots), out_shape=[j...  2.05 us
    unnamed x26, local copies, waits for them, and re-layouts  1.77 us
    ppermute x1, starting transfers between devices, on_device(): y_before = y_after = lax.ppermute(y_layers[0], 'sub', [(0, 1), (1, 0)])  1.55 us
    ppermute x2, waiting for transfers between devices, along(): return lax.ppermute(layer, axis, pairs)  1.04 us
  transfers between devices with their start and end apart: 7, of which 2 were waited for; matrix products, arithmetic and copies ran while one was open for 0% of the time, Pallas kernels for 9%

profile of v2, /device:TPU:0, one launch (start us, length us, event | category | flops | bytes accessed | tf_op | source)
XLA Modules:
  0.0 23.7 jit_solution(16881217352378141091)
XLA Ops:
  1.3 0.0 copy-start.9
  1.3 0.0 copy-start.10
  1.3 0.0 copy-start.7
  1.3 0.0 copy-start.8
  1.3 0.0 copy-start.5
  1.3 0.0 copy-start.6
  1.3 0.0 copy-start.4
  1.3 0.6 %copy-done.9 = s32[1,1,1,192]{3,2,1,0:T(1,128)S(1)} copy-done((s32[1,1,1,192]{3,2,1,0:T(1,128)S(1)}, s32[1,1,1,192]{3,2,1,0:T(1,128)}, u32[]{:S(2)}) %copy-start.9) | copy-done | bytes 792
  2.0 0.0 copy-done.10
  2.0 0.0 copy-done.7
  2.0 0.0 copy-done.8
  2.0 0.0 copy-done.5
  2.0 0.0 copy-done.6
  2.0 0.0 copy-done.4
  2.1 0.5 %plan_records.1 = (f32[8,192]{1,0:T(8,128)S(1)}, f32[192,8]{1,0:T(8,128)S(1)}, s32[1,192]{1,0:T(1,128)S(1)}, bf16[256,1024]{1,0:T(8,128)(2,1)S(1)}, bf16[128,1024]{1,0:T(8,128)(2,1)S(1)}) custom-call(s32[1,192]{1,0:T(1,128)S(1)} %bitcast.17, s32[1,192]{1,0:T(1,128)S(1)} %bitcast.18, s32[1,192]{1,0:T(1,128)S(1)} %bitcast.19, s32[1,192]{1,0:T(1,128)S(1)} %bitcast.20, ...), custom_call_target="tpu_custom_call" | custom-call | flops 10000000 | bytes 1048576 | tf_op jit(solution)/shard_map/plan_records/pallas_call | solution.py:468
  2.6 0.0 copy-start
  2.6 1.0 %copy-done = f32[1,4,8,32,128]{4,3,2,1,0:T(8,128)S(1)} copy-done((f32[1,4,8,32,128]{4,3,2,1,0:T(8,128)S(1)}, f32[1,4,8,32,128]{4,3,2,1,0:T(8,128)}, u32[]{:S(2)}) %copy-start) | copy-done | bytes 524312
  3.6 0.0 copy-start.1
  3.6 0.0 copy-start.2
  3.6 2.1 %send_faces.1 = (f32[200,128]{1,0:T(8,128)S(1)}, f32[200,128]{1,0:T(8,128)S(1)}, f32[200,128]{1,0:T(8,128)S(1)}, f32[200,128]{1,0:T(8,128)S(1)}, f32[256,384]{1,...) custom-call(f32[1024,128]{1,0:T(8,128)S(1)} %bitcast.13, ...), custom_call_target="tpu_custom_call" | custom-call | flops 100000000 | bytes 2097152 | tf_op jit(solution)/shard_map/send_faces/pallas_call | solution.py:487
  5.7 0.5 %collective-permute-start = (f32[200,128]{1,0:T(8,128)S(1)}, f32[200,128]{1,0:T(8,128)S(1)}, u32[]{:S(2)}, u32[]{:S(2)}) collective-permute-start(f32[200,128]{1,0:T(8,128)S(1)} %get-tuple-element.31), channel_id=1, source_target_pairs={{0,2},{2,0},{4,6},{6,4},{8,10},{10,8},{12,14},{14,12},{1,3},{3,1},... | collective-permute-start | bytes 307208 | tf_op jit(solution)/shard_map/ppermute | solution.py:505
  6.2 2.7 %collective-permute-start.1 = (f32[200,128]{1,0:T(8,128)S(1)}, f32[200,128]{1,0:T(8,128)S(1)}, u32[]{:S(2)}, u32[]{:S(2)}) collective-permute-start(f32[200,128]{1,0:T(8,128)S(1)} %get-tuple-element.33), channel_id=1, source_target_pairs={{0,6},{2,4},{4,10},{6,8},{8,14},{10,12},{12,2},{14,0},{1,7},{3,5},... | collective-permute-start | bytes 307208 | tf_op jit(solution)/shard_map/ppermute | solution.py:505
  8.9 2.3 %collective-permute-start.2 = (f32[200,128]{1,0:T(8,128)S(1)}, f32[200,128]{1,0:T(8,128)S(1)}, u32[]{:S(2)}, u32[]{:S(2)}) collective-permute-start(f32[200,128]{1,0:T(8,128)S(1)} %get-tuple-element.34), channel_id=1, source_target_pairs={{0,10},{2,8},{4,14},{6,12},{8,2},{10,0},{12,6},{14,4},{1,11},{3,9}... | collective-permute-start | bytes 307208 | tf_op jit(solution)/shard_map/ppermute | solution.py:505
  11.2 0.0 copy-start.3
  11.2 1.4 %collective-permute-start.3 = (f32[200,128]{1,0:T(8,128)S(1)}, f32[200,128]{1,0:T(8,128)S(1)}, u32[]{:S(2)}, u32[]{:S(2)}) collective-permute-start(f32[200,128]{1,0:T(8,128)S(1)} %get-tuple-element.35), channel_id=1, source_target_pairs={{0,14},{2,12},{4,2},{6,0},{8,6},{10,4},{12,10},{14,8},{1,15},{3,13... | collective-permute-start | bytes 307208 | tf_op jit(solution)/shard_map/ppermute | solution.py:505
  12.6 0.0 collective-permute-done.after.refs_0_
  12.6 0.0 copy-start.12
  12.6 0.0 copy-start.11
  12.6 2.7 %collective-permute-start.4 = (f32[128,128]{1,0:T(8,128)S(1)}, f32[128,128]{1,0:T(8,128)S(1)}, u32[]{:S(2)}, u32[]{:S(2)}) collective-permute-start(f32[128,128]{1,0:T(8,128)S(1)} %get-tuple-element.38), channel_id=1, source_target_pairs={{0,4},{4,8},{8,12},{1,5},{5,9},{9,13},{2,6},{6,10},{10,14},{3,7},{... | collective-permute-start | bytes 196616 | tf_op jit(solution)/shard_map/ppermute | solution.py:452
  15.3 1.3 %collective-permute-start.5 = (f32[128,128]{1,0:T(8,128)S(1)}, f32[128,128]{1,0:T(8,128)S(1)}, u32[]{:S(2)}, u32[]{:S(2)}) collective-permute-start(f32[128,128]{1,0:T(8,128)S(1)} %get-tuple-element.39), channel_id=1, source_target_pairs={{4,0},{8,4},{12,8},{5,1},{9,5},{13,9},{6,2},{10,6},{14,10},{7,3},{... | collective-permute-start | bytes 196616 | tf_op jit(solution)/shard_map/ppermute | solution.py:452
  16.6 0.0 collective-permute-done.1.refs_1_
  16.6 1.6 %collective-permute-start.6 = (f32[32,128]{1,0:T(8,128)S(1)}, f32[32,128]{1,0:T(8,128)S(1)}, u32[]{:S(2)}, u32[]{:S(2)}) collective-permute-start(f32[32,128]{1,0:T(8,128)S(1)} %get-tuple-element.40), channel_id=1, source_target_pairs={{0,1},{1,0},{2,3},{3,2},{4,5},{5,4},{6,7},{7,6},{8,9},{9,8},{10,11... | collective-permute-start | bytes 49160 | tf_op jit(solution)/shard_map/ppermute | solution.py:513
  18.2 0.0 copy-done.1
  18.2 0.0 copy-done.2
  18.2 0.0 copy-done.3
  18.2 0.0 copy-done.12
  18.2 0.0 copy-done.11
  18.2 2.1 %local_rate.1 = (f32[1024,128]{1,0:T(8,128)S(1)}, f32[8,128]{1,0:T(8,128)S(1)}) custom-call(f32[1024,128]{1,0:T(8,128)S(1)} %bitcast.14, f32[1024,128]{1,0:T(8,128)S(1)} %bitcast.16, f32[2,3]{1,0:T(2,128)S(1)} %copy-done.11, f32[2,4,4]{2,1,0:T(4,128)S(1)} %copy-done.3, f32[2,4]{1,0:T(2,128)S(1)} %copy-done.12, f32[200,128]{1,0:T(8,128)S(1)} %collective-permute-done.after.refs_0_), custom_call_target="tpu_custom_call" | custom-call | flops 500000000 | bytes 4194304 | tf_op jit(solution)/shard_map/local_rate/pallas_call | solution.py:517
  20.3 0.0 collective-permute-done.2.refs_2_
  20.3 0.0 collective-permute-done.3.refs_3_
  20.3 0.1 collective-permute-done.6.refs_9_.refs_10_
  20.4 0.0 collective-permute-done.4.refs_7_
  20.4 1.0 %collective-permute-done.5.refs_8_ = f32[128,128]{1,0:T(8,128)S(1)} collective-permute-done((f32[128,128]{1,0:T(8,128)S(1)}, f32[128,128]{1,0:T(8,128)S(1)}, u32[]{:S(2)}, u32[]{:S(2)}) %collective-permute-start.5) | collective-permute-done | bytes 65568 | tf_op jit(solution)/shard_map/ppermute | solution.py:452
  21.4 2.3 %couple_and_finish.1 = (f32[1024,128]{1,0:T(8,128)}, f32[1024,128]{1,0:T(8,128)}) custom-call(f32[200,128]{1,0:T(8,128)S(1)} %collective-permute-done.after.refs_0_, f32[200,128]{1,0:T(8,128)S(1)} %collective-permute-done.1.refs_1_, f32[200,128]{1,0:T(8,128)S(1)} %collective-permute-done.2.refs_2_, f32[200,128]{1,0:T(8,128)S(1)} %collective-permute-done.3.refs_3_, ...), custom_call_target="tpu_custom_call" | custom-call | flops 100000000 | bytes 4194304 | tf_op jit(solution)/shard_map/couple_and_finish/pallas_call | solution.py:531
Async XLA Ops:
  1.3 0.7 %copy-start.9 = (s32[1,1,1,192]{3,2,1,0:T(1,128)S(1)}, s32[1,1,1,192]{3,2,1,0:T(1,128)}, u32[]{:S(2)}) copy-start(s32[1,1,1,192]{3,2,1,0:T(1,128)} %param.23) | copy-start | bytes 2308
  1.3 0.7 %copy-start.10 = (s32[1,1,1,192]{3,2,1,0:T(1,128)S(1)}, s32[1,1,1,192]{3,2,1,0:T(1,128)}, u32[]{:S(2)}) copy-start(s32[1,1,1,192]{3,2,1,0:T(1,128)} %param.24) | copy-start | bytes 2308
  1.3 0.7 %copy-start.7 = (s32[1,1,1,192,1]{3,4,2,1,0:T(1,128)S(1)}, s32[1,1,1,192,1]{3,4,2,1,0:T(1,128)}, u32[]{:S(2)}) copy-start(s32[1,1,1,192,1]{3,4,2,1,0:T(1,128)} %param.21) | copy-start | bytes 2308
  1.3 0.7 %copy-start.8 = (s32[1,1,1,192]{3,2,1,0:T(1,128)S(1)}, s32[1,1,1,192]{3,2,1,0:T(1,128)}, u32[]{:S(2)}) copy-start(s32[1,1,1,192]{3,2,1,0:T(1,128)} %param.22) | copy-start | bytes 2308
  1.3 0.7 %copy-start.5 = (s32[1,1,1,192]{3,2,1,0:T(1,128)S(1)}, s32[1,1,1,192]{3,2,1,0:T(1,128)}, u32[]{:S(2)}) copy-start(s32[1,1,1,192]{3,2,1,0:T(1,128)} %param.19) | copy-start | bytes 2308
  1.3 0.7 %copy-start.6 = (s32[1,1,1,192]{3,2,1,0:T(1,128)S(1)}, s32[1,1,1,192]{3,2,1,0:T(1,128)}, u32[]{:S(2)}) copy-start(s32[1,1,1,192]{3,2,1,0:T(1,128)} %param.20) | copy-start | bytes 2308
  1.3 0.7 %copy-start.4 = (s32[1,1,1,192]{3,2,1,0:T(1,128)S(1)}, s32[1,1,1,192]{3,2,1,0:T(1,128)}, u32[]{:S(2)}) copy-start(s32[1,1,1,192]{3,2,1,0:T(1,128)} %param.18) | copy-start | bytes 2308
  2.6 1.0 %copy-start = (f32[1,4,8,32,128]{4,3,2,1,0:T(8,128)S(1)}, f32[1,4,8,32,128]{4,3,2,1,0:T(8,128)}, u32[]{:S(2)}) copy-start(f32[1,4,8,32,128]{4,3,2,1,0:T(8,128)} %param.13) | copy-start | bytes 1572868
  3.6 14.5 %copy-start.1 = (f32[1,4,8,32,128]{4,3,2,1,0:T(8,128)S(1)}, f32[1,4,8,32,128]{4,3,2,1,0:T(8,128)}, u32[]{:S(2)}) copy-start(f32[1,4,8,32,128]{4,3,2,1,0:T(8,128)} %param.13) | copy-start | bytes 1572868
  3.6 14.5 %copy-start.2 = (f32[1,4,8,32,128]{4,3,2,1,0:T(8,128)S(1)}, f32[1,4,8,32,128]{4,3,2,1,0:T(8,128)}, u32[]{:S(2)}) copy-start(f32[1,4,8,32,128]{4,3,2,1,0:T(8,128)} %param.14) | copy-start | bytes 1572868
  5.7 6.9 %collective-permute-start = (f32[200,128]{1,0:T(8,128)S(1)}, f32[200,128]{1,0:T(8,128)S(1)}, u32[]{:S(2)}, u32[]{:S(2)}) collective-permute-start(f32[200,128]{1,0:T(8,128)S(1)} %get-tuple-element.31), channel_id=1, source_target_pairs={{0,2},{2,0},{4,6},{6,4},{8,10},{10,8},{12,14},{14,12},{1,3},{3,1},... | collective-permute-start | bytes 307208 | tf_op jit(solution)/shard_map/ppermute | solution.py:505
  6.2 10.4 %collective-permute-start.1 = (f32[200,128]{1,0:T(8,128)S(1)}, f32[200,128]{1,0:T(8,128)S(1)}, u32[]{:S(2)}, u32[]{:S(2)}) collective-permute-start(f32[200,128]{1,0:T(8,128)S(1)} %get-tuple-element.33), channel_id=1, source_target_pairs={{0,6},{2,4},{4,10},{6,8},{8,14},{10,12},{12,2},{14,0},{1,7},{3,5},... | collective-permute-start | bytes 307208 | tf_op jit(solution)/shard_map/ppermute | solution.py:505
  8.9 11.4 %collective-permute-start.2 = (f32[200,128]{1,0:T(8,128)S(1)}, f32[200,128]{1,0:T(8,128)S(1)}, u32[]{:S(2)}, u32[]{:S(2)}) collective-permute-start(f32[200,128]{1,0:T(8,128)S(1)} %get-tuple-element.34), channel_id=1, source_target_pairs={{0,10},{2,8},{4,14},{6,12},{8,2},{10,0},{12,6},{14,4},{1,11},{3,9}... | collective-permute-start | bytes 307208 | tf_op jit(solution)/shard_map/ppermute | solution.py:505
  11.2 7.0 %copy-start.3 = (f32[2,4,4]{2,1,0:T(4,128)S(1)}, f32[2,4,4]{2,1,0:T(4,128)}, u32[]{:S(2)}) copy-start(f32[2,4,4]{2,1,0:T(4,128)} %mixing.1) | copy-start | bytes 388
  11.2 9.2 %collective-permute-start.3 = (f32[200,128]{1,0:T(8,128)S(1)}, f32[200,128]{1,0:T(8,128)S(1)}, u32[]{:S(2)}, u32[]{:S(2)}) collective-permute-start(f32[200,128]{1,0:T(8,128)S(1)} %get-tuple-element.35), channel_id=1, source_target_pairs={{0,14},{2,12},{4,2},{6,0},{8,6},{10,4},{12,10},{14,8},{1,15},{3,13... | collective-permute-start | bytes 307208 | tf_op jit(solution)/shard_map/ppermute | solution.py:505
  12.6 5.6 %copy-start.12 = (f32[2,4]{1,0:T(2,128)S(1)}, f32[2,4]{1,0:T(2,128)}, u32[]{:S(2)}) copy-start(f32[2,4]{1,0:T(2,128)} %drag.1) | copy-start | bytes 100
  12.6 5.6 %copy-start.11 = (f32[2,3]{1,0:T(2,128)S(1)}, f32[2,3]{1,0:T(2,128)}, u32[]{:S(2)}) copy-start(f32[2,3]{1,0:T(2,128)} %advect.1) | copy-start | bytes 76
  12.6 7.8 %collective-permute-start.4 = (f32[128,128]{1,0:T(8,128)S(1)}, f32[128,128]{1,0:T(8,128)S(1)}, u32[]{:S(2)}, u32[]{:S(2)}) collective-permute-start(f32[128,128]{1,0:T(8,128)S(1)} %get-tuple-element.38), channel_id=1, source_target_pairs={{0,4},{4,8},{8,12},{1,5},{5,9},{9,13},{2,6},{6,10},{10,14},{3,7},{... | collective-permute-start | bytes 196616 | tf_op jit(solution)/shard_map/ppermute | solution.py:452
  15.3 6.2 %collective-permute-start.5 = (f32[128,128]{1,0:T(8,128)S(1)}, f32[128,128]{1,0:T(8,128)S(1)}, u32[]{:S(2)}, u32[]{:S(2)}) collective-permute-start(f32[128,128]{1,0:T(8,128)S(1)} %get-tuple-element.39), channel_id=1, source_target_pairs={{4,0},{8,4},{12,8},{5,1},{9,5},{13,9},{6,2},{10,6},{14,10},{7,3},{... | collective-permute-start | bytes 196616 | tf_op jit(solution)/shard_map/ppermute | solution.py:452
  16.6 3.8 %collective-permute-start.6 = (f32[32,128]{1,0:T(8,128)S(1)}, f32[32,128]{1,0:T(8,128)S(1)}, u32[]{:S(2)}, u32[]{:S(2)}) collective-permute-start(f32[32,128]{1,0:T(8,128)S(1)} %get-tuple-element.40), channel_id=1, source_target_pairs={{0,1},{1,0},{2,3},{3,2},{4,5},{5,4},{6,7},{7,6},{8,9},{9,8},{10,11... | collective-permute-start | bytes 49160 | tf_op jit(solution)/shard_map/ppermute | solution.py:513

commit v3 on v2

--- a/solution.py
+++ b/solution.py
@@ -162,20 +162,23 @@
 
 
 def send_order(ranks):
-    return sorted(range(ranks), key=lambda k: -min(k, ranks - k))
+    return list(range(ranks))[::-1]
+
+
+def neighbour_messages(ranks):
+    return [k for k in range(1, ranks) if k & (k + 1) == 0]
 
 
 def plan_kernel(
     ranks, slots, elem, side, code, rank, p_elem, p_side, p_quadrant,
-    head_out, columns_out, slot_out, maps_high, maps_low,
+    head_out, which_out, picked_out, placed_out, maps_high, maps_low,
 ):
     capacity = elem.shape[1]
     me = lax.axis_index("elem")
     group, ez = face_number(elem[...], side[...])
     codes = code[...]
     map_index = jnp.where(codes == 5, 5 + p_quadrant[...], codes)
-    apart = rank[...] - me
-    apart = jnp.where(apart < 0, apart + ranks, apart)
+    apart = rank[...] ^ me
     to_group, to_ez = face_number(p_elem[...], p_side[...])
     kind = jnp.where(codes == 5, 2 + p_quadrant[...], 1)
     rows = [group, ez, map_index, apart, to_group, to_ez, kind]
@@ -185,10 +188,13 @@
     head_out[...] = head
     here, there = iota((capacity, capacity), 0), iota((capacity, capacity), 1)
     columns = dot_t(one(here == there), head.astype(bf16))
-    columns_out[...] = columns
+    which_out[...] = columns[:, 2:3]
+    source = (columns[:, 0:1] * 16.0 + columns[:, 1:2]).astype(jnp.int32)
+    picked_out[...] = one(source == iota((capacity, FACES), 1))
     earlier = (columns[:, 3:4] == apart.astype(f32)) & (here < there)
     position = jnp.sum(jnp.where(earlier, 1.0, 0.0), axis=0, keepdims=True).astype(jnp.int32)
-    slot_out[...] = jnp.where(position < slots, apart * slots + position, -1)
+    slot = jnp.where(position < slots, apart * slots + position, -1)
+    placed_out[...] = one(iota((ranks * slots, capacity), 0) == slot)
 
     _, _, fine, coarse = node_tables(NODES)
     lane = iota((8, 128), 1)
@@ -208,21 +214,30 @@
         maps_low[:, lanes] = low
 
 
-def send_kernel(ranks, slots, field, count, planned, columns_in, slot_in, maps_high, maps_low, *outs):
-    messages, faces_out, layers = outs[:ranks], outs[ranks], outs[ranks + 1 :]
+def send_kernel(
+    ranks, slots, field, count, planned, which_in, picked, placed_in, maps_high, maps_low, *outs
+):
+    messages, faces_out, x_layers, y_layers = (
+        outs[:ranks], outs[ranks], outs[ranks + 1 : ranks + 1 + len(neighbour_messages(ranks))],
+        outs[ranks + 1 + len(neighbour_messages(ranks)) :],
+    )
     capacity = planned.shape[1]
     lines = iota((8, capacity), 0)
     unused = (lines == 6) & (iota((8, capacity), 1) >= count[...])
     head = jnp.where(unused, 0.0, planned[...]).astype(bf16)
-    columns, slot = columns_in[...], slot_in[...]
-    for v in range(4):
-        layers[0][v * 32 : v * 32 + 32, :] = field[v * 256 : v * 256 + 32, :]
-        layers[1][v * 32 : v * 32 + 32, :] = field[v * 256 + 224 : v * 256 + 256, :]
-    if len(layers) == 3:
-        layers[2][...] = jnp.where(lax.axis_index("sub") == 0, y_row(field, 31), y_row(field, 0))
+    me = lax.axis_index("elem")
+    for i, k in enumerate(neighbour_messages(ranks)):
+        for v in range(4):
+            x_layers[i][v * 32 : v * 32 + 32, :] = jnp.where(
+                me ^ k == me + 1,
+                field[v * 256 + 224 : v * 256 + 256, :],
+                field[v * 256 : v * 256 + 32, :],
+            )
+    if len(y_layers) == 1:
+        y_layers[0][...] = jnp.where(lax.axis_index("sub") == 0, y_row(field, 31), y_row(field, 0))
     else:
-        layers[2][...] = y_row(field, 0)
-        layers[3][...] = y_row(field, 31)
+        y_layers[0][...] = y_row(field, 0)
+        y_layers[1][...] = y_row(field, 31)
 
     order = lane_order(False)
     parts = []
@@ -260,10 +275,8 @@
     faces_out[...] = faces
 
     faces_high, faces_low = split(faces)
-    source = (columns[:, 0:1] * 16.0 + columns[:, 1:2]).astype(jnp.int32)
-    picked = one(source == iota((capacity, FACES), 1))
-    values = dot_t(picked, faces_high) + dot_t(picked, faces_low)
-    which = columns[:, 2:3]
+    values = dot_t(picked[...], faces_high) + dot_t(picked[...], faces_low)
+    which = which_in[...]
     pair = jnp.concatenate([values[:, :128], values[:, 128:]], axis=0)
     pair_high, pair_low = split(pair)
     out = dot(jnp.concatenate([pair_high, pair_low], axis=1), maps_high[...])
@@ -274,7 +287,7 @@
     mapped = [pair[:capacity], pair[capacity:]]
     mapped_high, mapped_low = split(jnp.concatenate(mapped, axis=1))
     for message, k in zip(messages, send_order(ranks)):
-        placed = one(iota((slots, capacity), 0) + k * slots == slot)
+        placed = placed_in[k * slots : (k + 1) * slots, :]
         rows = dot(placed, mapped_high) + dot(placed, mapped_low)
         message[0:slots, :] = rows[:, :128]
         message[slots : 2 * slots, :] = rows[:, 128:]
@@ -296,12 +309,13 @@
 
     me, sub, subs = lax.axis_index("elem"), lax.axis_index("sub"), lax.axis_size("sub")
     values = [drag[comp, v] * scale for v in range(4)]
-    values.append(jnp.where(me > 0, left[0], 0.0))
-    values.append(jnp.where(me < ranks - 1, right[0], 0.0))
     values.append(jnp.where(sub > 0, left[1], 0.0))
     values.append(jnp.where(sub < subs - 1, right[1], 0.0))
-    line = iota((8, 128), 0)
-    lines = jnp.zeros((8, 128), f32)
+    for k in neighbour_messages(ranks):
+        values.append(jnp.where(me ^ k == me - 1, left[0], 0.0))
+        values.append(jnp.where(me ^ k == me + 1, right[0], 0.0))
+    line = iota(gains.shape, 0)
+    lines = jnp.zeros(gains.shape, f32)
     for i, value in enumerate(values):
         lines = jnp.where(line == i, time_step * value, lines)
     gains[...] = lines
@@ -368,8 +382,9 @@
 
 def finish_kernel(ranks, slots, *refs):
     messages = refs[:ranks]
-    base, field, faces, x_before, x_after, y_before, y_after, gains = refs[ranks : ranks + 8]
-    new_out, advanced_out, new, advanced, left = refs[ranks + 8 :]
+    base, field, faces, y_before, y_after, gains = refs[ranks : ranks + 6]
+    layers = refs[ranks + 6 : -5]
+    new_out, advanced_out, new, advanced, left = refs[-5:]
     total = jnp.zeros((FACES, 256), f32)
     masks = jnp.zeros((16, FACES), f32)
     for message in messages:
@@ -420,11 +435,11 @@
                     at = ((8 + (4 if j else 0) + ey) * 4 + v) * 8
                     rate += moved[at : at + 8]
                 if y == 0:
-                    rate += gains[6:7, :] * y_before[v * 8 : v * 8 + 8, :]
+                    rate += gains[4:5, :] * y_before[v * 8 : v * 8 + 8, :]
                 if y == 31:
-                    rate += gains[7:8, :] * y_after[v * 8 : v * 8 + 8, :]
+                    rate += gains[5:6, :] * y_after[v * 8 : v * 8 + 8, :]
                 new[pl.ds(v * 256 + y, 8, stride=32), :] = rate
-        for end, beside in ((0, x_before), (1, x_after)):
+        for end in (0, 1):
             at = v * 256 + (NODES - 1) * end * 32
             coupled = jnp.concatenate(
                 [
@@ -433,7 +448,9 @@
                 ],
                 axis=0,
             )
-            coupled += gains[4 + end : 5 + end, :] * beside[v * 32 : v * 32 + 32, :]
+            for i in range(len(layers)):
+                beside = layers[i][v * 32 : v * 32 + 32, :]
+                coupled += gains[6 + 2 * i + end : 7 + 2 * i + end, :] * beside
             new[pl.ds(at, 32), :] = new[pl.ds(at, 32), :] + coupled
         rows = pl.ds(v * 256, 256)
         advanced[rows, :] = field[rows, :] + section_weight * new[rows, :]
@@ -461,6 +478,7 @@
     slots = max(2, 2 * capacity // ranks)
     subs = lax.axis_size("sub")
     layers = 1 if subs == 2 else 2
+    carriers = neighbour_messages(ranks)
     flat = field.reshape(1024, 128)
     vmem = pl.BlockSpec(memory_space=pltpu.VMEM)
     smem = pl.BlockSpec(memory_space=pltpu.SMEM)
@@ -469,46 +487,48 @@
         functools.partial(plan_kernel, ranks, slots),
         out_shape=[
             jax.ShapeDtypeStruct((8, capacity), f32),
-            jax.ShapeDtypeStruct((capacity, 8), f32),
-            jax.ShapeDtypeStruct(row, jnp.int32),
+            jax.ShapeDtypeStruct((capacity, 1), f32),
+            jax.ShapeDtypeStruct((capacity, FACES), bf16),
+            jax.ShapeDtypeStruct((ranks * slots, capacity), bf16),
             jax.ShapeDtypeStruct((256, CODES * 128), bf16),
             jax.ShapeDtypeStruct((128, CODES * 128), bf16),
         ],
         in_specs=[vmem] * 7,
-        out_specs=[vmem] * 5,
+        out_specs=[vmem] * 6,
         compiler_params=pltpu.CompilerParams(vmem_limit_bytes=32 << 20),
-        cost_estimate=pl.CostEstimate(flops=10**7, bytes_accessed=1 << 20, transcendentals=0),
+        cost_estimate=pl.CostEstimate(flops=10**9, bytes_accessed=8 << 20, transcendentals=0),
         name="plan_records",
     )(
         face_elem.reshape(row), face_side.reshape(row), mortar_code.reshape(row),
         partner_rank.reshape(row), partner_elem.reshape(row), partner_side.reshape(row),
         partner_quadrant.reshape(row),
     )
+    face_count, plan = lax.optimization_barrier((face_count, plan))
     outs = pl.pallas_call(
         functools.partial(send_kernel, ranks, slots),
         out_shape=[jax.ShapeDtypeStruct((2 * slots + 8, 128), f32)] * ranks
         + [jax.ShapeDtypeStruct((256, FACES), f32)]
-        + [jax.ShapeDtypeStruct((128, 128), f32)] * 2
+        + [jax.ShapeDtypeStruct((128, 128), f32)] * len(carriers)
         + [jax.ShapeDtypeStruct((32, 128), f32)] * layers,
-        in_specs=[vmem] * 7,
-        out_specs=[vmem] * (ranks + 3 + layers),
+        in_specs=[vmem] * 8,
+        out_specs=[vmem] * (ranks + 1 + len(carriers) + layers),
         compiler_params=pltpu.CompilerParams(vmem_limit_bytes=32 << 20),
         cost_estimate=pl.CostEstimate(flops=10**8, bytes_accessed=2 << 20, transcendentals=0),
         name="send_faces",
     )(flat, face_count.reshape(1, 1), *plan)
-    faces = outs[ranks]
-    received = [None] * ranks
-    for out, k in zip(outs, send_order(ranks)):
-        pairs = [
-            (2 * e + c, 2 * ((e + k) % ranks) + 1 - c) for e in range(ranks) for c in range(2)
-        ]
-        received[k] = lax.ppermute(out, ("elem", "comp"), pairs)
-
-    (x_first, x_last, *y_layers), received[0] = lax.optimization_barrier(
-        (outs[ranks + 1 :], received[0])
-    )
-    x_before = along(x_last, "elem", 1)
-    x_after = along(x_first, "elem", -1)
+    faces, layers_out = outs[ranks], outs[ranks + 1 :]
+    outgoing = dict(zip(send_order(ranks), outs))
+    received = {}
+    for k in send_order(ranks):
+        pairs = [(2 * e + c, 2 * (e ^ k) + 1 - c) for e in range(ranks) for c in range(2)]
+        received[k] = lax.ppermute(outgoing[k], ("elem", "comp"), pairs)
+
+    layers_out, received[0] = lax.optimization_barrier((layers_out, received[0]))
+    x_layers, y_layers = layers_out[: len(carriers)], layers_out[len(carriers) :]
+    beside = []
+    for k, layer in zip(carriers, x_layers):
+        pairs = [(e, e ^ k) for e in range(ranks) if abs((e ^ k) - e) == 1]
+        beside.append(lax.ppermute(layer, "elem", pairs))
     if layers == 1:
         y_before = y_after = lax.ppermute(y_layers[0], "sub", [(0, 1), (1, 0)])
     else:
@@ -518,7 +538,7 @@
         functools.partial(local_kernel, ranks),
         out_shape=[
             jax.ShapeDtypeStruct((1024, 128), f32),
-            jax.ShapeDtypeStruct((8, 128), f32),
+            jax.ShapeDtypeStruct((16, 128), f32),
         ],
         in_specs=[vmem, vmem, smem, smem, smem, pl.BlockSpec(memory_space=pl.ANY)],
         out_specs=[vmem] * 2,
@@ -531,13 +551,15 @@
     new, advanced = pl.pallas_call(
         functools.partial(finish_kernel, ranks, slots),
         out_shape=[jax.ShapeDtypeStruct((1024, 128), f32)] * 2,
-        in_specs=[vmem] * (ranks + 8),
+        in_specs=[vmem] * (ranks + 6 + len(carriers)),
         out_specs=[pl.BlockSpec(memory_space=pl.ANY)] * 2,
         scratch_shapes=[pltpu.VMEM((1024, 128), f32)] * 2 + [pltpu.SemaphoreType.DMA((8,))],
         compiler_params=pltpu.CompilerParams(vmem_limit_bytes=32 << 20),
         cost_estimate=pl.CostEstimate(flops=10**8, bytes_accessed=4 << 20, transcendentals=0),
         name="couple_and_finish",
-    )(*received, base, flat, faces, x_before, x_after, y_before, y_after, gains)
+    )(
+        *[received[k] for k in send_order(ranks)], base, flat, faces, y_before, y_after, gains, *beside
+    )
     return new.reshape(field.shape), advanced.reshape(field.shape)
 
 

time: 24 us -> 22 us (0.917)
  starting transfers between devices: 12.4 us -> 9.06 us
  waiting for transfers between devices: 1.13 us -> 2.93 us
  local copies, waits for them, and re-layouts: 1.77 us -> 1.1 us
    ppermute x6, starting transfers between devices: 10.9 us -> 7.59 us  [the longest x4 5.55 us: on_device(): received[k] = lax.ppermute(outgoing[k], ('elem', 'comp'), pairs)]
    ppermute x6, waiting for transfers between devices: 1.05 us -> 2.93 us  [the longest x4 2.69 us: on_device(): received[k] = lax.ppermute(outgoing[k], ('elem', 'comp'), pairs)]
    unnamed x26 -> x24, local copies, waits for them, and re-layouts: 1.77 us -> 1.1 us
  transfers between devices with their start and end apart: 7 -> 7, of which waited for: 2 -> 3; matrix products, arithmetic and copies ran while one was open for 0% -> 0% of each run, Pallas kernels for 9% -> 10%
where the time goes in v3:
time: 22 us; the launch traced here: 21.6 us
  starting transfers between devices  9.06 us (41%)
  Pallas kernels  7.09 us (32%)
  waiting for transfers between devices  2.93 us (13%)
  between operations  1.38 us (6%)
  local copies, waits for them, and re-layouts  1.1 us (5%)
    ppermute x4, starting transfers between devices, on_device(): received[k] = lax.ppermute(outgoing[k], ('elem', 'comp'), pairs)  5.55 us
    ppermute x4, waiting for transfers between devices, on_device(): received[k] = lax.ppermute(outgoing[k], ('elem', 'comp'), pairs)  2.69 us
    pallas_call x1, Pallas kernels, on_device(): pl.pallas_call(functools.partial(finish_kernel, ranks, slots), out_shape=...  2.29 us
    pallas_call x1, Pallas kernels, on_device(): pl.pallas_call(functools.partial(local_kernel, ranks), out_shape=[jax.Sha...  2.11 us
    ppermute x2, starting transfers between devices, on_device(): beside.append(lax.ppermute(layer, 'elem', pairs))  2.04 us
    pallas_call x1, Pallas kernels, on_device(): pl.pallas_call(functools.partial(send_kernel, ranks, slots), out_shape=[j...  2.02 us
    ppermute x1, starting transfers between devices, on_device(): y_before = y_after = lax.ppermute(y_layers[0], 'sub', [(0, 1), (1, 0)])  1.47 us
    unnamed x24, local copies, waits for them, and re-layouts  1.1 us
  transfers between devices with their start and end apart: 7, of which 3 were waited for; matrix products, arithmetic and copies ran while one was open for 0% of the time, Pallas kernels for 10%

profile of v3, /device:TPU:0, one launch (start us, length us, event | category | flops | bytes accessed | tf_op | source)
XLA Modules:
  0.0 21.6 jit_solution(8127155497384186136)
XLA Ops:
  1.3 0.0 copy-start.8
  1.3 0.0 copy-start.9
  1.3 0.0 copy-start.6
  1.3 0.0 copy-start.7
  1.3 0.0 copy-start.4
  1.3 0.0 copy-start.5
  1.3 0.0 copy-start.3
  1.3 0.6 %copy-done.8 = s32[1,1,1,192]{3,2,1,0:T(1,128)S(1)} copy-done((s32[1,1,1,192]{3,2,1,0:T(1,128)S(1)}, s32[1,1,1,192]{3,2,1,0:T(1,128)}, u32[]{:S(2)}) %copy-start.8) | copy-done | bytes 792
  2.0 0.0 copy-done.9
  2.0 0.0 copy-done.6
  2.0 0.0 copy-done.7
  2.0 0.0 copy-done.4
  2.0 0.0 copy-done.5
  2.0 0.0 copy-done.3
  2.1 0.0 copy-start
  2.1 0.7 %plan_records.1 = (f32[8,192]{1,0:T(8,128)S(1)}, f32[192,1]{1,0:T(8,128)S(1)}, bf16[192,384]{1,0:T(8,128)(2,1)S(1)}, bf16[384,192]{1,0:T(8,128)(2,1)S(1)}, bf16[...) custom-call(s32[1,192]{1,0:T(1,128)S(1)} %bitcast.17, s32[1,192]{1,0:T(1,128)S(1)} %bitcast.18, ...), custom_call_target="tpu_custom_call" | custom-call | flops 1000000000 | bytes 8388608 | tf_op jit(solution)/shard_map/plan_records/pallas_call | solution.py:486
  2.7 0.4 %copy-done = f32[1,4,8,32,128]{4,3,2,1,0:T(8,128)S(1)} copy-done((f32[1,4,8,32,128]{4,3,2,1,0:T(8,128)S(1)}, f32[1,4,8,32,128]{4,3,2,1,0:T(8,128)}, u32[]{:S(2)}) %copy-start) | copy-done | bytes 524312
  3.1 0.0 copy-start.1
  3.1 2.0 %send_faces.1 = (f32[200,128]{1,0:T(8,128)S(1)}, f32[200,128]{1,0:T(8,128)S(1)}, f32[200,128]{1,0:T(8,128)S(1)}, f32[200,128]{1,0:T(8,128)S(1)}, f32[256,384]{1,...) custom-call(f32[1024,128]{1,0:T(8,128)S(1)} %bitcast.13, ...), custom_call_target="tpu_custom_call" | custom-call | flops 100000000 | bytes 2097152 | tf_op jit(solution)/shard_map/send_faces/pallas_call | solution.py:507
  5.1 0.5 %collective-permute-start.3 = (f32[200,128]{1,0:T(8,128)S(1)}, f32[200,128]{1,0:T(8,128)S(1)}, u32[]{:S(2)}, u32[]{:S(2)}) collective-permute-start(f32[200,128]{1,0:T(8,128)S(1)} %get-tuple-element.50), channel_id=1, source_target_pairs={{0,2},{2,0},{4,6},{6,4},{8,10},{10,8},{12,14},{14,12},{1,3},{3,1},... | collective-permute-start | bytes 307208 | tf_op jit(solution)/shard_map/ppermute | solution.py:524
  5.6 4.7 %collective-permute-start = (f32[200,128]{1,0:T(8,128)S(1)}, f32[200,128]{1,0:T(8,128)S(1)}, u32[]{:S(2)}, u32[]{:S(2)}) collective-permute-start(f32[200,128]{1,0:T(8,128)S(1)} %get-tuple-element.44), channel_id=1, source_target_pairs={{0,14},{2,12},{4,10},{6,8},{8,6},{10,4},{12,2},{14,0},{1,15},{3,13... | collective-permute-start | bytes 307208 | tf_op jit(solution)/shard_map/ppermute | solution.py:524
  10.4 0.0 collective-permute-start.1
  10.4 0.0 copy-start.2
  10.4 0.3 %collective-permute-start.2 = (f32[200,128]{1,0:T(8,128)S(1)}, f32[200,128]{1,0:T(8,128)S(1)}, u32[]{:S(2)}, u32[]{:S(2)}) collective-permute-start(f32[200,128]{1,0:T(8,128)S(1)} %get-tuple-element.46), channel_id=1, source_target_pairs={{0,6},{2,4},{4,2},{6,0},{8,14},{10,12},{12,10},{14,8},{1,7},{3,5},... | collective-permute-start | bytes 307208 | tf_op jit(solution)/shard_map/ppermute | solution.py:524
  10.7 0.0 collective-permute-done.3.after.refs_3_
  10.7 0.0 copy-start.11
  10.7 0.0 copy-start.10
  10.7 1.4 %collective-permute-start.5 = (f32[128,128]{1,0:T(8,128)S(1)}, f32[128,128]{1,0:T(8,128)S(1)}, u32[]{:S(2)}, u32[]{:S(2)}) collective-permute-start(f32[128,128]{1,0:T(8,128)S(1)} %get-tuple-element.56), channel_id=1, source_target_pairs={{0,4},{4,0},{8,12},{12,8},{1,5},{5,1},{9,13},{13,9},{2,6},{6,2},{1... | collective-permute-start | bytes 196616 | tf_op jit(solution)/shard_map/ppermute | solution.py:531
  12.1 0.7 %collective-permute-start.6 = (f32[128,128]{1,0:T(8,128)S(1)}, f32[128,128]{1,0:T(8,128)S(1)}, u32[]{:S(2)}, u32[]{:S(2)}) collective-permute-start(f32[128,128]{1,0:T(8,128)S(1)} %get-tuple-element.57), channel_id=1, source_target_pairs={{4,8},{8,4},{5,9},{9,5},{6,10},{10,6},{7,11},{11,7},{20,24},{24,20... | collective-permute-start | bytes 196616 | tf_op jit(solution)/shard_map/ppermute | solution.py:531
  12.7 0.9 %collective-permute-done.refs_0_ = f32[200,128]{1,0:T(8,128)S(1)} collective-permute-done((f32[200,128]{1,0:T(8,128)S(1)}, f32[200,128]{1,0:T(8,128)S(1)}, u32[]{:S(2)}, u32[]{:S(2)}) %collective-permute-start) | collective-permute-done | bytes 102432 | tf_op jit(solution)/shard_map/ppermute | solution.py:524
  13.7 1.5 %collective-permute-start.4 = (f32[32,128]{1,0:T(8,128)S(1)}, f32[32,128]{1,0:T(8,128)S(1)}, u32[]{:S(2)}, u32[]{:S(2)}) collective-permute-start(f32[32,128]{1,0:T(8,128)S(1)} %get-tuple-element.54), channel_id=1, source_target_pairs={{0,1},{1,0},{2,3},{3,2},{4,5},{5,4},{6,7},{7,6},{8,9},{9,8},{10,11... | collective-permute-start | bytes 49160 | tf_op jit(solution)/shard_map/ppermute | solution.py:533
  15.1 0.0 copy-done.1
  15.1 0.0 copy-done.2
  15.1 0.0 copy-done.11
  15.1 0.0 copy-done.10
  15.1 2.1 %local_rate.1 = (f32[1024,128]{1,0:T(8,128)S(1)}, f32[16,128]{1,0:T(8,128)S(1)}) custom-call(f32[1024,128]{1,0:T(8,128)S(1)} %bitcast.14, f32[1024,128]{1,0:T(8,128)S(1)} %bitcast.16, f32[2,3]{1,0:T(2,128)S(1)} %copy-done.10, f32[2,4,4]{2,1,0:T(4,128)S(1)} %copy-done.2, f32[2,4]{1,0:T(2,128)S(1)} %copy-done.11, ...), custom_call_target="tpu_custom_call" | custom-call | flops 500000000 | bytes 4194304 | tf_op jit(solution)/shard_map/local_rate/pallas_call | solution.py:537
  17.3 1.8 %collective-permute-done.1.refs_1_ = f32[200,128]{1,0:T(8,128)S(1)} collective-permute-done((f32[200,128]{1,0:T(8,128)S(1)}, f32[200,128]{1,0:T(8,128)S(1)}, u32[]{:S(2)}, u32[]{:S(2)}) %collective-permute-start.1) | collective-permute-done | bytes 102432 | tf_op jit(solution)/shard_map/ppermute | solution.py:524
  19.0 0.0 collective-permute-done.2.refs_2_
  19.0 0.0 collective-permute-done.4.refs_7_.refs_8_
  19.0 0.2 %collective-permute-done.5.refs_10_ = f32[128,128]{1,0:T(8,128)S(1)} collective-permute-done((f32[128,128]{1,0:T(8,128)S(1)}, f32[128,128]{1,0:T(8,128)S(1)}, u32[]{:S(2)}, u32[]{:S(2)}) %collective-permute-start.5) | collective-permute-done | bytes 65568 | tf_op jit(solution)/shard_map/ppermute | solution.py:531
  19.3 0.0 collective-permute-done.6.refs_11_
  19.3 2.3 %couple_and_finish.1 = (f32[1024,128]{1,0:T(8,128)}, f32[1024,128]{1,0:T(8,128)}) custom-call(f32[200,128]{1,0:T(8,128)S(1)} %collective-permute-done.refs_0_, f32[200,128]{1,0:T(8,128)S(1)} %collective-permute-done.1.refs_1_, f32[200,128]{1,0:T(8,128)S(1)} %collective-permute-done.2.refs_2_, f32[200,128]{1,0:T(8,128)S(1)} %collective-permute-done.3.after.refs_3_, ...), custom_call_target="tpu_custom_call" | custom-call | flops 100000000 | bytes 4194304 | tf_op jit(solution)/shard_map/couple_and_finish/pallas_call | solution.py:551
Async XLA Ops:
  1.3 0.7 %copy-start.8 = (s32[1,1,1,192]{3,2,1,0:T(1,128)S(1)}, s32[1,1,1,192]{3,2,1,0:T(1,128)}, u32[]{:S(2)}) copy-start(s32[1,1,1,192]{3,2,1,0:T(1,128)} %param.23) | copy-start | bytes 2308
  1.3 0.7 %copy-start.9 = (s32[1,1,1,192]{3,2,1,0:T(1,128)S(1)}, s32[1,1,1,192]{3,2,1,0:T(1,128)}, u32[]{:S(2)}) copy-start(s32[1,1,1,192]{3,2,1,0:T(1,128)} %param.24) | copy-start | bytes 2308
  1.3 0.7 %copy-start.6 = (s32[1,1,1,192,1]{3,4,2,1,0:T(1,128)S(1)}, s32[1,1,1,192,1]{3,4,2,1,0:T(1,128)}, u32[]{:S(2)}) copy-start(s32[1,1,1,192,1]{3,4,2,1,0:T(1,128)} %param.21) | copy-start | bytes 2308
  1.3 0.7 %copy-start.7 = (s32[1,1,1,192]{3,2,1,0:T(1,128)S(1)}, s32[1,1,1,192]{3,2,1,0:T(1,128)}, u32[]{:S(2)}) copy-start(s32[1,1,1,192]{3,2,1,0:T(1,128)} %param.22) | copy-start | bytes 2308
  1.3 0.7 %copy-start.4 = (s32[1,1,1,192]{3,2,1,0:T(1,128)S(1)}, s32[1,1,1,192]{3,2,1,0:T(1,128)}, u32[]{:S(2)}) copy-start(s32[1,1,1,192]{3,2,1,0:T(1,128)} %param.19) | copy-start | bytes 2308
  1.3 0.7 %copy-start.5 = (s32[1,1,1,192]{3,2,1,0:T(1,128)S(1)}, s32[1,1,1,192]{3,2,1,0:T(1,128)}, u32[]{:S(2)}) copy-start(s32[1,1,1,192]{3,2,1,0:T(1,128)} %param.20) | copy-start | bytes 2308
  1.3 0.7 %copy-start.3 = (s32[1,1,1,192]{3,2,1,0:T(1,128)S(1)}, s32[1,1,1,192]{3,2,1,0:T(1,128)}, u32[]{:S(2)}) copy-start(s32[1,1,1,192]{3,2,1,0:T(1,128)} %param.18) | copy-start | bytes 2308
  2.1 1.0 %copy-start = (f32[1,4,8,32,128]{4,3,2,1,0:T(8,128)S(1)}, f32[1,4,8,32,128]{4,3,2,1,0:T(8,128)}, u32[]{:S(2)}) copy-start(f32[1,4,8,32,128]{4,3,2,1,0:T(8,128)} %param.13) | copy-start | bytes 1572868
  3.1 12.0 %copy-start.1 = (f32[1,4,8,32,128]{4,3,2,1,0:T(8,128)S(1)}, f32[1,4,8,32,128]{4,3,2,1,0:T(8,128)}, u32[]{:S(2)}) copy-start(f32[1,4,8,32,128]{4,3,2,1,0:T(8,128)} %param.14) | copy-start | bytes 1572868
  5.1 5.6 %collective-permute-start.3 = (f32[200,128]{1,0:T(8,128)S(1)}, f32[200,128]{1,0:T(8,128)S(1)}, u32[]{:S(2)}, u32[]{:S(2)}) collective-permute-start(f32[200,128]{1,0:T(8,128)S(1)} %get-tuple-element.50), channel_id=1, source_target_pairs={{0,2},{2,0},{4,6},{6,4},{8,10},{10,8},{12,14},{14,12},{1,3},{3,1},... | collective-permute-start | bytes 307208 | tf_op jit(solution)/shard_map/ppermute | solution.py:524
  5.6 8.0 %collective-permute-start = (f32[200,128]{1,0:T(8,128)S(1)}, f32[200,128]{1,0:T(8,128)S(1)}, u32[]{:S(2)}, u32[]{:S(2)}) collective-permute-start(f32[200,128]{1,0:T(8,128)S(1)} %get-tuple-element.44), channel_id=1, source_target_pairs={{0,14},{2,12},{4,10},{6,8},{8,6},{10,4},{12,2},{14,0},{1,15},{3,13... | collective-permute-start | bytes 307208 | tf_op jit(solution)/shard_map/ppermute | solution.py:524
  10.4 8.7 %collective-permute-start.1 = (f32[200,128]{1,0:T(8,128)S(1)}, f32[200,128]{1,0:T(8,128)S(1)}, u32[]{:S(2)}, u32[]{:S(2)}) collective-permute-start(f32[200,128]{1,0:T(8,128)S(1)} %get-tuple-element.45), channel_id=1, source_target_pairs={{0,10},{2,8},{4,14},{6,12},{8,2},{10,0},{12,6},{14,4},{1,11},{3,9}... | collective-permute-start | bytes 307208 | tf_op jit(solution)/shard_map/ppermute | solution.py:524
  10.4 4.8 %copy-start.2 = (f32[2,4,4]{2,1,0:T(4,128)S(1)}, f32[2,4,4]{2,1,0:T(4,128)}, u32[]{:S(2)}) copy-start(f32[2,4,4]{2,1,0:T(4,128)} %mixing.1) | copy-start | bytes 388
  10.4 8.7 %collective-permute-start.2 = (f32[200,128]{1,0:T(8,128)S(1)}, f32[200,128]{1,0:T(8,128)S(1)}, u32[]{:S(2)}, u32[]{:S(2)}) collective-permute-start(f32[200,128]{1,0:T(8,128)S(1)} %get-tuple-element.46), channel_id=1, source_target_pairs={{0,6},{2,4},{4,2},{6,0},{8,14},{10,12},{12,10},{14,8},{1,7},{3,5},... | collective-permute-start | bytes 307208 | tf_op jit(solution)/shard_map/ppermute | solution.py:524
  10.7 4.4 %copy-start.11 = (f32[2,4]{1,0:T(2,128)S(1)}, f32[2,4]{1,0:T(2,128)}, u32[]{:S(2)}) copy-start(f32[2,4]{1,0:T(2,128)} %drag.1) | copy-start | bytes 100
  10.7 4.4 %copy-start.10 = (f32[2,3]{1,0:T(2,128)S(1)}, f32[2,3]{1,0:T(2,128)}, u32[]{:S(2)}) copy-start(f32[2,3]{1,0:T(2,128)} %advect.1) | copy-start | bytes 76
  10.7 8.6 %collective-permute-start.5 = (f32[128,128]{1,0:T(8,128)S(1)}, f32[128,128]{1,0:T(8,128)S(1)}, u32[]{:S(2)}, u32[]{:S(2)}) collective-permute-start(f32[128,128]{1,0:T(8,128)S(1)} %get-tuple-element.56), channel_id=1, source_target_pairs={{0,4},{4,0},{8,12},{12,8},{1,5},{5,1},{9,13},{13,9},{2,6},{6,2},{1... | collective-permute-start | bytes 196616 | tf_op jit(solution)/shard_map/ppermute | solution.py:531
  12.1 7.2 %collective-permute-start.6 = (f32[128,128]{1,0:T(8,128)S(1)}, f32[128,128]{1,0:T(8,128)S(1)}, u32[]{:S(2)}, u32[]{:S(2)}) collective-permute-start(f32[128,128]{1,0:T(8,128)S(1)} %get-tuple-element.57), channel_id=1, source_target_pairs={{4,8},{8,4},{5,9},{9,5},{6,10},{10,6},{7,11},{11,7},{20,24},{24,20... | collective-permute-start | bytes 196616 | tf_op jit(solution)/shard_map/ppermute | solution.py:531
  13.7 5.4 %collective-permute-start.4 = (f32[32,128]{1,0:T(8,128)S(1)}, f32[32,128]{1,0:T(8,128)S(1)}, u32[]{:S(2)}, u32[]{:S(2)}) collective-permute-start(f32[32,128]{1,0:T(8,128)S(1)} %get-tuple-element.54), channel_id=1, source_target_pairs={{0,1},{1,0},{2,3},{3,2},{4,5},{5,4},{6,7},{7,6},{8,9},{9,8},{10,11... | collective-permute-start | bytes 49160 | tf_op jit(solution)/shard_map/ppermute | solution.py:533

commit v4 on v3

--- a/solution.py
+++ b/solution.py
@@ -171,7 +171,7 @@
 
 def plan_kernel(
     ranks, slots, elem, side, code, rank, p_elem, p_side, p_quadrant,
-    head_out, which_out, picked_out, placed_out, maps_high, maps_low,
+    head_out, which_out, picked_out, placed_out, maps,
 ):
     capacity = elem.shape[1]
     me = lax.axis_index("elem")
@@ -200,45 +200,33 @@
     lane = iota((8, 128), 1)
     along_a = table_tiles(fine + coarse, lane % 8)
     along_b = table_tiles(fine + coarse, lane // 8 % 8)
-    for index in range(CODES):
-        first = along_a[index // 4 * 2 + index % 4 // 2]
-        second = along_b[index // 4 * 2 + index % 2]
-        blocks = []
-        for v in range(2):
-            kept = jnp.where(lane // 64 == v, first, 0.0)
-            blocks += [kept * second[b : b + 1, :] for b in range(8)]
-        high, low = split(jnp.concatenate(blocks, axis=0))
-        lanes = slice(index * 128, index * 128 + 128)
-        maps_high[0:128, lanes] = high
-        maps_high[128:256, lanes] = high
-        maps_low[:, lanes] = low
+    lower = lane < 64
+    for pair in range(CODES // 2):
+        tiles = []
+        for index in (2 * pair, 2 * pair + 1):
+            tiles.append(
+                (along_a[index // 4 * 2 + index % 4 // 2], along_b[index // 4 * 2 + index % 2])
+            )
+        first = jnp.where(lower, tiles[0][0], tiles[1][0])
+        second = jnp.where(lower, tiles[0][1], tiles[1][1])
+        high, low = split(
+            jnp.concatenate([first * second[b : b + 1, :] for b in range(8)], axis=0)
+        )
+        lanes = slice(pair * 128, pair * 128 + 128)
+        maps[0:64, lanes] = high
+        maps[64:128, lanes] = high
+        maps[128:192, lanes] = low
+        maps[192:256, lanes] = jnp.zeros((64, 128), bf16)
 
 
 def send_kernel(
-    ranks, slots, field, count, planned, which_in, picked, placed_in, maps_high, maps_low, *outs
+    ranks, slots, field, count, planned, which_in, picked, placed_in, maps, *outs
 ):
-    messages, faces_out, x_layers, y_layers = (
-        outs[:ranks], outs[ranks], outs[ranks + 1 : ranks + 1 + len(neighbour_messages(ranks))],
-        outs[ranks + 1 + len(neighbour_messages(ranks)) :],
-    )
+    messages, faces_out = outs[:ranks], outs[ranks]
     capacity = planned.shape[1]
     lines = iota((8, capacity), 0)
     unused = (lines == 6) & (iota((8, capacity), 1) >= count[...])
     head = jnp.where(unused, 0.0, planned[...]).astype(bf16)
-    me = lax.axis_index("elem")
-    for i, k in enumerate(neighbour_messages(ranks)):
-        for v in range(4):
-            x_layers[i][v * 32 : v * 32 + 32, :] = jnp.where(
-                me ^ k == me + 1,
-                field[v * 256 + 224 : v * 256 + 256, :],
-                field[v * 256 : v * 256 + 32, :],
-            )
-    if len(y_layers) == 1:
-        y_layers[0][...] = jnp.where(lax.axis_index("sub") == 0, y_row(field, 31), y_row(field, 0))
-    else:
-        y_layers[0][...] = y_row(field, 0)
-        y_layers[1][...] = y_row(field, 31)
-
     order = lane_order(False)
     parts = []
     for kind_of in (0, 1):
@@ -275,24 +263,61 @@
     faces_out[...] = faces
 
     faces_high, faces_low = split(faces)
-    values = dot_t(picked[...], faces_high) + dot_t(picked[...], faces_low)
-    which = which_in[...]
-    pair = jnp.concatenate([values[:, :128], values[:, 128:]], axis=0)
-    pair_high, pair_low = split(pair)
-    out = dot(jnp.concatenate([pair_high, pair_low], axis=1), maps_high[...])
-    out += dot(pair_high, maps_low[...])
-    which = jnp.concatenate([which, which], axis=0)
-    for index in range(CODES):
-        pair = jnp.where(which == float(index + 1), out[:, index * 128 : (index + 1) * 128], pair)
-    mapped = [pair[:capacity], pair[capacity:]]
+    values = dot_t(
+        jnp.concatenate([picked[...], picked[...]], axis=1),
+        jnp.concatenate([faces_high, faces_low], axis=1),
+    )
+    lower = iota((capacity, 128), 1) < 64
+    halves = [values[:, :128], values[:, 128:]]
+    stacked = []
+    for half in halves:
+        crossed = pltpu.roll(half, 64, 1)
+        high, crossed_high = [part.astype(bf16).astype(f32) for part in (half, crossed)]
+        low, crossed_low = half - high, crossed - crossed_high
+        stacked.append(jnp.concatenate([jnp.where(lower, high, crossed_low), high], axis=1))
+        stacked.append(
+            jnp.concatenate([jnp.where(lower, crossed_high, low), crossed_high], axis=1)
+        )
+    out = dot(jnp.concatenate(stacked, axis=0).astype(bf16), maps[...])
+    which = which_in[...].astype(jnp.int32)
+    column, odd = (which - 1) >> 1, (which - 1) & 1
+    mapped = []
+    for h, half in enumerate(halves):
+        sides = []
+        for v in (2 * h, 2 * h + 1):
+            rows = out[v * capacity : (v + 1) * capacity]
+            taken = rows[:, :128]
+            for pair in range(1, CODES // 2):
+                taken = jnp.where(column == pair, rows[:, pair * 128 : pair * 128 + 128], taken)
+            sides.append(jnp.where(odd == v % 2, taken, pltpu.roll(taken, 64, 1)))
+        mapped.append(jnp.where(which == 0, half, jnp.where(lower, sides[0], sides[1])))
     mapped_high, mapped_low = split(jnp.concatenate(mapped, axis=1))
+    rows = dot(placed_in[...], mapped_high) + dot(placed_in[...], mapped_low)
+    heads = dot_t(head, placed_in[...])
     for message, k in zip(messages, send_order(ranks)):
-        placed = placed_in[k * slots : (k + 1) * slots, :]
-        rows = dot(placed, mapped_high) + dot(placed, mapped_low)
-        message[0:slots, :] = rows[:, :128]
-        message[slots : 2 * slots, :] = rows[:, 128:]
+        here = slice(k * slots, (k + 1) * slots)
+        message[0:slots, :] = rows[here, :128]
+        message[slots : 2 * slots, :] = rows[here, 128:]
         message[2 * slots : 2 * slots + 8, :] = jnp.zeros((8, 128), f32)
-        message[2 * slots : 2 * slots + 8, 0:slots] = dot_t(head, placed)
+        message[2 * slots : 2 * slots + 8, 0:slots] = heads[:, here]
+
+
+def layers_kernel(ranks, field, after, *outs):
+    carriers = len(neighbour_messages(ranks))
+    x_layers, y_layers = outs[:carriers], outs[carriers:]
+    me = lax.axis_index("elem")
+    for i, k in enumerate(neighbour_messages(ranks)):
+        for v in range(4):
+            x_layers[i][v * 32 : v * 32 + 32, :] = jnp.where(
+                me ^ k == me + 1,
+                field[v * 256 + 224 : v * 256 + 256, :],
+                field[v * 256 : v * 256 + 32, :],
+            )
+    if len(y_layers) == 1:
+        y_layers[0][...] = jnp.where(lax.axis_index("sub") == 0, y_row(field, 31), y_row(field, 0))
+    else:
+        y_layers[0][...] = y_row(field, 0)
+        y_layers[1][...] = y_row(field, 31)
 
 
 def local_kernel(
@@ -490,11 +515,10 @@
             jax.ShapeDtypeStruct((capacity, 1), f32),
             jax.ShapeDtypeStruct((capacity, FACES), bf16),
             jax.ShapeDtypeStruct((ranks * slots, capacity), bf16),
-            jax.ShapeDtypeStruct((256, CODES * 128), bf16),
-            jax.ShapeDtypeStruct((128, CODES * 128), bf16),
+            jax.ShapeDtypeStruct((256, CODES * 64), bf16),
         ],
         in_specs=[vmem] * 7,
-        out_specs=[vmem] * 6,
+        out_specs=[vmem] * 5,
         compiler_params=pltpu.CompilerParams(vmem_limit_bytes=32 << 20),
         cost_estimate=pl.CostEstimate(flops=10**9, bytes_accessed=8 << 20, transcendentals=0),
         name="plan_records",
@@ -507,23 +531,30 @@
     outs = pl.pallas_call(
         functools.partial(send_kernel, ranks, slots),
         out_shape=[jax.ShapeDtypeStruct((2 * slots + 8, 128), f32)] * ranks
-        + [jax.ShapeDtypeStruct((256, FACES), f32)]
-        + [jax.ShapeDtypeStruct((128, 128), f32)] * len(carriers)
-        + [jax.ShapeDtypeStruct((32, 128), f32)] * layers,
-        in_specs=[vmem] * 8,
-        out_specs=[vmem] * (ranks + 1 + len(carriers) + layers),
+        + [jax.ShapeDtypeStruct((256, FACES), f32)],
+        in_specs=[vmem] * 7,
+        out_specs=[vmem] * (ranks + 1),
         compiler_params=pltpu.CompilerParams(vmem_limit_bytes=32 << 20),
         cost_estimate=pl.CostEstimate(flops=10**8, bytes_accessed=2 << 20, transcendentals=0),
         name="send_faces",
     )(flat, face_count.reshape(1, 1), *plan)
-    faces, layers_out = outs[ranks], outs[ranks + 1 :]
+    faces = outs[ranks]
     outgoing = dict(zip(send_order(ranks), outs))
     received = {}
     for k in send_order(ranks):
         pairs = [(2 * e + c, 2 * (e ^ k) + 1 - c) for e in range(ranks) for c in range(2)]
         received[k] = lax.ppermute(outgoing[k], ("elem", "comp"), pairs)
 
-    layers_out, received[0] = lax.optimization_barrier((layers_out, received[0]))
+    layers_out = pl.pallas_call(
+        functools.partial(layers_kernel, ranks),
+        out_shape=[jax.ShapeDtypeStruct((128, 128), f32)] * len(carriers)
+        + [jax.ShapeDtypeStruct((32, 128), f32)] * layers,
+        in_specs=[vmem, pl.BlockSpec(memory_space=pl.ANY)],
+        out_specs=[vmem] * (len(carriers) + layers),
+        compiler_params=pltpu.CompilerParams(vmem_limit_bytes=8 << 20),
+        cost_estimate=pl.CostEstimate(flops=10**4, bytes_accessed=1 << 18, transcendentals=0),
+        name="halo_layers",
+    )(flat, received[0])
     x_layers, y_layers = layers_out[: len(carriers)], layers_out[len(carriers) :]
     beside = []
     for k, layer in zip(carriers, x_layers):

time: 22 us -> 21.7 us (0.986)
  Pallas kernels: 7.09 us -> 6.61 us
    pallas_call x1, Pallas kernels: 2.02 us -> 1.74 us  [on_device(): pl.pallas_call(functools.partial(send_kernel, ranks, slots), out_shape=[j...]
where the time goes in v4:
time: 21.7 us; the launch traced here: 21.2 us
  starting transfers between devices  9.08 us (42%)
  Pallas kernels  6.61 us (30%)
  waiting for transfers between devices  2.89 us (13%)
  between operations  1.39 us (6%)
  local copies, waits for them, and re-layouts  1.26 us (6%)
    ppermute x4, starting transfers between devices, on_device(): received[k] = lax.ppermute(outgoing[k], ('elem', 'comp'), pairs)  5.51 us
    ppermute x4, waiting for transfers between devices, on_device(): received[k] = lax.ppermute(outgoing[k], ('elem', 'comp'), pairs)  2.65 us
    pallas_call x1, Pallas kernels, on_device(): pl.pallas_call(functools.partial(finish_kernel, ranks, slots), out_shape=...  2.29 us
    ppermute x2, starting transfers between devices, on_device(): beside.append(lax.ppermute(layer, 'elem', pairs))  2.1 us
    pallas_call x1, Pallas kernels, on_device(): pl.pallas_call(functools.partial(local_kernel, ranks), out_shape=[jax.Sha...  2.04 us
    pallas_call x1, Pallas kernels, on_device(): pl.pallas_call(functools.partial(send_kernel, ranks, slots), out_shape=[j...  1.74 us
    ppermute x1, starting transfers between devices, on_device(): y_before = y_after = lax.ppermute(y_layers[0], 'sub', [(0, 1), (1, 0)])  1.46 us
    unnamed x24, local copies, waits for them, and re-layouts  1.26 us
  transfers between devices with their start and end apart: 7, of which 3 were waited for; matrix products, arithmetic and copies ran while one was open for 0% of the time, Pallas kernels for 10%

profile of v4, /device:TPU:0, one launch (start us, length us, event | category | flops | bytes accessed | tf_op | source)
XLA Modules:
  0.0 21.2 jit_solution(12438218676696088533)
XLA Ops:
  1.3 0.0 copy-start.8
  1.3 0.0 copy-start.9
  1.3 0.0 copy-start.6
  1.3 0.0 copy-start.7
  1.3 0.0 copy-start.4
  1.3 0.0 copy-start.5
  1.3 0.0 copy-start.3
  1.3 0.6 %copy-done.8 = s32[1,1,1,192]{3,2,1,0:T(1,128)S(1)} copy-done((s32[1,1,1,192]{3,2,1,0:T(1,128)S(1)}, s32[1,1,1,192]{3,2,1,0:T(1,128)}, u32[]{:S(2)}) %copy-start.8) | copy-done | bytes 792
  2.0 0.0 copy-done.9
  2.0 0.0 copy-done.6
  2.0 0.0 copy-done.7
  2.0 0.0 copy-done.4
  2.0 0.0 copy-done.5
  2.0 0.0 copy-done.3
  2.1 0.0 copy-start
  2.1 0.5 %plan_records.1 = (f32[8,192]{1,0:T(8,128)S(1)}, f32[192,1]{1,0:T(8,128)S(1)}, bf16[192,384]{1,0:T(8,128)(2,1)S(1)}, bf16[384,192]{1,0:T(8,128)(2,1)S(1)}, bf16[256,512]{1,0:T(8,128)(2,1)S(1)}) custom-call(s32[1,192]{1,0:T(1,128)S(1)} %bitcast.18, s32[1,192]{1,0:T(1,128)S(1)} %bitcast.19, s32[1,192]{1,0:T(1,128)S(1)} %bitcast.20, s32[1,192]{1,0:T(1,128)S(1)} %bitcast.21, ...), custom_call_target="tpu_custom_call" | custom-call | flops 1000000000 | bytes 8388608 | tf_op jit(solution)/shard_map/plan_records/pallas_call | solution.py:511
  2.6 0.5 %copy-done = f32[1,4,8,32,128]{4,3,2,1,0:T(8,128)S(1)} copy-done((f32[1,4,8,32,128]{4,3,2,1,0:T(8,128)S(1)}, f32[1,4,8,32,128]{4,3,2,1,0:T(8,128)}, u32[]{:S(2)}) %copy-start) | copy-done | bytes 524312
  3.1 1.7 %send_faces.1 = (f32[200,128]{1,0:T(8,128)S(1)}, f32[200,128]{1,0:T(8,128)S(1)}, f32[200,128]{1,0:T(8,128)S(1)}, f32[200,128]{1,0:T(8,128)S(1)}, f32[256,384]{1,0:T(8,128)S(1)}) custom-call(f32[1024,128]{1,0:T(8,128)S(1)} %bitcast.13, s32[1,1]{1,0:T(1,128)} %bitcast.12.count, f32[8,192]{1,0:T(8,128)S(1)} %get-tuple-element.31.planned, ...), custom_call_target="tpu_custom_call" | custom-call | flops 100000000 | bytes 2097152 | tf_op jit(solution)/shard_map/send_faces/pallas_call | solution.py:531
  4.8 0.0 copy-start.1
  4.8 0.5 %collective-permute-start.3 = (f32[200,128]{1,0:T(8,128)S(1)}, f32[200,128]{1,0:T(8,128)S(1)}, u32[]{:S(2)}, u32[]{:S(2)}) collective-permute-start(f32[200,128]{1,0:T(8,128)S(1)} %get-tuple-element.39), channel_id=1, source_target_pairs={{0,2},{2,0},{4,6},{6,4},{8,10},{10,8},{12,14},{14,12},{1,3},{3,1},... | collective-permute-start | bytes 307208 | tf_op jit(solution)/shard_map/ppermute | solution.py:546
  5.3 4.7 %collective-permute-start = (f32[200,128]{1,0:T(8,128)S(1)}, f32[200,128]{1,0:T(8,128)S(1)}, u32[]{:S(2)}, u32[]{:S(2)}) collective-permute-start(f32[200,128]{1,0:T(8,128)S(1)} %get-tuple-element.36), channel_id=1, source_target_pairs={{0,14},{2,12},{4,10},{6,8},{8,6},{10,4},{12,2},{14,0},{1,15},{3,13... | collective-permute-start | bytes 307208 | tf_op jit(solution)/shard_map/ppermute | solution.py:546
  10.0 0.0 collective-permute-start.1
  10.0 0.3 %collective-permute-start.2 = (f32[200,128]{1,0:T(8,128)S(1)}, f32[200,128]{1,0:T(8,128)S(1)}, u32[]{:S(2)}, u32[]{:S(2)}) collective-permute-start(f32[200,128]{1,0:T(8,128)S(1)} %get-tuple-element.38), channel_id=1, source_target_pairs={{0,6},{2,4},{4,2},{6,0},{8,14},{10,12},{12,10},{14,8},{1,7},{3,5},... | collective-permute-start | bytes 307208 | tf_op jit(solution)/shard_map/ppermute | solution.py:546
  10.3 0.0 collective-permute-done.3.after.refs_3_
  10.4 0.0 copy-start.2
  10.4 1.5 %collective-permute-start.5 = (f32[128,128]{1,0:T(8,128)S(1)}, f32[128,128]{1,0:T(8,128)S(1)}, u32[]{:S(2)}, u32[]{:S(2)}) collective-permute-start(f32[128,128]{1,0:T(8,128)S(1)} %get-tuple-element.44), channel_id=1, source_target_pairs={{0,4},{4,0},{8,12},{12,8},{1,5},{5,1},{9,13},{13,9},{2,6},{6,2},{1... | collective-permute-start | bytes 196616 | tf_op jit(solution)/shard_map/ppermute | solution.py:562
  11.9 0.7 %collective-permute-start.6 = (f32[128,128]{1,0:T(8,128)S(1)}, f32[128,128]{1,0:T(8,128)S(1)}, u32[]{:S(2)}, u32[]{:S(2)}) collective-permute-start(f32[128,128]{1,0:T(8,128)S(1)} %get-tuple-element.45), channel_id=1, source_target_pairs={{4,8},{8,4},{5,9},{9,5},{6,10},{10,6},{7,11},{11,7},{20,24},{24,20... | collective-permute-start | bytes 196616 | tf_op jit(solution)/shard_map/ppermute | solution.py:562
  12.5 0.8 %collective-permute-done.refs_0_ = f32[200,128]{1,0:T(8,128)S(1)} collective-permute-done((f32[200,128]{1,0:T(8,128)S(1)}, f32[200,128]{1,0:T(8,128)S(1)}, u32[]{:S(2)}, u32[]{:S(2)}) %collective-permute-start) | collective-permute-done | bytes 102432 | tf_op jit(solution)/shard_map/ppermute | solution.py:546
  13.3 0.0 copy-start.11
  13.3 0.0 copy-start.10
  13.3 1.5 %collective-permute-start.4 = (f32[32,128]{1,0:T(8,128)S(1)}, f32[32,128]{1,0:T(8,128)S(1)}, u32[]{:S(2)}, u32[]{:S(2)}) collective-permute-start(f32[32,128]{1,0:T(8,128)S(1)} %get-tuple-element.42), channel_id=1, source_target_pairs={{0,1},{1,0},{2,3},{3,2},{4,5},{5,4},{6,7},{7,6},{8,9},{9,8},{10,11... | collective-permute-start | bytes 49160 | tf_op jit(solution)/shard_map/ppermute | solution.py:564
  14.8 0.0 copy-done.1
  14.8 0.0 copy-done.2
  14.8 0.0 copy-done.11
  14.8 0.0 copy-done.10
  14.8 2.0 %local_rate.1 = (f32[1024,128]{1,0:T(8,128)S(1)}, f32[16,128]{1,0:T(8,128)S(1)}) custom-call(f32[1024,128]{1,0:T(8,128)S(1)} %bitcast.15, f32[1024,128]{1,0:T(8,128)S(1)} %bitcast.17, f32[2,3]{1,0:T(2,128)S(1)} %copy-done.10, f32[2,4,4]{2,1,0:T(4,128)S(1)} %copy-done.2, f32[2,4]{1,0:T(2,128)S(1)} %copy-done.11, ...), custom_call_target="tpu_custom_call" | custom-call | flops 500000000 | bytes 4194304 | tf_op jit(solution)/shard_map/local_rate/pallas_call | solution.py:568
  16.9 1.8 %collective-permute-done.1.refs_1_ = f32[200,128]{1,0:T(8,128)S(1)} collective-permute-done((f32[200,128]{1,0:T(8,128)S(1)}, f32[200,128]{1,0:T(8,128)S(1)}, u32[]{:S(2)}, u32[]{:S(2)}) %collective-permute-start.1) | collective-permute-done | bytes 102432 | tf_op jit(solution)/shard_map/ppermute | solution.py:546
  18.7 0.0 collective-permute-done.2.refs_2_
  18.7 0.0 collective-permute-done.4.refs_7_.refs_8_
  18.7 0.2 %collective-permute-done.5.refs_10_ = f32[128,128]{1,0:T(8,128)S(1)} collective-permute-done((f32[128,128]{1,0:T(8,128)S(1)}, f32[128,128]{1,0:T(8,128)S(1)}, u32[]{:S(2)}, u32[]{:S(2)}) %collective-permute-start.5) | collective-permute-done | bytes 65568 | tf_op jit(solution)/shard_map/ppermute | solution.py:562
  18.9 0.0 collective-permute-done.6.refs_11_
  18.9 2.3 %couple_and_finish.1 = (f32[1024,128]{1,0:T(8,128)}, f32[1024,128]{1,0:T(8,128)}) custom-call(f32[200,128]{1,0:T(8,128)S(1)} %collective-permute-done.refs_0_, f32[200,128]{1,0:T(8,128)S(1)} %collective-permute-done.1.refs_1_, f32[200,128]{1,0:T(8,128)S(1)} %collective-permute-done.2.refs_2_, f32[200,128]{1,0:T(8,128)S(1)} %collective-permute-done.3.after.refs_3_, ...), custom_call_target="tpu_custom_call" | custom-call | flops 100000000 | bytes 4194304 | tf_op jit(solution)/shard_map/couple_and_finish/pallas_call | solution.py:582
  (1 shorter events, 0.0 us)
Async XLA Ops:
  1.3 0.7 %copy-start.8 = (s32[1,1,1,192]{3,2,1,0:T(1,128)S(1)}, s32[1,1,1,192]{3,2,1,0:T(1,128)}, u32[]{:S(2)}) copy-start(s32[1,1,1,192]{3,2,1,0:T(1,128)} %param.23) | copy-start | bytes 2308
  1.3 0.7 %copy-start.9 = (s32[1,1,1,192]{3,2,1,0:T(1,128)S(1)}, s32[1,1,1,192]{3,2,1,0:T(1,128)}, u32[]{:S(2)}) copy-start(s32[1,1,1,192]{3,2,1,0:T(1,128)} %param.24) | copy-start | bytes 2308
  1.3 0.7 %copy-start.6 = (s32[1,1,1,192,1]{3,4,2,1,0:T(1,128)S(1)}, s32[1,1,1,192,1]{3,4,2,1,0:T(1,128)}, u32[]{:S(2)}) copy-start(s32[1,1,1,192,1]{3,4,2,1,0:T(1,128)} %param.21) | copy-start | bytes 2308
  1.3 0.7 %copy-start.7 = (s32[1,1,1,192]{3,2,1,0:T(1,128)S(1)}, s32[1,1,1,192]{3,2,1,0:T(1,128)}, u32[]{:S(2)}) copy-start(s32[1,1,1,192]{3,2,1,0:T(1,128)} %param.22) | copy-start | bytes 2308
  1.3 0.7 %copy-start.4 = (s32[1,1,1,192]{3,2,1,0:T(1,128)S(1)}, s32[1,1,1,192]{3,2,1,0:T(1,128)}, u32[]{:S(2)}) copy-start(s32[1,1,1,192]{3,2,1,0:T(1,128)} %param.19) | copy-start | bytes 2308
  1.3 0.7 %copy-start.5 = (s32[1,1,1,192]{3,2,1,0:T(1,128)S(1)}, s32[1,1,1,192]{3,2,1,0:T(1,128)}, u32[]{:S(2)}) copy-start(s32[1,1,1,192]{3,2,1,0:T(1,128)} %param.20) | copy-start | bytes 2308
  1.3 0.7 %copy-start.3 = (s32[1,1,1,192]{3,2,1,0:T(1,128)S(1)}, s32[1,1,1,192]{3,2,1,0:T(1,128)}, u32[]{:S(2)}) copy-start(s32[1,1,1,192]{3,2,1,0:T(1,128)} %param.18) | copy-start | bytes 2308
  2.1 1.0 %copy-start = (f32[1,4,8,32,128]{4,3,2,1,0:T(8,128)S(1)}, f32[1,4,8,32,128]{4,3,2,1,0:T(8,128)}, u32[]{:S(2)}) copy-start(f32[1,4,8,32,128]{4,3,2,1,0:T(8,128)} %param.13) | copy-start | bytes 1572868
  4.8 10.0 %copy-start.1 = (f32[1,4,8,32,128]{4,3,2,1,0:T(8,128)S(1)}, f32[1,4,8,32,128]{4,3,2,1,0:T(8,128)}, u32[]{:S(2)}) copy-start(f32[1,4,8,32,128]{4,3,2,1,0:T(8,128)} %param.14) | copy-start | bytes 1572868
  4.8 5.5 %collective-permute-start.3 = (f32[200,128]{1,0:T(8,128)S(1)}, f32[200,128]{1,0:T(8,128)S(1)}, u32[]{:S(2)}, u32[]{:S(2)}) collective-permute-start(f32[200,128]{1,0:T(8,128)S(1)} %get-tuple-element.39), channel_id=1, source_target_pairs={{0,2},{2,0},{4,6},{6,4},{8,10},{10,8},{12,14},{14,12},{1,3},{3,1},... | collective-permute-start | bytes 307208 | tf_op jit(solution)/shard_map/ppermute | solution.py:546
  5.3 8.0 %collective-permute-start = (f32[200,128]{1,0:T(8,128)S(1)}, f32[200,128]{1,0:T(8,128)S(1)}, u32[]{:S(2)}, u32[]{:S(2)}) collective-permute-start(f32[200,128]{1,0:T(8,128)S(1)} %get-tuple-element.36), channel_id=1, source_target_pairs={{0,14},{2,12},{4,10},{6,8},{8,6},{10,4},{12,2},{14,0},{1,15},{3,13... | collective-permute-start | bytes 307208 | tf_op jit(solution)/shard_map/ppermute | solution.py:546
  10.0 8.7 %collective-permute-start.1 = (f32[200,128]{1,0:T(8,128)S(1)}, f32[200,128]{1,0:T(8,128)S(1)}, u32[]{:S(2)}, u32[]{:S(2)}) collective-permute-start(f32[200,128]{1,0:T(8,128)S(1)} %get-tuple-element.37), channel_id=1, source_target_pairs={{0,10},{2,8},{4,14},{6,12},{8,2},{10,0},{12,6},{14,4},{1,11},{3,9}... | collective-permute-start | bytes 307208 | tf_op jit(solution)/shard_map/ppermute | solution.py:546
  10.0 8.7 %collective-permute-start.2 = (f32[200,128]{1,0:T(8,128)S(1)}, f32[200,128]{1,0:T(8,128)S(1)}, u32[]{:S(2)}, u32[]{:S(2)}) collective-permute-start(f32[200,128]{1,0:T(8,128)S(1)} %get-tuple-element.38), channel_id=1, source_target_pairs={{0,6},{2,4},{4,2},{6,0},{8,14},{10,12},{12,10},{14,8},{1,7},{3,5},... | collective-permute-start | bytes 307208 | tf_op jit(solution)/shard_map/ppermute | solution.py:546
  10.4 4.4 %copy-start.2 = (f32[2,4,4]{2,1,0:T(4,128)S(1)}, f32[2,4,4]{2,1,0:T(4,128)}, u32[]{:S(2)}) copy-start(f32[2,4,4]{2,1,0:T(4,128)} %mixing.1) | copy-start | bytes 388
  10.4 8.5 %collective-permute-start.5 = (f32[128,128]{1,0:T(8,128)S(1)}, f32[128,128]{1,0:T(8,128)S(1)}, u32[]{:S(2)}, u32[]{:S(2)}) collective-permute-start(f32[128,128]{1,0:T(8,128)S(1)} %get-tuple-element.44), channel_id=1, source_target_pairs={{0,4},{4,0},{8,12},{12,8},{1,5},{5,1},{9,13},{13,9},{2,6},{6,2},{1... | collective-permute-start | bytes 196616 | tf_op jit(solution)/shard_map/ppermute | solution.py:562
  11.9 7.1 %collective-permute-start.6 = (f32[128,128]{1,0:T(8,128)S(1)}, f32[128,128]{1,0:T(8,128)S(1)}, u32[]{:S(2)}, u32[]{:S(2)}) collective-permute-start(f32[128,128]{1,0:T(8,128)S(1)} %get-tuple-element.45), channel_id=1, source_target_pairs={{4,8},{8,4},{5,9},{9,5},{6,10},{10,6},{7,11},{11,7},{20,24},{24,20... | collective-permute-start | bytes 196616 | tf_op jit(solution)/shard_map/ppermute | solution.py:562
  13.3 1.5 %copy-start.11 = (f32[2,4]{1,0:T(2,128)S(1)}, f32[2,4]{1,0:T(2,128)}, u32[]{:S(2)}) copy-start(f32[2,4]{1,0:T(2,128)} %drag.1) | copy-start | bytes 100
  13.3 1.5 %copy-start.10 = (f32[2,3]{1,0:T(2,128)S(1)}, f32[2,3]{1,0:T(2,128)}, u32[]{:S(2)}) copy-start(f32[2,3]{1,0:T(2,128)} %advect.1) | copy-start | bytes 76
  13.3 5.4 %collective-permute-start.4 = (f32[32,128]{1,0:T(8,128)S(1)}, f32[32,128]{1,0:T(8,128)S(1)}, u32[]{:S(2)}, u32[]{:S(2)}) collective-permute-start(f32[32,128]{1,0:T(8,128)S(1)} %get-tuple-element.42), channel_id=1, source_target_pairs={{0,1},{1,0},{2,3},{3,2},{4,5},{5,4},{6,7},{7,6},{8,9},{9,8},{10,11... | collective-permute-start | bytes 49160 | tf_op jit(solution)/shard_map/ppermute | solution.py:564

commit v5 on v4

--- a/solution.py
+++ b/solution.py
@@ -162,7 +162,8 @@
 
 
 def send_order(ranks):
-    return list(range(ranks))[::-1]
+    near = neighbour_messages(ranks)[::-1]
+    return near + [k for k in range(1, ranks)[::-1] if k not in near] + [0]
 
 
 def neighbour_messages(ranks):
@@ -405,27 +406,40 @@
         base[ey * 256 : (ey + 1) * 256, :] = register_keep * kept + time_step * rate
 
 
-def finish_kernel(ranks, slots, *refs):
-    messages = refs[:ranks]
-    base, field, faces, y_before, y_after, gains = refs[ranks : ranks + 6]
-    layers = refs[ranks + 6 : -5]
+def scattered(slots, message):
+    head = message[2 * slots : 2 * slots + 8, 0:slots]
+    kind = head[6:7]
+    target = jnp.where(kind > 0.0, head[4:5] * 16.0 + head[5:6], -1.0).astype(jnp.int32)
+    both = jnp.concatenate([target, target], axis=1)
+    placed = one(iota((FACES, 2 * slots), 0) == both)
+    values = jnp.concatenate([message[0:slots, :], message[slots : 2 * slots, :]], axis=1)
+    high = values.astype(bf16).astype(f32)
+    total = dot(placed, jnp.concatenate([high, values - high], axis=0).astype(bf16))
+    row = iota((16, 2 * slots), 0)
+    quadrant = ((row % 8) // 4) * 2 + row // 8
+    kind = jnp.where(iota((1, 2 * slots), 1) < slots, jnp.concatenate([kind, kind], axis=1), 0.0)
+    live = (kind == 1.0) | (kind == 2.0 + quadrant.astype(f32))
+    return total, dot_t(one(live & (kind > 0.0)), placed)
+
+
+def early_kernel(slots, *refs):
+    *messages, total_out, masks_out = refs
+    parts = [scattered(slots, message) for message in messages]
+    total_out[...] = sum(part[0] for part in parts)
+    masks_out[...] = sum(part[1] for part in parts)
+
+
+def finish_kernel(late, slots, *refs):
+    messages = refs[:late]
+    early_total, early_masks, *refs = refs[late:]
+    base, field, faces, y_before, y_after, gains = refs[:6]
+    layers = refs[6:-5]
     new_out, advanced_out, new, advanced, left = refs[-5:]
-    total = jnp.zeros((FACES, 256), f32)
-    masks = jnp.zeros((16, FACES), f32)
+    total, masks = early_total[...], early_masks[...]
     for message in messages:
-        head = message[2 * slots : 2 * slots + 8, 0:slots]
-        kind = head[6:7]
-        target = jnp.where(kind > 0.0, head[4:5] * 16.0 + head[5:6], -1.0).astype(jnp.int32)
-        both = jnp.concatenate([target, target], axis=1)
-        placed = one(iota((FACES, 2 * slots), 0) == both)
-        values = jnp.concatenate([message[0:slots, :], message[slots : 2 * slots, :]], axis=1)
-        high = values.astype(bf16).astype(f32)
-        total += dot(placed, jnp.concatenate([high, values - high], axis=0).astype(bf16))
-        row = iota((16, 2 * slots), 0)
-        quadrant = ((row % 8) // 4) * 2 + row // 8
-        kind = jnp.where(iota((1, 2 * slots), 1) < slots, jnp.concatenate([kind, kind], axis=1), 0.0)
-        live = (kind == 1.0) | (kind == 2.0 + quadrant.astype(f32))
-        masks += dot_t(one(live & (kind > 0.0)), placed)
+        part, named = scattered(slots, message)
+        total += part
+        masks += named
     total = total.T
     terms = []
     for v in range(4):
@@ -579,17 +593,28 @@
     )(
         flat, register.reshape(1024, 128), advect, mixing, drag, received[0],
     )
+    order = send_order(ranks)
+    early, late = order[: len(carriers)] + order[-1:], order[len(carriers) : -1]
+    sums = pl.pallas_call(
+        functools.partial(early_kernel, slots),
+        out_shape=[jax.ShapeDtypeStruct((FACES, 256), f32), jax.ShapeDtypeStruct((16, FACES), f32)],
+        in_specs=[vmem] * len(early),
+        out_specs=[vmem] * 2,
+        compiler_params=pltpu.CompilerParams(vmem_limit_bytes=16 << 20),
+        cost_estimate=pl.CostEstimate(flops=10**6, bytes_accessed=1 << 18, transcendentals=0),
+        name="early_sums",
+    )(*[received[k] for k in early])
     new, advanced = pl.pallas_call(
-        functools.partial(finish_kernel, ranks, slots),
+        functools.partial(finish_kernel, len(late), slots),
         out_shape=[jax.ShapeDtypeStruct((1024, 128), f32)] * 2,
-        in_specs=[vmem] * (ranks + 6 + len(carriers)),
+        in_specs=[vmem] * (len(late) + 8 + len(carriers)),
         out_specs=[pl.BlockSpec(memory_space=pl.ANY)] * 2,
         scratch_shapes=[pltpu.VMEM((1024, 128), f32)] * 2 + [pltpu.SemaphoreType.DMA((8,))],
         compiler_params=pltpu.CompilerParams(vmem_limit_bytes=32 << 20),
         cost_estimate=pl.CostEstimate(flops=10**8, bytes_accessed=4 << 20, transcendentals=0),
         name="couple_and_finish",
     )(
-        *[received[k] for k in send_order(ranks)], base, flat, faces, y_before, y_after, gains, *beside
+        *[received[k] for k in late], *sums, base, flat, faces, y_before, y_after, gains, *beside
     )
     return new.reshape(field.shape), advanced.reshape(field.shape)
 

time: 21.7 us -> 21.4 us (0.986)
  waiting for transfers between devices: 2.89 us -> 2.45 us
  Pallas kernels: 6.61 us -> 6.87 us
    ppermute x4, waiting for transfers between devices: 2.65 us -> 2.15 us  [on_device(): received[k] = lax.ppermute(outgoing[k], ('elem', 'comp'), pairs)]
    pallas_call x1 -> x2, Pallas kernels: 2.29 us -> 2.55 us  [the longest x1 2.05 us: on_device(): pl.pallas_call(functools.partial(finish_kernel, len(late), slots), out_sh...]
  transfers between devices with their start and end apart: 7 -> 7, of which waited for: 3 -> 3; matrix products, arithmetic and copies ran while one was open for 0% -> 0% of each run, Pallas kernels for 10% -> 12%
where the time goes in v5:
time: 21.4 us; the launch traced here: 21.1 us
  starting transfers between devices  9.07 us (42%)
  Pallas kernels  6.87 us (32%)
  waiting for transfers between devices  2.45 us (11%)
  between operations  1.4 us (7%)
  local copies, waits for them, and re-layouts  1.26 us (6%)
    ppermute x4, starting transfers between devices, on_device(): received[k] = lax.ppermute(outgoing[k], ('elem', 'comp'), pairs)  5.51 us
    ppermute x4, waiting for transfers between devices, on_device(): received[k] = lax.ppermute(outgoing[k], ('elem', 'comp'), pairs)  2.15 us
    ppermute x2, starting transfers between devices, on_device(): beside.append(lax.ppermute(layer, 'elem', pairs))  2.1 us
    pallas_call x1, Pallas kernels, on_device(): pl.pallas_call(functools.partial(finish_kernel, len(late), slots), out_sh...  2.05 us
    pallas_call x1, Pallas kernels, on_device(): pl.pallas_call(functools.partial(local_kernel, ranks), out_shape=[jax.Sha...  2.04 us
    pallas_call x1, Pallas kernels, on_device(): pl.pallas_call(functools.partial(send_kernel, ranks, slots), out_shape=[j...  1.74 us
    ppermute x1, starting transfers between devices, on_device(): y_before = y_after = lax.ppermute(y_layers[0], 'sub', [(0, 1), (1, 0)])  1.46 us
    unnamed x24, local copies, waits for them, and re-layouts  1.26 us
  transfers between devices with their start and end apart: 7, of which 3 were waited for; matrix products, arithmetic and copies ran while one was open for 0% of the time, Pallas kernels for 12%

profile of v5, /device:TPU:0, one launch (start us, length us, event | category | flops | bytes accessed | tf_op | source)
XLA Modules:
  0.0 21.1 jit_solution(17593111950147171936)
XLA Ops:
  1.3 0.0 copy-start.8
  1.3 0.0 copy-start.9
  1.3 0.0 copy-start.6
  1.3 0.0 copy-start.7
  1.3 0.0 copy-start.4
  1.3 0.0 copy-start.5
  1.3 0.0 copy-start.3
  1.3 0.6 %copy-done.8 = s32[1,1,1,192]{3,2,1,0:T(1,128)S(1)} copy-done((s32[1,1,1,192]{3,2,1,0:T(1,128)S(1)}, s32[1,1,1,192]{3,2,1,0:T(1,128)}, u32[]{:S(2)}) %copy-start.8) | copy-done | bytes 792
  2.0 0.0 copy-done.9
  2.0 0.0 copy-done.6
  2.0 0.0 copy-done.7
  2.0 0.0 copy-done.4
  2.0 0.0 copy-done.5
  2.0 0.0 copy-done.3
  2.1 0.0 copy-start
  2.1 0.5 %plan_records.1 = (f32[8,192]{1,0:T(8,128)S(1)}, f32[192,1]{1,0:T(8,128)S(1)}, bf16[192,384]{1,0:T(8,128)(2,1)S(1)}, bf16[384,192]{1,0:T(8,128)(2,1)S(1)}, bf16[256,512]{1,0:T(8,128)(2,1)S(1)}) custom-call(s32[1,192]{1,0:T(1,128)S(1)} %bitcast.18, s32[1,192]{1,0:T(1,128)S(1)} %bitcast.19, s32[1,192]{1,0:T(1,128)S(1)} %bitcast.20, s32[1,192]{1,0:T(1,128)S(1)} %bitcast.21, ...), custom_call_target="tpu_custom_call" | custom-call | flops 1000000000 | bytes 8388608 | tf_op jit(solution)/shard_map/plan_records/pallas_call | solution.py:525
  2.6 0.5 %copy-done = f32[1,4,8,32,128]{4,3,2,1,0:T(8,128)S(1)} copy-done((f32[1,4,8,32,128]{4,3,2,1,0:T(8,128)S(1)}, f32[1,4,8,32,128]{4,3,2,1,0:T(8,128)}, u32[]{:S(2)}) %copy-start) | copy-done | bytes 524312
  3.1 1.7 %send_faces.1 = (f32[200,128]{1,0:T(8,128)S(1)}, f32[200,128]{1,0:T(8,128)S(1)}, f32[200,128]{1,0:T(8,128)S(1)}, f32[200,128]{1,0:T(8,128)S(1)}, f32[256,384]{1,0:T(8,128)S(1)}) custom-call(f32[1024,128]{1,0:T(8,128)S(1)} %bitcast.13, s32[1,1]{1,0:T(1,128)} %bitcast.12.count, f32[8,192]{1,0:T(8,128)S(1)} %get-tuple-element.33.planned, ...), custom_call_target="tpu_custom_call" | custom-call | flops 100000000 | bytes 2097152 | tf_op jit(solution)/shard_map/send_faces/pallas_call | solution.py:545
  4.8 0.0 copy-start.1
  4.8 0.5 %collective-permute-start.3 = (f32[200,128]{1,0:T(8,128)S(1)}, f32[200,128]{1,0:T(8,128)S(1)}, u32[]{:S(2)}, u32[]{:S(2)}) collective-permute-start(f32[200,128]{1,0:T(8,128)S(1)} %get-tuple-element.41), channel_id=1, source_target_pairs={{0,2},{2,0},{4,6},{6,4},{8,10},{10,8},{12,14},{14,12},{1,3},{3,1},... | collective-permute-start | bytes 307208 | tf_op jit(solution)/shard_map/ppermute | solution.py:560
  5.3 4.7 %collective-permute-start.1 = (f32[200,128]{1,0:T(8,128)S(1)}, f32[200,128]{1,0:T(8,128)S(1)}, u32[]{:S(2)}, u32[]{:S(2)}) collective-permute-start(f32[200,128]{1,0:T(8,128)S(1)} %get-tuple-element.39), channel_id=1, source_target_pairs={{0,14},{2,12},{4,10},{6,8},{8,6},{10,4},{12,2},{14,0},{1,15},{3,13... | collective-permute-start | bytes 307208 | tf_op jit(solution)/shard_map/ppermute | solution.py:560
  10.0 0.0 collective-permute-start.2
  10.0 0.3 %collective-permute-start = (f32[200,128]{1,0:T(8,128)S(1)}, f32[200,128]{1,0:T(8,128)S(1)}, u32[]{:S(2)}, u32[]{:S(2)}) collective-permute-start(f32[200,128]{1,0:T(8,128)S(1)} %get-tuple-element.38), channel_id=1, source_target_pairs={{0,10},{2,8},{4,14},{6,12},{8,2},{10,0},{12,6},{14,4},{1,11},{3,9}... | collective-permute-start | bytes 307208 | tf_op jit(solution)/shard_map/ppermute | solution.py:560
  10.4 0.0 collective-permute-done.3.refs_2_.after
  10.4 0.0 copy-start.2
  10.4 1.5 %collective-permute-start.5 = (f32[128,128]{1,0:T(8,128)S(1)}, f32[128,128]{1,0:T(8,128)S(1)}, u32[]{:S(2)}, u32[]{:S(2)}) collective-permute-start(f32[128,128]{1,0:T(8,128)S(1)} %get-tuple-element.48), channel_id=1, source_target_pairs={{0,4},{4,0},{8,12},{12,8},{1,5},{5,1},{9,13},{13,9},{2,6},{6,2},{1... | collective-permute-start | bytes 196616 | tf_op jit(solution)/shard_map/ppermute | solution.py:576
  11.9 0.7 %collective-permute-start.6 = (f32[128,128]{1,0:T(8,128)S(1)}, f32[128,128]{1,0:T(8,128)S(1)}, u32[]{:S(2)}, u32[]{:S(2)}) collective-permute-start(f32[128,128]{1,0:T(8,128)S(1)} %get-tuple-element.49), channel_id=1, source_target_pairs={{4,8},{8,4},{5,9},{9,5},{6,10},{10,6},{7,11},{11,7},{20,24},{24,20... | collective-permute-start | bytes 196616 | tf_op jit(solution)/shard_map/ppermute | solution.py:576
  12.5 0.8 %collective-permute-done.1.refs_0_ = f32[200,128]{1,0:T(8,128)S(1)} collective-permute-done((f32[200,128]{1,0:T(8,128)S(1)}, f32[200,128]{1,0:T(8,128)S(1)}, u32[]{:S(2)}, u32[]{:S(2)}) %collective-permute-start.1) | collective-permute-done | bytes 102432 | tf_op jit(solution)/shard_map/ppermute | solution.py:560
  13.3 0.0 copy-start.11
  13.3 0.0 copy-start.10
  13.3 1.5 %collective-permute-start.4 = (f32[32,128]{1,0:T(8,128)S(1)}, f32[32,128]{1,0:T(8,128)S(1)}, u32[]{:S(2)}, u32[]{:S(2)}) collective-permute-start(f32[32,128]{1,0:T(8,128)S(1)} %get-tuple-element.46), channel_id=1, source_target_pairs={{0,1},{1,0},{2,3},{3,2},{4,5},{5,4},{6,7},{7,6},{8,9},{9,8},{10,11... | collective-permute-start | bytes 49160 | tf_op jit(solution)/shard_map/ppermute | solution.py:578
  14.8 0.0 copy-done.1
  14.8 0.0 copy-done.2
  14.8 0.0 copy-done.11
  14.8 0.0 copy-done.10
  14.8 2.0 %local_rate.1 = (f32[1024,128]{1,0:T(8,128)S(1)}, f32[16,128]{1,0:T(8,128)S(1)}) custom-call(f32[1024,128]{1,0:T(8,128)S(1)} %bitcast.15, f32[1024,128]{1,0:T(8,128)S(1)} %bitcast.17, f32[2,3]{1,0:T(2,128)S(1)} %copy-done.10, f32[2,4,4]{2,1,0:T(4,128)S(1)} %copy-done.2, f32[2,4]{1,0:T(2,128)S(1)} %copy-done.11, ...), custom_call_target="tpu_custom_call" | custom-call | flops 500000000 | bytes 4194304 | tf_op jit(solution)/shard_map/local_rate/pallas_call | solution.py:582
  16.9 0.0 collective-permute-done.2.refs_1_
  16.9 0.5 %early_sums.1 = (f32[384,256]{1,0:T(8,128)S(1)}, f32[16,384]{1,0:T(8,128)S(1)}) custom-call(f32[200,128]{1,0:T(8,128)S(1)} %collective-permute-done.1.refs_0_, f32[200,128]{1,0:T(8,128)S(1)} %collective-permute-done.2.refs_1_, f32[200,128]{1,0:T(8,128)S(1)} %collective-permute-done.3.refs_2_.after), custom_call_target="tpu_custom_call" | custom-call | flops 1000000 | bytes 262144 | tf_op jit(solution)/shard_map/early_sums/pallas_call | solution.py:598
  17.4 1.3 %collective-permute-done.refs_0_ = f32[200,128]{1,0:T(8,128)S(1)} collective-permute-done((f32[200,128]{1,0:T(8,128)S(1)}, f32[200,128]{1,0:T(8,128)S(1)}, u32[]{:S(2)}, u32[]{:S(2)}) %collective-permute-start) | collective-permute-done | bytes 102432 | tf_op jit(solution)/shard_map/ppermute | solution.py:560
  18.7 0.0 collective-permute-done.4.refs_6_.refs_7_
  18.7 0.3 %collective-permute-done.5.refs_9_ = f32[128,128]{1,0:T(8,128)S(1)} collective-permute-done((f32[128,128]{1,0:T(8,128)S(1)}, f32[128,128]{1,0:T(8,128)S(1)}, u32[]{:S(2)}, u32[]{:S(2)}) %collective-permute-start.5) | collective-permute-done | bytes 65568 | tf_op jit(solution)/shard_map/ppermute | solution.py:576
  19.0 0.0 collective-permute-done.6.refs_10_
  19.0 2.1 %couple_and_finish.1 = (f32[1024,128]{1,0:T(8,128)}, f32[1024,128]{1,0:T(8,128)}) custom-call(f32[200,128]{1,0:T(8,128)S(1)} %collective-permute-done.refs_0_, f32[384,256]{1,0:T(8,128)S(1)} %get-tuple-element.42.refs_1_, f32[16,384]{1,0:T(8,128)S(1)} %get-tuple-element.43.refs_2_, f32[1024,128]{1,0:T(8,128)S(1)} %get-tuple-element.44.refs_3_, ...), custom_call_target="tpu_custom_call" | custom-call | flops 100000000 | bytes 4194304 | tf_op jit(solution)/shard_map/couple_and_finish/pallas_call | solution.py:607
  (1 shorter events, 0.0 us)
Async XLA Ops:
  1.3 0.7 %copy-start.8 = (s32[1,1,1,192]{3,2,1,0:T(1,128)S(1)}, s32[1,1,1,192]{3,2,1,0:T(1,128)}, u32[]{:S(2)}) copy-start(s32[1,1,1,192]{3,2,1,0:T(1,128)} %param.23) | copy-start | bytes 2308
  1.3 0.7 %copy-start.9 = (s32[1,1,1,192]{3,2,1,0:T(1,128)S(1)}, s32[1,1,1,192]{3,2,1,0:T(1,128)}, u32[]{:S(2)}) copy-start(s32[1,1,1,192]{3,2,1,0:T(1,128)} %param.24) | copy-start | bytes 2308
  1.3 0.7 %copy-start.6 = (s32[1,1,1,192,1]{3,4,2,1,0:T(1,128)S(1)}, s32[1,1,1,192,1]{3,4,2,1,0:T(1,128)}, u32[]{:S(2)}) copy-start(s32[1,1,1,192,1]{3,4,2,1,0:T(1,128)} %param.21) | copy-start | bytes 2308
  1.3 0.7 %copy-start.7 = (s32[1,1,1,192]{3,2,1,0:T(1,128)S(1)}, s32[1,1,1,192]{3,2,1,0:T(1,128)}, u32[]{:S(2)}) copy-start(s32[1,1,1,192]{3,2,1,0:T(1,128)} %param.22) | copy-start | bytes 2308
  1.3 0.7 %copy-start.4 = (s32[1,1,1,192]{3,2,1,0:T(1,128)S(1)}, s32[1,1,1,192]{3,2,1,0:T(1,128)}, u32[]{:S(2)}) copy-start(s32[1,1,1,192]{3,2,1,0:T(1,128)} %param.19) | copy-start | bytes 2308
  1.3 0.7 %copy-start.5 = (s32[1,1,1,192]{3,2,1,0:T(1,128)S(1)}, s32[1,1,1,192]{3,2,1,0:T(1,128)}, u32[]{:S(2)}) copy-start(s32[1,1,1,192]{3,2,1,0:T(1,128)} %param.20) | copy-start | bytes 2308
  1.3 0.7 %copy-start.3 = (s32[1,1,1,192]{3,2,1,0:T(1,128)S(1)}, s32[1,1,1,192]{3,2,1,0:T(1,128)}, u32[]{:S(2)}) copy-start(s32[1,1,1,192]{3,2,1,0:T(1,128)} %param.18) | copy-start | bytes 2308
  2.1 1.0 %copy-start = (f32[1,4,8,32,128]{4,3,2,1,0:T(8,128)S(1)}, f32[1,4,8,32,128]{4,3,2,1,0:T(8,128)}, u32[]{:S(2)}) copy-start(f32[1,4,8,32,128]{4,3,2,1,0:T(8,128)} %param.13) | copy-start | bytes 1572868
  4.8 10.0 %copy-start.1 = (f32[1,4,8,32,128]{4,3,2,1,0:T(8,128)S(1)}, f32[1,4,8,32,128]{4,3,2,1,0:T(8,128)}, u32[]{:S(2)}) copy-start(f32[1,4,8,32,128]{4,3,2,1,0:T(8,128)} %param.14) | copy-start | bytes 1572868
  4.8 5.5 %collective-permute-start.3 = (f32[200,128]{1,0:T(8,128)S(1)}, f32[200,128]{1,0:T(8,128)S(1)}, u32[]{:S(2)}, u32[]{:S(2)}) collective-permute-start(f32[200,128]{1,0:T(8,128)S(1)} %get-tuple-element.41), channel_id=1, source_target_pairs={{0,2},{2,0},{4,6},{6,4},{8,10},{10,8},{12,14},{14,12},{1,3},{3,1},... | collective-permute-start | bytes 307208 | tf_op jit(solution)/shard_map/ppermute | solution.py:560
  5.3 8.0 %collective-permute-start.1 = (f32[200,128]{1,0:T(8,128)S(1)}, f32[200,128]{1,0:T(8,128)S(1)}, u32[]{:S(2)}, u32[]{:S(2)}) collective-permute-start(f32[200,128]{1,0:T(8,128)S(1)} %get-tuple-element.39), channel_id=1, source_target_pairs={{0,14},{2,12},{4,10},{6,8},{8,6},{10,4},{12,2},{14,0},{1,15},{3,13... | collective-permute-start | bytes 307208 | tf_op jit(solution)/shard_map/ppermute | solution.py:560
  10.0 6.8 %collective-permute-start.2 = (f32[200,128]{1,0:T(8,128)S(1)}, f32[200,128]{1,0:T(8,128)S(1)}, u32[]{:S(2)}, u32[]{:S(2)}) collective-permute-start(f32[200,128]{1,0:T(8,128)S(1)} %get-tuple-element.40), channel_id=1, source_target_pairs={{0,6},{2,4},{4,2},{6,0},{8,14},{10,12},{12,10},{14,8},{1,7},{3,5},... | collective-permute-start | bytes 307208 | tf_op jit(solution)/shard_map/ppermute | solution.py:560
  10.0 8.7 %collective-permute-start = (f32[200,128]{1,0:T(8,128)S(1)}, f32[200,128]{1,0:T(8,128)S(1)}, u32[]{:S(2)}, u32[]{:S(2)}) collective-permute-start(f32[200,128]{1,0:T(8,128)S(1)} %get-tuple-element.38), channel_id=1, source_target_pairs={{0,10},{2,8},{4,14},{6,12},{8,2},{10,0},{12,6},{14,4},{1,11},{3,9}... | collective-permute-start | bytes 307208 | tf_op jit(solution)/shard_map/ppermute | solution.py:560
  10.4 4.4 %copy-start.2 = (f32[2,4,4]{2,1,0:T(4,128)S(1)}, f32[2,4,4]{2,1,0:T(4,128)}, u32[]{:S(2)}) copy-start(f32[2,4,4]{2,1,0:T(4,128)} %mixing.1) | copy-start | bytes 388
  10.4 8.6 %collective-permute-start.5 = (f32[128,128]{1,0:T(8,128)S(1)}, f32[128,128]{1,0:T(8,128)S(1)}, u32[]{:S(2)}, u32[]{:S(2)}) collective-permute-start(f32[128,128]{1,0:T(8,128)S(1)} %get-tuple-element.48), channel_id=1, source_target_pairs={{0,4},{4,0},{8,12},{12,8},{1,5},{5,1},{9,13},{13,9},{2,6},{6,2},{1... | collective-permute-start | bytes 196616 | tf_op jit(solution)/shard_map/ppermute | solution.py:576
  11.9 7.1 %collective-permute-start.6 = (f32[128,128]{1,0:T(8,128)S(1)}, f32[128,128]{1,0:T(8,128)S(1)}, u32[]{:S(2)}, u32[]{:S(2)}) collective-permute-start(f32[128,128]{1,0:T(8,128)S(1)} %get-tuple-element.49), channel_id=1, source_target_pairs={{4,8},{8,4},{5,9},{9,5},{6,10},{10,6},{7,11},{11,7},{20,24},{24,20... | collective-permute-start | bytes 196616 | tf_op jit(solution)/shard_map/ppermute | solution.py:576
  13.3 1.5 %copy-start.11 = (f32[2,4]{1,0:T(2,128)S(1)}, f32[2,4]{1,0:T(2,128)}, u32[]{:S(2)}) copy-start(f32[2,4]{1,0:T(2,128)} %drag.1) | copy-start | bytes 100
  13.3 1.5 %copy-start.10 = (f32[2,3]{1,0:T(2,128)S(1)}, f32[2,3]{1,0:T(2,128)}, u32[]{:S(2)}) copy-start(f32[2,3]{1,0:T(2,128)} %advect.1) | copy-start | bytes 76
  13.3 5.4 %collective-permute-start.4 = (f32[32,128]{1,0:T(8,128)S(1)}, f32[32,128]{1,0:T(8,128)S(1)}, u32[]{:S(2)}, u32[]{:S(2)}) collective-permute-start(f32[32,128]{1,0:T(8,128)S(1)} %get-tuple-element.46), channel_id=1, source_target_pairs={{0,1},{1,0},{2,3},{3,2},{4,5},{5,4},{6,7},{7,6},{8,9},{9,8},{10,11... | collective-permute-start | bytes 49160 | tf_op jit(solution)/shard_map/ppermute | solution.py:578

commit v6 on v5

--- a/solution.py
+++ b/solution.py
@@ -172,8 +172,13 @@
 
 def plan_kernel(
     ranks, slots, elem, side, code, rank, p_elem, p_side, p_quadrant,
-    head_out, which_out, picked_out, placed_out, maps,
+    head_out, which_out, picked_out, placed_out, maps, order_out, ends_out, back_out, ends_back_out,
 ):
+    order_out[...] = twice(lane_order(False))
+    for ey in range(EY):
+        ends_out[ey * 256 : ey * 256 + 256, :] = twice(end_lanes(ey, False))
+        ends_back_out[:, ey * 128 : ey * 128 + 128] = twice(end_lanes(ey, True))
+    back_out[...] = twice(lane_order(True))
     capacity = elem.shape[1]
     me = lax.axis_index("elem")
     group, ez = face_number(elem[...], side[...])
@@ -221,14 +226,13 @@
 
 
 def send_kernel(
-    ranks, slots, field, count, planned, which_in, picked, placed_in, maps, *outs
+    ranks, slots, field, count, planned, which_in, picked, placed_in, maps, order, ends_of, *outs
 ):
     messages, faces_out = outs[:ranks], outs[ranks]
     capacity = planned.shape[1]
     lines = iota((8, capacity), 0)
     unused = (lines == 6) & (iota((8, capacity), 1) >= count[...])
     head = jnp.where(unused, 0.0, planned[...]).astype(bf16)
-    order = lane_order(False)
     parts = []
     for kind_of in (0, 1):
         blocks = []
@@ -242,23 +246,22 @@
                 else:
                     blocks.append(y_row(field, ey * 8 + (NODES - 1) * end))
         stacked_high, stacked_low = split(jnp.concatenate(blocks, axis=0))
-        moved = dot(jnp.concatenate([stacked_high, stacked_low], axis=1), twice(order))
+        moved = dot(jnp.concatenate([stacked_high, stacked_low], axis=1), order[...])
         turned = block_transpose([moved[g * 32 : (g + 1) * 32] for g in range(8)])
         parts.append(
             jnp.concatenate(
                 [turned[b][v * 8 : (v + 1) * 8] for v in range(4) for b in range(8)], axis=0
             )
         )
-    ends = jnp.zeros((256, 128), f32)
+    stacks = []
     for ey in range(EY):
         lines = [y_row(field, ey * 8 + b) for b in range(8)]
-        stacked = jnp.concatenate(
-            [lines[b][v * 8 : (v + 1) * 8] for v in range(4) for b in range(8)], axis=0
+        stacks += split(
+            jnp.concatenate(
+                [lines[b][v * 8 : (v + 1) * 8] for v in range(4) for b in range(8)], axis=0
+            )
         )
-        stacked_high, stacked_low = split(stacked)
-        ends += dot(
-            jnp.concatenate([stacked_high, stacked_low], axis=1), twice(end_lanes(ey, False))
-        )
+    ends = dot(jnp.concatenate(stacks, axis=1), ends_of[...])
     parts.append(ends)
     faces = jnp.concatenate(parts, axis=1)
     faces_out[...] = faces
@@ -432,8 +435,8 @@
 def finish_kernel(late, slots, *refs):
     messages = refs[:late]
     early_total, early_masks, *refs = refs[late:]
-    base, field, faces, y_before, y_after, gains = refs[:6]
-    layers = refs[6:-5]
+    base, field, faces, y_before, y_after, gains, back, ends_back = refs[:8]
+    layers = refs[8:-5]
     new_out, advanced_out, new, advanced, left = refs[-5:]
     total, masks = early_total[...], early_masks[...]
     for message in messages:
@@ -457,10 +460,9 @@
             ]
         )
     high, low = split(jnp.concatenate(turned, axis=0))
-    moved = dot(jnp.concatenate([high, low], axis=1), twice(lane_order(True)))
+    moved = dot(jnp.concatenate([high, low], axis=1), back[...])
     high, low = split(jnp.concatenate([term[:, 256:384] for term in terms], axis=0))
-    ends = jnp.concatenate([end_lanes(ey, True) for ey in range(EY)], axis=1)
-    on_z = dot(jnp.concatenate([high, low], axis=1), twice(ends))
+    on_z = dot(jnp.concatenate([high, low], axis=1), ends_back[...])
 
     copies = []
     for v in range(4):
@@ -530,9 +532,13 @@
             jax.ShapeDtypeStruct((capacity, FACES), bf16),
             jax.ShapeDtypeStruct((ranks * slots, capacity), bf16),
             jax.ShapeDtypeStruct((256, CODES * 64), bf16),
+            jax.ShapeDtypeStruct((256, 128), bf16),
+            jax.ShapeDtypeStruct((EY * 256, 128), bf16),
+            jax.ShapeDtypeStruct((256, 128), bf16),
+            jax.ShapeDtypeStruct((256, EY * 128), bf16),
         ],
         in_specs=[vmem] * 7,
-        out_specs=[vmem] * 5,
+        out_specs=[vmem] * 9,
         compiler_params=pltpu.CompilerParams(vmem_limit_bytes=32 << 20),
         cost_estimate=pl.CostEstimate(flops=10**9, bytes_accessed=8 << 20, transcendentals=0),
         name="plan_records",
@@ -546,12 +552,12 @@
         functools.partial(send_kernel, ranks, slots),
         out_shape=[jax.ShapeDtypeStruct((2 * slots + 8, 128), f32)] * ranks
         + [jax.ShapeDtypeStruct((256, FACES), f32)],
-        in_specs=[vmem] * 7,
+        in_specs=[vmem] * 9,
         out_specs=[vmem] * (ranks + 1),
         compiler_params=pltpu.CompilerParams(vmem_limit_bytes=32 << 20),
         cost_estimate=pl.CostEstimate(flops=10**8, bytes_accessed=2 << 20, transcendentals=0),
         name="send_faces",
-    )(flat, face_count.reshape(1, 1), *plan)
+    )(flat, face_count.reshape(1, 1), *plan[:-2])
     faces = outs[ranks]
     outgoing = dict(zip(send_order(ranks), outs))
     received = {}
@@ -607,14 +613,14 @@
     new, advanced = pl.pallas_call(
         functools.partial(finish_kernel, len(late), slots),
         out_shape=[jax.ShapeDtypeStruct((1024, 128), f32)] * 2,
-        in_specs=[vmem] * (len(late) + 8 + len(carriers)),
+        in_specs=[vmem] * (len(late) + 10 + len(carriers)),
         out_specs=[pl.BlockSpec(memory_space=pl.ANY)] * 2,
         scratch_shapes=[pltpu.VMEM((1024, 128), f32)] * 2 + [pltpu.SemaphoreType.DMA((8,))],
         compiler_params=pltpu.CompilerParams(vmem_limit_bytes=32 << 20),
         cost_estimate=pl.CostEstimate(flops=10**8, bytes_accessed=4 << 20, transcendentals=0),
         name="couple_and_finish",
     )(
-        *[received[k] for k in late], *sums, base, flat, faces, y_before, y_after, gains, *beside
+        *[received[k] for k in late], *sums, base, flat, faces, y_before, y_after, gains, *plan[-2:], *beside
     )
     return new.reshape(field.shape), advanced.reshape(field.shape)
 

time: 21.4 us -> 21.4 us (level)
  no operation moved by 1% of the time
where the time goes in v6:
time: 21.4 us; the launch traced here: 21.1 us
  starting transfers between devices  9.08 us (42%)
  Pallas kernels  7.02 us (33%)
  waiting for transfers between devices  2.36 us (11%)
  between operations  1.4 us (7%)
  local copies, waits for them, and re-layouts  1.21 us (6%)
    ppermute x4, starting transfers between devices, on_device(): received[k] = lax.ppermute(outgoing[k], ('elem', 'comp'), pairs)  5.51 us
    pallas_call x1, Pallas kernels, on_device(): pl.pallas_call(functools.partial(local_kernel, ranks), out_shape=[jax.Sha...  2.11 us
    ppermute x2, starting transfers between devices, on_device(): beside.append(lax.ppermute(layer, 'elem', pairs))  2.1 us
    pallas_call x1, Pallas kernels, on_device(): pl.pallas_call(functools.partial(finish_kernel, len(late), slots), out_sh...  2.1 us
    ppermute x4, waiting for transfers between devices, on_device(): received[k] = lax.ppermute(outgoing[k], ('elem', 'comp'), pairs)  2.07 us
    pallas_call x1, Pallas kernels, on_device(): pl.pallas_call(functools.partial(send_kernel, ranks, slots), out_shape=[j...  1.74 us
    ppermute x1, starting transfers between devices, on_device(): y_before = y_after = lax.ppermute(y_layers[0], 'sub', [(0, 1), (1, 0)])  1.46 us
    unnamed x24, local copies, waits for them, and re-layouts  1.21 us
  transfers between devices with their start and end apart: 7, of which 3 were waited for; matrix products, arithmetic and copies ran while one was open for 0% of the time, Pallas kernels for 12%

profile of v6, /device:TPU:0, one launch (start us, length us, event | category | flops | bytes accessed | tf_op | source)
XLA Modules:
  0.0 21.1 jit_solution(12948822894209682294)
XLA Ops:
  1.3 0.0 copy-start.8
  1.3 0.0 copy-start.9
  1.3 0.0 copy-start.6
  1.3 0.0 copy-start.7
  1.3 0.0 copy-start.4
  1.3 0.0 copy-start.5
  1.3 0.0 copy-start.3
  1.3 0.6 %copy-done.8 = s32[1,1,1,192]{3,2,1,0:T(1,128)S(1)} copy-done((s32[1,1,1,192]{3,2,1,0:T(1,128)S(1)}, s32[1,1,1,192]{3,2,1,0:T(1,128)}, u32[]{:S(2)}) %copy-start.8) | copy-done | bytes 792
  2.0 0.0 copy-done.9
  2.0 0.0 copy-done.6
  2.0 0.0 copy-done.7
  2.0 0.0 copy-done.4
  2.0 0.0 copy-done.5
  2.0 0.0 copy-done.3
  2.1 0.0 copy-start
  2.1 0.6 %plan_records.1 = (f32[8,192]{1,0:T(8,128)S(1)}, f32[192,1]{1,0:T(8,128)S(1)}, bf16[192,384]{1,0:T(8,128)(2,1)S(1)}, bf16[384,192]{1,0:T(8,128)(2,1)S(1)}, bf16[...) custom-call(s32[1,192]{1,0:T(1,128)S(1)} %bitcast.18, ...), custom_call_target="tpu_custom_call" | custom-call | flops 1000000000 | bytes 8388608 | tf_op jit(solution)/shard_map/plan_records/pallas_call | solution.py:527
  2.6 0.5 %copy-done = f32[1,4,8,32,128]{4,3,2,1,0:T(8,128)S(1)} copy-done((f32[1,4,8,32,128]{4,3,2,1,0:T(8,128)S(1)}, f32[1,4,8,32,128]{4,3,2,1,0:T(8,128)}, u32[]{:S(2)}) %copy-start) | copy-done | bytes 524312
  3.1 1.7 %send_faces.1 = (f32[200,128]{1,0:T(8,128)S(1)}, f32[200,128]{1,0:T(8,128)S(1)}, f32[200,128]{1,0:T(8,128)S(1)}, f32[200,128]{1,0:T(8,128)S(1)}, f32[256,384]{1,0:T(8,128)S(1)}) custom-call(f32[1024,128]{1,0:T(8,128)S(1)} %bitcast.13, s32[1,1]{1,0:T(1,128)} %bitcast.12.count, f32[8,192]{1,0:T(8,128)S(1)} %get-tuple-element.45.planned, ...), custom_call_target="tpu_custom_call" | custom-call | flops 100000000 | bytes 2097152 | tf_op jit(solution)/shard_map/send_faces/pallas_call | solution.py:551
  4.8 0.0 copy-start.1
  4.8 0.5 %collective-permute-start.3 = (f32[200,128]{1,0:T(8,128)S(1)}, f32[200,128]{1,0:T(8,128)S(1)}, u32[]{:S(2)}, u32[]{:S(2)}) collective-permute-start(f32[200,128]{1,0:T(8,128)S(1)} %get-tuple-element.55), channel_id=1, source_target_pairs={{0,2},{2,0},{4,6},{6,4},{8,10},{10,8},{12,14},{14,12},{1,3},{3,1},... | collective-permute-start | bytes 307208 | tf_op jit(solution)/shard_map/ppermute | solution.py:566
  5.3 4.7 %collective-permute-start.1 = (f32[200,128]{1,0:T(8,128)S(1)}, f32[200,128]{1,0:T(8,128)S(1)}, u32[]{:S(2)}, u32[]{:S(2)}) collective-permute-start(f32[200,128]{1,0:T(8,128)S(1)} %get-tuple-element.53), channel_id=1, source_target_pairs={{0,14},{2,12},{4,10},{6,8},{8,6},{10,4},{12,2},{14,0},{1,15},{3,13... | collective-permute-start | bytes 307208 | tf_op jit(solution)/shard_map/ppermute | solution.py:566
  10.0 0.0 collective-permute-start.2
  10.0 0.3 %collective-permute-start = (f32[200,128]{1,0:T(8,128)S(1)}, f32[200,128]{1,0:T(8,128)S(1)}, u32[]{:S(2)}, u32[]{:S(2)}) collective-permute-start(f32[200,128]{1,0:T(8,128)S(1)} %get-tuple-element.52), channel_id=1, source_target_pairs={{0,10},{2,8},{4,14},{6,12},{8,2},{10,0},{12,6},{14,4},{1,11},{3,9}... | collective-permute-start | bytes 307208 | tf_op jit(solution)/shard_map/ppermute | solution.py:566
  10.3 0.0 collective-permute-done.3.refs_2_.after
  10.4 0.0 copy-start.2
  10.4 1.5 %collective-permute-start.5 = (f32[128,128]{1,0:T(8,128)S(1)}, f32[128,128]{1,0:T(8,128)S(1)}, u32[]{:S(2)}, u32[]{:S(2)}) collective-permute-start(f32[128,128]{1,0:T(8,128)S(1)} %get-tuple-element.64), channel_id=1, source_target_pairs={{0,4},{4,0},{8,12},{12,8},{1,5},{5,1},{9,13},{13,9},{2,6},{6,2},{1... | collective-permute-start | bytes 196616 | tf_op jit(solution)/shard_map/ppermute | solution.py:582
  11.9 0.7 %collective-permute-start.6 = (f32[128,128]{1,0:T(8,128)S(1)}, f32[128,128]{1,0:T(8,128)S(1)}, u32[]{:S(2)}, u32[]{:S(2)}) collective-permute-start(f32[128,128]{1,0:T(8,128)S(1)} %get-tuple-element.65), channel_id=1, source_target_pairs={{4,8},{8,4},{5,9},{9,5},{6,10},{10,6},{7,11},{11,7},{20,24},{24,20... | collective-permute-start | bytes 196616 | tf_op jit(solution)/shard_map/ppermute | solution.py:582
  12.5 0.8 %collective-permute-done.1.refs_0_ = f32[200,128]{1,0:T(8,128)S(1)} collective-permute-done((f32[200,128]{1,0:T(8,128)S(1)}, f32[200,128]{1,0:T(8,128)S(1)}, u32[]{:S(2)}, u32[]{:S(2)}) %collective-permute-start.1) | collective-permute-done | bytes 102432 | tf_op jit(solution)/shard_map/ppermute | solution.py:566
  13.3 0.0 copy-start.11
  13.3 0.0 copy-start.10
  13.3 1.5 %collective-permute-start.4 = (f32[32,128]{1,0:T(8,128)S(1)}, f32[32,128]{1,0:T(8,128)S(1)}, u32[]{:S(2)}, u32[]{:S(2)}) collective-permute-start(f32[32,128]{1,0:T(8,128)S(1)} %get-tuple-element.60), channel_id=1, source_target_pairs={{0,1},{1,0},{2,3},{3,2},{4,5},{5,4},{6,7},{7,6},{8,9},{9,8},{10,11... | collective-permute-start | bytes 49160 | tf_op jit(solution)/shard_map/ppermute | solution.py:584
  14.8 0.0 copy-done.1
  14.8 0.0 copy-done.2
  14.8 0.0 copy-done.11
  14.8 0.0 copy-done.10
  14.8 2.1 %local_rate.1 = (f32[1024,128]{1,0:T(8,128)S(1)}, f32[16,128]{1,0:T(8,128)S(1)}) custom-call(f32[1024,128]{1,0:T(8,128)S(1)} %bitcast.15, f32[1024,128]{1,0:T(8,128)S(1)} %bitcast.17, f32[2,3]{1,0:T(2,128)S(1)} %copy-done.10, f32[2,4,4]{2,1,0:T(4,128)S(1)} %copy-done.2, f32[2,4]{1,0:T(2,128)S(1)} %copy-done.11, ...), custom_call_target="tpu_custom_call" | custom-call | flops 500000000 | bytes 4194304 | tf_op jit(solution)/shard_map/local_rate/pallas_call | solution.py:588
  16.9 0.0 collective-permute-done.2.refs_1_
  16.9 0.5 %early_sums.1 = (f32[384,256]{1,0:T(8,128)S(1)}, f32[16,384]{1,0:T(8,128)S(1)}) custom-call(f32[200,128]{1,0:T(8,128)S(1)} %collective-permute-done.1.refs_0_, f32[200,128]{1,0:T(8,128)S(1)} %collective-permute-done.2.refs_1_, f32[200,128]{1,0:T(8,128)S(1)} %collective-permute-done.3.refs_2_.after), custom_call_target="tpu_custom_call" | custom-call | flops 1000000 | bytes 262144 | tf_op jit(solution)/shard_map/early_sums/pallas_call | solution.py:604
  17.4 1.3 %collective-permute-done.refs_0_ = f32[200,128]{1,0:T(8,128)S(1)} collective-permute-done((f32[200,128]{1,0:T(8,128)S(1)}, f32[200,128]{1,0:T(8,128)S(1)}, u32[]{:S(2)}, u32[]{:S(2)}) %collective-permute-start) | collective-permute-done | bytes 102432 | tf_op jit(solution)/shard_map/ppermute | solution.py:566
  18.7 0.0 collective-permute-done.4.refs_6_.refs_7_
  18.7 0.3 %collective-permute-done.5.refs_11_ = f32[128,128]{1,0:T(8,128)S(1)} collective-permute-done((f32[128,128]{1,0:T(8,128)S(1)}, f32[128,128]{1,0:T(8,128)S(1)}, u32[]{:S(2)}, u32[]{:S(2)}) %collective-permute-start.5) | collective-permute-done | bytes 65568 | tf_op jit(solution)/shard_map/ppermute | solution.py:582
  19.0 0.0 collective-permute-done.6.refs_12_
  19.0 2.1 %couple_and_finish.1 = (f32[1024,128]{1,0:T(8,128)}, f32[1024,128]{1,0:T(8,128)}) custom-call(f32[200,128]{1,0:T(8,128)S(1)} %collective-permute-done.refs_0_, f32[384,256]{1,0:T(8,128)S(1)} %get-tuple-element.56.refs_1_, f32[16,384]{1,0:T(8,128)S(1)} %get-tuple-element.57.refs_2_, f32[1024,128]{1,0:T(8,128)S(1)} %get-tuple-element.58.refs_3_, ...), custom_call_target="tpu_custom_call" | custom-call | flops 100000000 | bytes 4194304 | tf_op jit(solution)/shard_map/couple_and_finish/pallas_call | solution.py:613
  (1 shorter events, 0.0 us)
Async XLA Ops:
  1.3 0.7 %copy-start.8 = (s32[1,1,1,192]{3,2,1,0:T(1,128)S(1)}, s32[1,1,1,192]{3,2,1,0:T(1,128)}, u32[]{:S(2)}) copy-start(s32[1,1,1,192]{3,2,1,0:T(1,128)} %param.23) | copy-start | bytes 2308
  1.3 0.7 %copy-start.9 = (s32[1,1,1,192]{3,2,1,0:T(1,128)S(1)}, s32[1,1,1,192]{3,2,1,0:T(1,128)}, u32[]{:S(2)}) copy-start(s32[1,1,1,192]{3,2,1,0:T(1,128)} %param.24) | copy-start | bytes 2308
  1.3 0.7 %copy-start.6 = (s32[1,1,1,192,1]{3,4,2,1,0:T(1,128)S(1)}, s32[1,1,1,192,1]{3,4,2,1,0:T(1,128)}, u32[]{:S(2)}) copy-start(s32[1,1,1,192,1]{3,4,2,1,0:T(1,128)} %param.21) | copy-start | bytes 2308
  1.3 0.7 %copy-start.7 = (s32[1,1,1,192]{3,2,1,0:T(1,128)S(1)}, s32[1,1,1,192]{3,2,1,0:T(1,128)}, u32[]{:S(2)}) copy-start(s32[1,1,1,192]{3,2,1,0:T(1,128)} %param.22) | copy-start | bytes 2308
  1.3 0.7 %copy-start.4 = (s32[1,1,1,192]{3,2,1,0:T(1,128)S(1)}, s32[1,1,1,192]{3,2,1,0:T(1,128)}, u32[]{:S(2)}) copy-start(s32[1,1,1,192]{3,2,1,0:T(1,128)} %param.19) | copy-start | bytes 2308
  1.3 0.7 %copy-start.5 = (s32[1,1,1,192]{3,2,1,0:T(1,128)S(1)}, s32[1,1,1,192]{3,2,1,0:T(1,128)}, u32[]{:S(2)}) copy-start(s32[1,1,1,192]{3,2,1,0:T(1,128)} %param.20) | copy-start | bytes 2308
  1.3 0.7 %copy-start.3 = (s32[1,1,1,192]{3,2,1,0:T(1,128)S(1)}, s32[1,1,1,192]{3,2,1,0:T(1,128)}, u32[]{:S(2)}) copy-start(s32[1,1,1,192]{3,2,1,0:T(1,128)} %param.18) | copy-start | bytes 2308
  2.1 1.0 %copy-start = (f32[1,4,8,32,128]{4,3,2,1,0:T(8,128)S(1)}, f32[1,4,8,32,128]{4,3,2,1,0:T(8,128)}, u32[]{:S(2)}) copy-start(f32[1,4,8,32,128]{4,3,2,1,0:T(8,128)} %param.13) | copy-start | bytes 1572868
  4.8 10.0 %copy-start.1 = (f32[1,4,8,32,128]{4,3,2,1,0:T(8,128)S(1)}, f32[1,4,8,32,128]{4,3,2,1,0:T(8,128)}, u32[]{:S(2)}) copy-start(f32[1,4,8,32,128]{4,3,2,1,0:T(8,128)} %param.14) | copy-start | bytes 1572868
  4.8 5.5 %collective-permute-start.3 = (f32[200,128]{1,0:T(8,128)S(1)}, f32[200,128]{1,0:T(8,128)S(1)}, u32[]{:S(2)}, u32[]{:S(2)}) collective-permute-start(f32[200,128]{1,0:T(8,128)S(1)} %get-tuple-element.55), channel_id=1, source_target_pairs={{0,2},{2,0},{4,6},{6,4},{8,10},{10,8},{12,14},{14,12},{1,3},{3,1},... | collective-permute-start | bytes 307208 | tf_op jit(solution)/shard_map/ppermute | solution.py:566
  5.3 8.0 %collective-permute-start.1 = (f32[200,128]{1,0:T(8,128)S(1)}, f32[200,128]{1,0:T(8,128)S(1)}, u32[]{:S(2)}, u32[]{:S(2)}) collective-permute-start(f32[200,128]{1,0:T(8,128)S(1)} %get-tuple-element.53), channel_id=1, source_target_pairs={{0,14},{2,12},{4,10},{6,8},{8,6},{10,4},{12,2},{14,0},{1,15},{3,13... | collective-permute-start | bytes 307208 | tf_op jit(solution)/shard_map/ppermute | solution.py:566
  10.0 6.9 %collective-permute-start.2 = (f32[200,128]{1,0:T(8,128)S(1)}, f32[200,128]{1,0:T(8,128)S(1)}, u32[]{:S(2)}, u32[]{:S(2)}) collective-permute-start(f32[200,128]{1,0:T(8,128)S(1)} %get-tuple-element.54), channel_id=1, source_target_pairs={{0,6},{2,4},{4,2},{6,0},{8,14},{10,12},{12,10},{14,8},{1,7},{3,5},... | collective-permute-start | bytes 307208 | tf_op jit(solution)/shard_map/ppermute | solution.py:566
  10.0 8.7 %collective-permute-start = (f32[200,128]{1,0:T(8,128)S(1)}, f32[200,128]{1,0:T(8,128)S(1)}, u32[]{:S(2)}, u32[]{:S(2)}) collective-permute-start(f32[200,128]{1,0:T(8,128)S(1)} %get-tuple-element.52), channel_id=1, source_target_pairs={{0,10},{2,8},{4,14},{6,12},{8,2},{10,0},{12,6},{14,4},{1,11},{3,9}... | collective-permute-start | bytes 307208 | tf_op jit(solution)/shard_map/ppermute | solution.py:566
  10.4 4.4 %copy-start.2 = (f32[2,4,4]{2,1,0:T(4,128)S(1)}, f32[2,4,4]{2,1,0:T(4,128)}, u32[]{:S(2)}) copy-start(f32[2,4,4]{2,1,0:T(4,128)} %mixing.1) | copy-start | bytes 388
  10.4 8.6 %collective-permute-start.5 = (f32[128,128]{1,0:T(8,128)S(1)}, f32[128,128]{1,0:T(8,128)S(1)}, u32[]{:S(2)}, u32[]{:S(2)}) collective-permute-start(f32[128,128]{1,0:T(8,128)S(1)} %get-tuple-element.64), channel_id=1, source_target_pairs={{0,4},{4,0},{8,12},{12,8},{1,5},{5,1},{9,13},{13,9},{2,6},{6,2},{1... | collective-permute-start | bytes 196616 | tf_op jit(solution)/shard_map/ppermute | solution.py:582
  11.9 7.1 %collective-permute-start.6 = (f32[128,128]{1,0:T(8,128)S(1)}, f32[128,128]{1,0:T(8,128)S(1)}, u32[]{:S(2)}, u32[]{:S(2)}) collective-permute-start(f32[128,128]{1,0:T(8,128)S(1)} %get-tuple-element.65), channel_id=1, source_target_pairs={{4,8},{8,4},{5,9},{9,5},{6,10},{10,6},{7,11},{11,7},{20,24},{24,20... | collective-permute-start | bytes 196616 | tf_op jit(solution)/shard_map/ppermute | solution.py:582
  13.3 1.5 %copy-start.11 = (f32[2,4]{1,0:T(2,128)S(1)}, f32[2,4]{1,0:T(2,128)}, u32[]{:S(2)}) copy-start(f32[2,4]{1,0:T(2,128)} %drag.1) | copy-start | bytes 100
  13.3 1.5 %copy-start.10 = (f32[2,3]{1,0:T(2,128)S(1)}, f32[2,3]{1,0:T(2,128)}, u32[]{:S(2)}) copy-start(f32[2,3]{1,0:T(2,128)} %advect.1) | copy-start | bytes 76
  13.3 5.4 %collective-permute-start.4 = (f32[32,128]{1,0:T(8,128)S(1)}, f32[32,128]{1,0:T(8,128)S(1)}, u32[]{:S(2)}, u32[]{:S(2)}) collective-permute-start(f32[32,128]{1,0:T(8,128)S(1)} %get-tuple-element.60), channel_id=1, source_target_pairs={{0,1},{1,0},{2,3},{3,2},{4,5},{5,4},{6,7},{7,6},{8,9},{9,8},{10,11... | collective-permute-start | bytes 49160 | tf_op jit(solution)/shard_map/ppermute | solution.py:584
